TPU v7x, 32 devices: a whole 2x2x4 slice. The times are simulated.
32 devices in a mesh: side: 2 (over y), grp: 2 (over x), dev: 8 (over z, core).
Axes of the slice: x: 2, y: 2, z: 4, core: 2. Of those that a mesh axis runs over, the one named last changes fastest.
Arguments:
- sources: float32 [2, 8, 4096], P('side', None, ('grp', 'dev')), may hold values from -2500 to 2500
- near_blocks: bfloat16 [2, 512, 128, 128], P('side', ('grp', 'dev')), may hold values from -0.125 to 0.125
- block_rows: int32 [2, 512], P('side', ('grp', 'dev')), may hold values from 0 to 1, as said below
- block_cols: int32 [2, 512], P('side', ('grp', 'dev')), may hold values from 0 to 31, as said below
- mirror: int32 [4096], P(('grp', 'dev')), may hold values from 0 to 127, as said below
Outputs:
- krylov_basis: float32 [4, 2, 8, 4096], P(None, 'side', None, ('grp', 'dev'))
- hessenberg: float32 [8, 4, 3], replicated
Inputs may be any that keep to these rules, and one draw needn't show every extreme that they name: `block_rows`: in each device's aligned run of 32 entries, the first 2 are 0 to 1 in order. `block_cols`: in each device's aligned run of 32 entries, the first 2 name that device's own blocks in order, and every entry names a block of an owner at most 4 owners before or after that device (owners of a half counted in the order grp, dev); where such owners exist, some entry names a block of the owner 4 before and some one of the owner 4 after. `mirror`: each aligned run of 128 entries is a permutation of 0 to 127.
All inputs are finite; a program needn't handle non-finite values.
Results may differ from a plain program's by a relative error of at most 0.005.
Values may be sent and summed in bfloat16 or wider, within the bound.
No kernel may reach another device: no remote copies, remote signals or barrier semaphores. Data moves between devices by JAX's collectives and lax.ppermute only.
A program may use at most 64 MiB of HBM per device.

v0:
```python
import jax
import jax.numpy as jnp
from jax import lax
from jax.sharding import PartitionSpec as P

BLOCK = 128
BLK_DEV = 2
WIN = 4
ITERS = 3


epsilon = 1e-06


def shifted(block, axis, distance):
    devices = range(lax.axis_size(axis))
    route = [(i - distance, i) for i in devices if i - distance in devices]
    return lax.ppermute(block, axis, route)


def swapped(value, axis, distance):
    return lax.ppermute(value, axis, [(i, i ^ 1 << distance) for i in range(lax.axis_size(axis))])


def on_device(sources, near_blocks, block_rows, block_cols, mirror):
    side_index = lax.axis_index("side")
    is_port = side_index == 0
    owner_index = lax.axis_index(("grp", "dev"))
    vectors = sources.shape[1]
    panels = sources.shape[2]
    total_panels = (
        1.0 * panels * lax.axis_size("side") * lax.axis_size("grp") * lax.axis_size("dev")
    )
    mirror_onehot = (
        mirror.reshape(BLK_DEV, BLOCK)[:, :, None]
        == jnp.arange(BLOCK, dtype=jnp.int32)[None, None, :]
    ).astype(jnp.float32)
    row_onehot = (block_rows[0][None, :] == jnp.arange(BLK_DEV, dtype=jnp.int32)[:, None]).astype(
        jnp.float32
    )
    window_cols = block_cols[0] - (owner_index - WIN) * BLK_DEV
    blocks = near_blocks[0]
    start = sources[0]
    inner_scale = 1.0 / total_panels
    squares = lax.psum(jnp.sum(start * start, axis=1), ("side", "grp", "dev"))
    length = jnp.sqrt(squares * inner_scale + epsilon)
    vectors_list = [start / length[:, None]]
    hessenberg = jnp.zeros((vectors, ITERS + 1, ITERS), jnp.float32)
    for column in range(ITERS):
        operator_vector = vectors_list[column]
        operator_partner = swapped(operator_vector, "side", 0)
        port_part = jnp.where(is_port, operator_vector, operator_partner)
        star_part = jnp.where(is_port, operator_partner, operator_vector)
        parity = jnp.where(is_port, 1.0, -1.0).astype(jnp.float32)
        mirrored_shaped = star_part.reshape(star_part.shape[:-1] + (BLK_DEV, BLOCK))
        field = port_part + parity * jnp.einsum(
            "bij,...bj->...bi", mirror_onehot, mirrored_shaped, precision=lax.Precision.HIGHEST
        ).reshape(star_part.shape)
        near_rounded = field.astype(jnp.bfloat16)
        below_list = []
        above_list = []
        for distance in range(1, WIN + 1):
            below_list.append(shifted(near_rounded, ("grp", "dev"), distance))
            above_list.append(shifted(near_rounded, ("grp", "dev"), -distance))
        window = jnp.concatenate(below_list[::-1] + [near_rounded] + above_list, axis=1)
        picked = window.reshape(vectors, -1, BLOCK)[:, window_cols]
        products = jnp.einsum("rkj,kij->rki", picked, blocks, preferred_element_type=jnp.float32)
        summed = jnp.einsum("bk,rki->rbi", row_onehot, products, precision=lax.Precision.HIGHEST)
        image = 0.5 * field + summed.reshape(vectors, panels)
        returned = swapped(image, "side", 0)
        symmetric = jnp.where(is_port, image, returned)
        antisym = jnp.where(is_port, returned, image)
        vector = 0.5 * (symmetric - antisym)
        shaped = vector.reshape(vector.shape[:-1] + (BLK_DEV, BLOCK))
        image = jnp.where(
            is_port,
            0.5 * (symmetric + antisym),
            jnp.einsum(
                "bij,...bi->...bj", mirror_onehot, shaped, precision=lax.Precision.HIGHEST
            ).reshape(vector.shape),
        )
        stacked = jnp.stack(vectors_list)
        products_local = jnp.sum(image[None] * stacked, axis=2)
        dot_sums = lax.psum(products_local, ("side", "grp", "dev"))
        coeffs = dot_sums * inner_scale
        remainder = image - jnp.einsum(
            "jr,jrp->rp", coeffs, stacked, precision=lax.Precision.HIGHEST
        )
        rem_squares = (
            lax.psum(jnp.sum(remainder * remainder, axis=1), ("side", "grp", "dev")) * inner_scale
        )
        rem_norm = jnp.sqrt(rem_squares + epsilon)
        vectors_list.append(remainder / rem_norm[:, None])
        hessenberg = hessenberg.at[:, : column + 1, column].set(coeffs.T)
        hessenberg = hessenberg.at[:, column + 1, column].set(rem_norm)
    final = jnp.stack(vectors_list)
    return (final[:, None], hessenberg)


def solution(mesh):
    placed = (
        P("side", None, ("grp", "dev")),
        P("side", ("grp", "dev"), None, None),
        P("side", ("grp", "dev")),
        P("side", ("grp", "dev")),
        P(("grp", "dev")),
    )
    return jax.shard_map(
        on_device,
        mesh=mesh,
        in_specs=placed,
        out_specs=(P(None, "side", None, ("grp", "dev")), P()),
        check_vma=False,
    )
```

profile of v0, /device:TPU:0, one launch (start us, length us, event | category | flops | bytes accessed | tf_op | source)
XLA Modules:
  0.0 402.0 jit_solution(3849384742922778589)
XLA Ops:
  1.6 42.0 %psum.49 = f32[8]{0:T(128)S(1)} all-reduce(f32[8]{0:T(128)S(1)} %fusion.35), channel_id=1, replica_groups=mesh['side'=2,'grp'=2,'dev'=8] {'side','grp','dev'}, use_global_device_ids=true, to_apply=%region_1.0 | all-reduce | flops 8 | bytes 64 | tf_op jit(solution)/shard_map/psum | solution.py:45
  43.7 2.3 collective-permute-start
  47.8 4.2 %collective-permute-start.1 = (bf16[8,256]{1,0:T(8,128)(2,1)S(1)}, bf16[8,256]{1,0:T(8,128)(2,1)S(1)}, u32[]{:S(2)}, u32[]{:S(2)}) collective-permute-start(bf16[8,256]{1,0:T(8,128)(2,1)S(1)} %get-tuple-element.98), channel_id=1, source_target_pairs={{0,4},{1,5},{2,6},{3,7},{4,8},{5,9},{6,10},{7,11},{8,12},{9,13},{1... | collective-permute-start | bytes 12296 | tf_op jit(solution)/shard_map/ppermute | solution.py:18
  52.1 1.3 collective-permute-start.2
  53.4 2.3 collective-permute-start.3
  55.7 5.5 %collective-permute-start.4 = (bf16[8,256]{1,0:T(8,128)(2,1)S(1)}, bf16[8,256]{1,0:T(8,128)(2,1)S(1)}, u32[]{:S(2)}, u32[]{:S(2)}) collective-permute-start(bf16[8,256]{1,0:T(8,128)(2,1)S(1)} %get-tuple-element.98), channel_id=1, source_target_pairs={{0,1},{1,2},{2,3},{3,4},{4,5},{5,6},{6,7},{7,8},{8,9},{9,10},{10,1... | collective-permute-start | bytes 12296 | tf_op jit(solution)/shard_map/ppermute | solution.py:18
  61.3 1.3 collective-permute-start.5
  62.6 1.3 collective-permute-start.6
  63.9 1.3 collective-permute-start.7
  65.2 1.3 collective-permute-start.8
  66.6 1.7 collective-permute-done.6
  68.3 1.9 collective-permute-done.7
  70.2 3.5 collective-permute-done.8
  76.4 3.1 collective-permute-done.9
  79.8 41.6 %psum.50 = f32[1,8]{1,0:T(1,128)S(1)} all-reduce(f32[1,8]{1,0:T(1,128)S(1)} %bitcast.209), channel_id=1, replica_groups=mesh['side'=2,'grp'=2,'dev'=8] {'side','grp','dev'}, use_global_device_ids=true, to_apply=%region_3.4 | all-reduce | flops 8 | bytes 64 | tf_op jit(solution)/shard_map/psum | solution.py:84
  121.6 41.1 %psum.51 = f32[8]{0:T(128)S(1)} all-reduce(f32[8]{0:T(128)S(1)} %get-tuple-element.76), channel_id=1, replica_groups=mesh['side'=2,'grp'=2,'dev'=8] {'side','grp','dev'}, use_global_device_ids=true, to_apply=%region_5.6 | all-reduce | flops 8 | bytes 64 | tf_op jit(solution)/shard_map/psum | solution.py:90
  162.8 2.3 collective-permute-start.10
  165.1 1.6 collective-permute-done.10
  167.0 2.4 collective-permute-start.11
  169.4 1.3 collective-permute-start.12
  170.7 3.5 collective-permute-start.13
  174.3 5.0 %collective-permute-start.14 = (bf16[8,256]{1,0:T(8,128)(2,1)S(1)}, bf16[8,256]{1,0:T(8,128)(2,1)S(1)}, u32[]{:S(2)}, u32[]{:S(2)}) collective-permute-start(bf16[8,256]{1,0:T(8,128)(2,1)S(1)} %get-tuple-element.102), channel_id=1, source_target_pairs={{0,1},{1,2},{2,3},{3,4},{4,5},{5,6},{6,7},{7,8},{8,9},{9,10},{10,1... | collective-permute-start | bytes 12296 | tf_op jit(solution)/shard_map/ppermute | solution.py:18
  179.3 1.3 collective-permute-start.15
  180.6 1.3 collective-permute-start.16
  181.9 1.3 collective-permute-start.17
  183.3 1.3 collective-permute-start.18
  184.6 2.2 collective-permute-done.16
  186.8 1.4 collective-permute-done.17
  188.2 3.9 collective-permute-done.18
  194.2 3.1 collective-permute-done.19
  197.7 41.6 %psum.52 = f32[2,8]{1,0:T(2,128)S(1)} all-reduce(f32[2,8]{1,0:T(2,128)S(1)} %get-tuple-element.81), channel_id=1, replica_groups=mesh['side'=2,'grp'=2,'dev'=8] {'side','grp','dev'}, use_global_device_ids=true, to_apply=%region_7.8 | all-reduce | flops 16 | bytes 128 | tf_op jit(solution)/shard_map/psum | solution.py:84
  239.7 39.8 %psum.53 = f32[8]{0:T(128)S(1)} all-reduce(f32[8]{0:T(128)S(1)} %multiply_reduce_fusion.3), channel_id=1, replica_groups=mesh['side'=2,'grp'=2,'dev'=8] {'side','grp','dev'}, use_global_device_ids=true, to_apply=%region_9.10 | all-reduce | flops 8 | bytes 64 | tf_op jit(solution)/shard_map/psum | solution.py:90
  279.6 2.3 collective-permute-start.20
  283.7 3.6 collective-permute-start.21
  287.4 1.3 collective-permute-start.22
  288.7 2.5 collective-permute-start.23
  291.2 6.1 %collective-permute-start.24 = (bf16[8,256]{1,0:T(8,128)(2,1)S(1)}, bf16[8,256]{1,0:T(8,128)(2,1)S(1)}, u32[]{:S(2)}, u32[]{:S(2)}) collective-permute-start(bf16[8,256]{1,0:T(8,128)(2,1)S(1)} %get-tuple-element.104), channel_id=1, source_target_pairs={{0,1},{1,2},{2,3},{3,4},{4,5},{5,6},{6,7},{7,8},{8,9},{9,10},{10,1... | collective-permute-start | bytes 12296 | tf_op jit(solution)/shard_map/ppermute | solution.py:18
  297.3 1.3 collective-permute-start.25
  298.6 1.3 collective-permute-start.26
  299.9 1.3 collective-permute-start.27
  301.2 1.3 collective-permute-start.28
  302.6 1.7 collective-permute-done.26
  304.4 1.9 collective-permute-done.27
  306.2 3.5 collective-permute-done.28
  313.1 1.3 scatter.24
  315.2 41.4 %psum.54 = f32[3,8]{1,0:T(4,128)S(1)} all-reduce(f32[3,8]{1,0:T(4,128)S(1)} %get-tuple-element.79), channel_id=1, replica_groups=mesh['side'=2,'grp'=2,'dev'=8] {'side','grp','dev'}, use_global_device_ids=true, to_apply=%region_11.12 | all-reduce | flops 24 | bytes 192 | tf_op jit(solution)/shard_map/psum | solution.py:84
  357.1 40.5 %psum.55 = f32[8]{0:T(128)S(1)} all-reduce(f32[8]{0:T(128)S(1)} %multiply_reduce_fusion.2), channel_id=1, replica_groups=mesh['side'=2,'grp'=2,'dev'=8] {'side','grp','dev'}, use_global_device_ids=true, to_apply=%region_13.14 | all-reduce | flops 8 | bytes 64 | tf_op jit(solution)/shard_map/psum | solution.py:90
  398.2 1.8 broadcast_select_fusion
  (111 shorter events, 18.5 us)
Async XLA Ops:
  0.6 73.6 %copy-start = (bf16[1,32,128,128]{3,2,1,0:T(8,128)(2,1)S(1)}, bf16[1,32,128,128]{3,2,1,0:T(8,128)(2,1)}, u32[]{:S(2)}) copy-start(bf16[1,32,128,128]{3,2,1,0:T(8,128)(2,1)} %param.18) | copy-start | bytes 3145732
  0.6 42.9 %copy-start.1 = (f32[1,8,256]{2,1,0:T(8,128)S(1)}, f32[1,8,256]{2,1,0:T(8,128)}, u32[]{:S(2)}) copy-start(f32[1,8,256]{2,1,0:T(8,128)} %param.17) | copy-start | bytes 24580
  43.7 3.9 collective-permute-start
  45.9 0.7 copy-start.4
  46.6 1.0 copy-start.3
  47.8 14.7 %collective-permute-start.1 = (bf16[8,256]{1,0:T(8,128)(2,1)S(1)}, bf16[8,256]{1,0:T(8,128)(2,1)S(1)}, u32[]{:S(2)}, u32[]{:S(2)}) collective-permute-start(bf16[8,256]{1,0:T(8,128)(2,1)S(1)} %get-tuple-element.98), channel_id=1, source_target_pairs={{0,4},{1,5},{2,6},{3,7},{4,8},{5,9},{6,10},{7,11},{8,12},{9,13},{1... | collective-permute-start | bytes 12296 | tf_op jit(solution)/shard_map/ppermute | solution.py:18
  52.1 11.8 %collective-permute-start.2 = (bf16[8,256]{1,0:T(8,128)(2,1)S(1)}, bf16[8,256]{1,0:T(8,128)(2,1)S(1)}, u32[]{:S(2)}, u32[]{:S(2)}) collective-permute-start(bf16[8,256]{1,0:T(8,128)(2,1)S(1)} %get-tuple-element.98), channel_id=1, source_target_pairs={{0,3},{1,4},{2,5},{3,6},{4,7},{5,8},{6,9},{7,10},{8,11},{9,12},{10... | collective-permute-start | bytes 12296 | tf_op jit(solution)/shard_map/ppermute | solution.py:18
  53.4 11.8 %collective-permute-start.3 = (bf16[8,256]{1,0:T(8,128)(2,1)S(1)}, bf16[8,256]{1,0:T(8,128)(2,1)S(1)}, u32[]{:S(2)}, u32[]{:S(2)}) collective-permute-start(bf16[8,256]{1,0:T(8,128)(2,1)S(1)} %get-tuple-element.98), channel_id=1, source_target_pairs={{0,2},{1,3},{2,4},{3,5},{4,6},{5,7},{6,8},{7,9},{8,10},{9,11},{10,... | collective-permute-start | bytes 12296 | tf_op jit(solution)/shard_map/ppermute | solution.py:18
  55.7 10.8 %collective-permute-start.4 = (bf16[8,256]{1,0:T(8,128)(2,1)S(1)}, bf16[8,256]{1,0:T(8,128)(2,1)S(1)}, u32[]{:S(2)}, u32[]{:S(2)}) collective-permute-start(bf16[8,256]{1,0:T(8,128)(2,1)S(1)} %get-tuple-element.98), channel_id=1, source_target_pairs={{0,1},{1,2},{2,3},{3,4},{4,5},{5,6},{6,7},{7,8},{8,9},{9,10},{10,1... | collective-permute-start | bytes 12296 | tf_op jit(solution)/shard_map/ppermute | solution.py:18
  61.3 5.3 %collective-permute-start.5 = (bf16[8,256]{1,0:T(8,128)(2,1)S(1)}, bf16[8,256]{1,0:T(8,128)(2,1)S(1)}, u32[]{:S(2)}, u32[]{:S(2)}) collective-permute-start(bf16[8,256]{1,0:T(8,128)(2,1)S(1)} %get-tuple-element.98), channel_id=1, source_target_pairs={{1,0},{2,1},{3,2},{4,3},{5,4},{6,5},{7,6},{8,7},{9,8},{10,9},{11,1... | collective-permute-start | bytes 12296 | tf_op jit(solution)/shard_map/ppermute | solution.py:18
  62.6 5.8 %collective-permute-start.6 = (bf16[8,256]{1,0:T(8,128)(2,1)S(1)}, bf16[8,256]{1,0:T(8,128)(2,1)S(1)}, u32[]{:S(2)}, u32[]{:S(2)}) collective-permute-start(bf16[8,256]{1,0:T(8,128)(2,1)S(1)} %get-tuple-element.98), channel_id=1, source_target_pairs={{2,0},{3,1},{4,2},{5,3},{6,4},{7,5},{8,6},{9,7},{10,8},{11,9},{12,... | collective-permute-start | bytes 12296 | tf_op jit(solution)/shard_map/ppermute | solution.py:18
  63.9 6.3 %collective-permute-start.7 = (bf16[8,256]{1,0:T(8,128)(2,1)S(1)}, bf16[8,256]{1,0:T(8,128)(2,1)S(1)}, u32[]{:S(2)}, u32[]{:S(2)}) collective-permute-start(bf16[8,256]{1,0:T(8,128)(2,1)S(1)} %get-tuple-element.98), channel_id=1, source_target_pairs={{3,0},{4,1},{5,2},{6,3},{7,4},{8,5},{9,6},{10,7},{11,8},{12,9},{13... | collective-permute-start | bytes 12296 | tf_op jit(solution)/shard_map/ppermute | solution.py:18
  65.2 8.5 %collective-permute-start.8 = (bf16[8,256]{1,0:T(8,128)(2,1)S(1)}, bf16[8,256]{1,0:T(8,128)(2,1)S(1)}, u32[]{:S(2)}, u32[]{:S(2)}) collective-permute-start(bf16[8,256]{1,0:T(8,128)(2,1)S(1)} %get-tuple-element.98), channel_id=1, source_target_pairs={{4,0},{5,1},{6,2},{7,3},{8,4},{9,5},{10,6},{11,7},{12,8},{13,9},{1... | collective-permute-start | bytes 12296 | tf_op jit(solution)/shard_map/ppermute | solution.py:18
  74.9 0.7 copy-start.2
  75.8 3.7 collective-permute-start.9
  162.8 3.9 collective-permute-start.10
  167.0 13.6 %collective-permute-start.11 = (bf16[8,256]{1,0:T(8,128)(2,1)S(1)}, bf16[8,256]{1,0:T(8,128)(2,1)S(1)}, u32[]{:S(2)}, u32[]{:S(2)}) collective-permute-start(bf16[8,256]{1,0:T(8,128)(2,1)S(1)} %get-tuple-element.102), channel_id=1, source_target_pairs={{0,4},{1,5},{2,6},{3,7},{4,8},{5,9},{6,10},{7,11},{8,12},{9,13},{1... | collective-permute-start | bytes 12296 | tf_op jit(solution)/shard_map/ppermute | solution.py:18
  169.4 12.5 %collective-permute-start.12 = (bf16[8,256]{1,0:T(8,128)(2,1)S(1)}, bf16[8,256]{1,0:T(8,128)(2,1)S(1)}, u32[]{:S(2)}, u32[]{:S(2)}) collective-permute-start(bf16[8,256]{1,0:T(8,128)(2,1)S(1)} %get-tuple-element.102), channel_id=1, source_target_pairs={{0,3},{1,4},{2,5},{3,6},{4,7},{5,8},{6,9},{7,10},{8,11},{9,12},{10... | collective-permute-start | bytes 12296 | tf_op jit(solution)/shard_map/ppermute | solution.py:18
  170.7 12.5 %collective-permute-start.13 = (bf16[8,256]{1,0:T(8,128)(2,1)S(1)}, bf16[8,256]{1,0:T(8,128)(2,1)S(1)}, u32[]{:S(2)}, u32[]{:S(2)}) collective-permute-start(bf16[8,256]{1,0:T(8,128)(2,1)S(1)} %get-tuple-element.102), channel_id=1, source_target_pairs={{0,2},{1,3},{2,4},{3,5},{4,6},{5,7},{6,8},{7,9},{8,10},{9,11},{10,... | collective-permute-start | bytes 12296 | tf_op jit(solution)/shard_map/ppermute | solution.py:18
  174.3 10.3 %collective-permute-start.14 = (bf16[8,256]{1,0:T(8,128)(2,1)S(1)}, bf16[8,256]{1,0:T(8,128)(2,1)S(1)}, u32[]{:S(2)}, u32[]{:S(2)}) collective-permute-start(bf16[8,256]{1,0:T(8,128)(2,1)S(1)} %get-tuple-element.102), channel_id=1, source_target_pairs={{0,1},{1,2},{2,3},{3,4},{4,5},{5,6},{6,7},{7,8},{8,9},{9,10},{10,1... | collective-permute-start | bytes 12296 | tf_op jit(solution)/shard_map/ppermute | solution.py:18
  179.3 5.3 %collective-permute-start.15 = (bf16[8,256]{1,0:T(8,128)(2,1)S(1)}, bf16[8,256]{1,0:T(8,128)(2,1)S(1)}, u32[]{:S(2)}, u32[]{:S(2)}) collective-permute-start(bf16[8,256]{1,0:T(8,128)(2,1)S(1)} %get-tuple-element.102), channel_id=1, source_target_pairs={{1,0},{2,1},{3,2},{4,3},{5,4},{6,5},{7,6},{8,7},{9,8},{10,9},{11,1... | collective-permute-start | bytes 12296 | tf_op jit(solution)/shard_map/ppermute | solution.py:18
  180.6 6.2 %collective-permute-start.16 = (bf16[8,256]{1,0:T(8,128)(2,1)S(1)}, bf16[8,256]{1,0:T(8,128)(2,1)S(1)}, u32[]{:S(2)}, u32[]{:S(2)}) collective-permute-start(bf16[8,256]{1,0:T(8,128)(2,1)S(1)} %get-tuple-element.102), channel_id=1, source_target_pairs={{2,0},{3,1},{4,2},{5,3},{6,4},{7,5},{8,6},{9,7},{10,8},{11,9},{12,... | collective-permute-start | bytes 12296 | tf_op jit(solution)/shard_map/ppermute | solution.py:18
  181.9 6.3 %collective-permute-start.17 = (bf16[8,256]{1,0:T(8,128)(2,1)S(1)}, bf16[8,256]{1,0:T(8,128)(2,1)S(1)}, u32[]{:S(2)}, u32[]{:S(2)}) collective-permute-start(bf16[8,256]{1,0:T(8,128)(2,1)S(1)} %get-tuple-element.102), channel_id=1, source_target_pairs={{3,0},{4,1},{5,2},{6,3},{7,4},{8,5},{9,6},{10,7},{11,8},{12,9},{13... | collective-permute-start | bytes 12296 | tf_op jit(solution)/shard_map/ppermute | solution.py:18
  183.3 8.9 %collective-permute-start.18 = (bf16[8,256]{1,0:T(8,128)(2,1)S(1)}, bf16[8,256]{1,0:T(8,128)(2,1)S(1)}, u32[]{:S(2)}, u32[]{:S(2)}) collective-permute-start(bf16[8,256]{1,0:T(8,128)(2,1)S(1)} %get-tuple-element.102), channel_id=1, source_target_pairs={{4,0},{5,1},{6,2},{7,3},{8,4},{9,5},{10,6},{11,7},{12,8},{13,9},{1... | collective-permute-start | bytes 12296 | tf_op jit(solution)/shard_map/ppermute | solution.py:18
  193.6 3.7 collective-permute-start.19
  279.6 3.9 collective-permute-start.20
  283.7 14.9 %collective-permute-start.21 = (bf16[8,256]{1,0:T(8,128)(2,1)S(1)}, bf16[8,256]{1,0:T(8,128)(2,1)S(1)}, u32[]{:S(2)}, u32[]{:S(2)}) collective-permute-start(bf16[8,256]{1,0:T(8,128)(2,1)S(1)} %get-tuple-element.104), channel_id=1, source_target_pairs={{0,4},{1,5},{2,6},{3,7},{4,8},{5,9},{6,10},{7,11},{8,12},{9,13},{1... | collective-permute-start | bytes 12296 | tf_op jit(solution)/shard_map/ppermute | solution.py:18
  287.4 12.5 %collective-permute-start.22 = (bf16[8,256]{1,0:T(8,128)(2,1)S(1)}, bf16[8,256]{1,0:T(8,128)(2,1)S(1)}, u32[]{:S(2)}, u32[]{:S(2)}) collective-permute-start(bf16[8,256]{1,0:T(8,128)(2,1)S(1)} %get-tuple-element.104), channel_id=1, source_target_pairs={{0,3},{1,4},{2,5},{3,6},{4,7},{5,8},{6,9},{7,10},{8,11},{9,12},{10... | collective-permute-start | bytes 12296 | tf_op jit(solution)/shard_map/ppermute | solution.py:18
  288.7 12.5 %collective-permute-start.23 = (bf16[8,256]{1,0:T(8,128)(2,1)S(1)}, bf16[8,256]{1,0:T(8,128)(2,1)S(1)}, u32[]{:S(2)}, u32[]{:S(2)}) collective-permute-start(bf16[8,256]{1,0:T(8,128)(2,1)S(1)} %get-tuple-element.104), channel_id=1, source_target_pairs={{0,2},{1,3},{2,4},{3,5},{4,6},{5,7},{6,8},{7,9},{8,10},{9,11},{10,... | collective-permute-start | bytes 12296 | tf_op jit(solution)/shard_map/ppermute | solution.py:18
  291.2 11.4 %collective-permute-start.24 = (bf16[8,256]{1,0:T(8,128)(2,1)S(1)}, bf16[8,256]{1,0:T(8,128)(2,1)S(1)}, u32[]{:S(2)}, u32[]{:S(2)}) collective-permute-start(bf16[8,256]{1,0:T(8,128)(2,1)S(1)} %get-tuple-element.104), channel_id=1, source_target_pairs={{0,1},{1,2},{2,3},{3,4},{4,5},{5,6},{6,7},{7,8},{8,9},{9,10},{10,1... | collective-permute-start | bytes 12296 | tf_op jit(solution)/shard_map/ppermute | solution.py:18
  297.3 5.3 %collective-permute-start.25 = (bf16[8,256]{1,0:T(8,128)(2,1)S(1)}, bf16[8,256]{1,0:T(8,128)(2,1)S(1)}, u32[]{:S(2)}, u32[]{:S(2)}) collective-permute-start(bf16[8,256]{1,0:T(8,128)(2,1)S(1)} %get-tuple-element.104), channel_id=1, source_target_pairs={{1,0},{2,1},{3,2},{4,3},{5,4},{6,5},{7,6},{8,7},{9,8},{10,9},{11,1... | collective-permute-start | bytes 12296 | tf_op jit(solution)/shard_map/ppermute | solution.py:18
  298.6 5.8 %collective-permute-start.26 = (bf16[8,256]{1,0:T(8,128)(2,1)S(1)}, bf16[8,256]{1,0:T(8,128)(2,1)S(1)}, u32[]{:S(2)}, u32[]{:S(2)}) collective-permute-start(bf16[8,256]{1,0:T(8,128)(2,1)S(1)} %get-tuple-element.104), channel_id=1, source_target_pairs={{2,0},{3,1},{4,2},{5,3},{6,4},{7,5},{8,6},{9,7},{10,8},{11,9},{12,... | collective-permute-start | bytes 12296 | tf_op jit(solution)/shard_map/ppermute | solution.py:18
  299.9 6.3 %collective-permute-start.27 = (bf16[8,256]{1,0:T(8,128)(2,1)S(1)}, bf16[8,256]{1,0:T(8,128)(2,1)S(1)}, u32[]{:S(2)}, u32[]{:S(2)}) collective-permute-start(bf16[8,256]{1,0:T(8,128)(2,1)S(1)} %get-tuple-element.104), channel_id=1, source_target_pairs={{3,0},{4,1},{5,2},{6,3},{7,4},{8,5},{9,6},{10,7},{11,8},{12,9},{13... | collective-permute-start | bytes 12296 | tf_op jit(solution)/shard_map/ppermute | solution.py:18
  301.2 8.5 %collective-permute-start.28 = (bf16[8,256]{1,0:T(8,128)(2,1)S(1)}, bf16[8,256]{1,0:T(8,128)(2,1)S(1)}, u32[]{:S(2)}, u32[]{:S(2)}) collective-permute-start(bf16[8,256]{1,0:T(8,128)(2,1)S(1)} %get-tuple-element.104), channel_id=1, source_target_pairs={{4,0},{5,1},{6,2},{7,3},{8,4},{9,5},{10,6},{11,7},{12,8},{13,9},{1... | collective-permute-start | bytes 12296 | tf_op jit(solution)/shard_map/ppermute | solution.py:18
  311.1 3.7 collective-permute-start.29
where the time goes:
time: 404 us; the launch traced here: 402 us
  blocking collectives  288 us (71%)
  starting transfers between devices  63.3 us (16%)
  waiting for transfers between devices  32 us (8%)
  local copies, waits for them, and re-layouts  7.85 us (2%)
  other arithmetic  5.01 us (1%)
  matrix products  4.45 us (1%)
    psum x3, blocking collectives, on_device(): dot_sums = lax.psum(products_local, ('side', 'grp', 'dev'))  125 us
    psum x3, blocking collectives, on_device(): lax.psum(jnp.sum(remainder * remainder, axis=1), ('side', 'grp', 'dev'))  121 us
    ppermute x24, starting transfers between devices, shifted(): return lax.ppermute(block, axis, route)  54.6 us
    psum x1, blocking collectives, on_device(): squares = lax.psum(jnp.sum(start * start, axis=1), ('side', 'grp', 'dev'))  42 us
    ppermute x24, waiting for transfers between devices, shifted(): return lax.ppermute(block, axis, route)  21.8 us
    ppermute x6, waiting for transfers between devices, swapped(): lax.ppermute(value, axis, [(i, i ^ 1 << distance) for i in range(lax.axis...  10.3 us
    ppermute x6, starting transfers between devices, swapped(): lax.ppermute(value, axis, [(i, i ^ 1 << distance) for i in range(lax.axis...  8.7 us
  transfers between devices with their start and end apart: 30, of which 15 were waited for; matrix products, arithmetic and copies ran while one was open for 1% of the time, Pallas kernels for 0%

commit v1 on v0

v1 whole, which is shorter than its diff:
```python
import functools

import jax
import jax.numpy as jnp
from jax import lax
from jax.experimental import pallas as pl
from jax.experimental.pallas import tpu as pltpu
from jax.sharding import PartitionSpec as P

BLOCK = 128
BLK_DEV = 2
ITERS = 3
ROWS = 8
HALF_RHS = 4
EPSILON = 1e-06
AXES = ("side", "grp", "dev")
VMEM_LIMIT = 48 * 2**20


def position():
    side = lax.axis_index("side")
    dev = lax.axis_index("dev")
    owner = lax.axis_index("grp") * lax.axis_size("dev") + dev
    return side, owner, lax.rem(dev, 2)


def per_rhs(tile):
    column = jnp.sum(tile, axis=1, keepdims=True)
    return column + jnp.concatenate([column[HALF_RHS:], column[:HALF_RHS]], axis=0)


def dot(left, right):
    return per_rhs(jnp.sum(left * right, axis=0))


def mirror_onehot(mirror_ref, block):
    rows = lax.broadcasted_iota(jnp.int32, (BLOCK, BLOCK), 0)
    return (rows == mirror_ref[block : block + 1, :]).astype(jnp.float32)


def exact_dot(left, right, dims):
    return lax.dot_general(
        left, right, (dims, ((), ())),
        precision=lax.Precision.HIGHEST, preferred_element_type=jnp.float32,
    )


def start_kernel(sources_ref, mirror_ref, chunk_ref):
    side, _, _ = position()
    pieces = []
    for block in range(BLK_DEV):
        part = sources_ref[:, block * BLOCK : (block + 1) * BLOCK]
        moved = exact_dot(part, mirror_onehot(mirror_ref, block), ((1,), (0,)))
        pieces.append(jnp.where(side == 0, part, moved))
    tiles = [
        jnp.concatenate([piece[HALF_RHS * c : HALF_RHS * (c + 1)] for piece in pieces], axis=0)
        for c in range(2)
    ]
    pairs = chunk_ref.shape[0] // 2

    def store(pair, carry):
        chunk_ref[2 * pair] = tiles[0]
        chunk_ref[2 * pair + 1] = tiles[1]
        return carry

    lax.fori_loop(0, pairs, store, 0, unroll=pairs <= 32)


def near_product(vector_ref, turned_ref, blocks_ref, places_ref):
    half_of_row = lax.broadcasted_iota(jnp.int32, (ROWS, BLOCK), 0) // HALF_RHS
    count = blocks_ref.shape[0]
    sums = [jnp.zeros((ROWS, BLOCK), jnp.float32) for _ in range(4)]
    for entry in range(count):
        row = places_ref[0, entry]
        col = places_ref[1, entry]
        owner = col // 2
        turn = lax.rem(row + col, 2)
        tile = turned_ref[turn, owner]
        tile = jnp.where(half_of_row == row, tile, 0.0).astype(jnp.bfloat16)
        product = lax.dot_general(
            tile, blocks_ref[entry], (((1,), (1,)), ((), ())), preferred_element_type=jnp.float32
        )
        sums[entry % 4] = sums[entry % 4] + product
    return (sums[0] + sums[1]) + (sums[2] + sums[3])


def image(vector_ref, turned_ref, own_ref, other_ref, own_places, other_places):
    side, owner, core = position()
    owners = vector_ref.shape[0] // 2
    first = side * owners

    def fill(index, carry):
        tile = vector_ref[first + index]
        turned_ref[0, index] = tile
        turned_ref[1, index] = jnp.concatenate([tile[HALF_RHS:], tile[:HALF_RHS]], axis=0)
        return carry

    lax.fori_loop(0, owners, fill, 0, unroll=owners <= 32)
    own = near_product(vector_ref, turned_ref, own_ref, own_places)
    other = near_product(vector_ref, turned_ref, other_ref, other_places)
    base = owner - core
    low = jnp.where(core == 0, own, other) + 0.5 * turned_ref[0, base]
    high = jnp.where(core == 0, other, own) + 0.5 * turned_ref[0, base + 1]
    return low, high


def spread(chunk_ref, low, high):
    chips = chunk_ref.shape[0]

    def store(chip, carry):
        chunk_ref[chip, 0] = low
        chunk_ref[chip, 1] = high
        return carry

    lax.fori_loop(0, chips, store, 0, unroll=chips <= 32)


def first_kernel(total, got_ref, own_ref, other_ref, own_places, other_places, chunk_ref,
                 basis_ref, turned_ref):
    owners = got_ref.shape[0] // 2
    port = got_ref[:owners]
    star = got_ref[owners:]
    squares = per_rhs(jnp.sum(port * port + star * star, axis=0))
    scale = 1.0 / jnp.sqrt(squares * (1.0 / total) + EPSILON)
    basis_ref[:owners] = (port + star) * scale
    basis_ref[owners:] = (port - star) * scale
    low, high = image(basis_ref, turned_ref, own_ref, other_ref, own_places, other_places)
    spread(chunk_ref, low, high)


def orthogonalized(total, got, basis_refs):
    inner = 0.5 / total
    coeffs = [dot(got, ref[...]) * inner for ref in basis_refs]
    rest = got
    for coeff, ref in zip(coeffs, basis_refs):
        rest = rest - coeff * ref[...]
    norm = jnp.sqrt(dot(rest, rest) * inner + EPSILON)
    return coeffs, norm, rest * (1.0 / norm)


def columns(values):
    lane = lax.broadcasted_iota(jnp.int32, (ROWS, BLOCK), 1)
    tile = jnp.zeros((ROWS, BLOCK), jnp.float32)
    for index, value in enumerate(values):
        tile = jnp.where(lane == index, value, tile)
    return tile


def middle_kernel(total, got_ref, basis_ref, own_ref, other_ref, own_places, other_places,
                  chunk_ref, next_ref, coeff_ref, turned_ref):
    coeffs, norm, vector = orthogonalized(total, got_ref[...], [basis_ref])
    next_ref[...] = vector
    coeff_ref[...] = columns(coeffs + [norm])
    low, high = image(next_ref, turned_ref, own_ref, other_ref, own_places, other_places)
    spread(chunk_ref, low, high)


def last_kernel(total, got_ref, zero_ref, one_ref, coeff_ref, own_ref, other_ref, own_places,
                other_places, chunk_ref, mine_ref, theirs_ref, two_ref, turned_ref):
    side, owner, core = position()
    owners = got_ref.shape[0] // 2
    inner = 0.5 / total
    coeffs, norm, vector = orthogonalized(total, got_ref[...], [zero_ref, one_ref])
    two_ref[...] = vector
    refs = [zero_ref, one_ref, two_ref]
    gram = [
        dot(refs[i][...], refs[j][...]) * inner for i in range(ITERS) for j in range(i, ITERS)
    ]
    low, high = image(two_ref, turned_ref, own_ref, other_ref, own_places, other_places)
    base = side * owners + owner - core
    partial = [per_rhs(low * ref[base] + high * ref[base + 1]) for ref in refs]
    partial.append(per_rhs(low * low + high * high))
    first = coeff_ref[...]
    sums = columns(partial + [first[:, 0:1], first[:, 1:2]] + coeffs + [norm] + gram)
    chips = chunk_ref.shape[0] // 2

    def store(chip, carry):
        chunk_ref[2 * chip, 0] = low
        chunk_ref[2 * chip, 1] = sums
        chunk_ref[2 * chip + 1, 0] = high
        chunk_ref[2 * chip + 1, 1] = sums
        return carry

    lax.fori_loop(0, chips, store, 0, unroll=chips <= 32)
    for index, ref in enumerate(refs):
        for half in range(2):
            mine_ref[2 * index + half] = ref[half * owners + owner]
            theirs_ref[2 * index + half] = ref[half * owners + owner + 1 - 2 * core]


def final_kernel(total, got_ref, mine_ref, theirs_ref, mirror_ref, basis_ref, hessenberg_ref):
    side, owner, core = position()
    devices = got_ref.shape[0]
    owners = devices // 2
    inner = 0.5 / total
    lane3 = lax.broadcasted_iota(jnp.int32, (ROWS, ITERS), 1)
    entries = []
    halves = []
    for which in range(2):
        sums = got_ref[which, 1]
        for device in range(1, devices // 2):
            sums = sums + got_ref[2 * device + which, 1]
        known = got_ref[which, 1]
        coeffs = [sums[:, j : j + 1] * inner for j in range(ITERS)]
        gram = {}
        place = 9
        for i in range(ITERS):
            for j in range(i, ITERS):
                gram[i, j] = gram[j, i] = known[:, place : place + 1]
                place += 1
        squares = sums[:, ITERS : ITERS + 1] * inner
        for i in range(ITERS):
            weight = -2.0 * coeffs[i]
            for j in range(ITERS):
                weight = weight + coeffs[j] * gram[i, j]
            squares = squares + coeffs[i] * weight
        norm = jnp.sqrt(jnp.maximum(squares, 0.0) + EPSILON)
        entries.append(
            {
                (0, 0): known[:, 4:5], (1, 0): known[:, 5:6],
                (0, 1): known[:, 6:7], (1, 1): known[:, 7:8], (2, 1): known[:, 8:9],
                (0, 2): coeffs[0], (1, 2): coeffs[1], (2, 2): coeffs[2], (3, 2): norm,
            }
        )
        is_mine = core == which
        tiles = [jnp.where(is_mine, mine_ref[n], theirs_ref[n]) for n in range(2 * ITERS)]
        scale = 1.0 / norm
        for half in range(2):
            rest = got_ref[half * owners + owner - core + which, 0]
            for j in range(ITERS):
                rest = rest - coeffs[j] * tiles[2 * j + half]
            tiles.append(rest * scale)
        halves.append(tiles)
    for block in range(BLK_DEV):
        onehot = mirror_onehot(mirror_ref, block)
        rows = slice(block * HALF_RHS, (block + 1) * HALF_RHS)
        stacked = []
        for vector in range(ITERS + 1):
            sym = jnp.concatenate([tiles[2 * vector][rows] for tiles in halves], axis=0)
            anti = jnp.concatenate([tiles[2 * vector + 1][rows] for tiles in halves], axis=0)
            stacked.append((0.5 * (sym + anti), 0.5 * (sym - anti)))
        star = jnp.concatenate([pair[1] for pair in stacked], axis=0)
        back = exact_dot(star, onehot, ((1,), (1,)))
        for vector in range(ITERS + 1):
            basis_ref[vector, :, block * BLOCK : (block + 1) * BLOCK] = jnp.where(
                side == 0, stacked[vector][0], back[vector * ROWS : (vector + 1) * ROWS]
            )
    for j in range(ITERS + 1):
        row = jnp.zeros((ROWS, ITERS), jnp.float32)
        for k in range(ITERS):
            if (j, k) in entries[0]:
                both = jnp.concatenate(
                    [entry[j, k][:HALF_RHS] for entry in entries], axis=0
                )
                row = jnp.where(lane3 == k, both, row)
        hessenberg_ref[:, j, :] = row


VMEM = pl.BlockSpec(memory_space=pltpu.VMEM)
SMEM = pl.BlockSpec(memory_space=pltpu.SMEM)


def call(kernel, outs, specs, scratch=(), name=None):
    return pl.pallas_call(
        kernel,
        out_shape=[jax.ShapeDtypeStruct(shape, jnp.float32) for shape in outs],
        in_specs=specs,
        out_specs=[VMEM] * len(outs),
        scratch_shapes=[pltpu.VMEM(shape, jnp.float32) for shape in scratch],
        compiler_params=pltpu.CompilerParams(vmem_limit_bytes=VMEM_LIMIT),
        name=name,
    )


def on_device(sources, near_blocks, block_rows, block_cols, mirror):
    devices = lax.axis_size(AXES)
    owners = devices // 2
    chips = devices // 2
    panels = sources.shape[2]
    total = 1.0 * panels * devices
    partner = [(i, i ^ 1) for i in range(devices)]
    same_core = [[i for i in range(devices) if i % 2 == core] for core in range(2)]
    mirror_rows = mirror.reshape(BLK_DEV, BLOCK)
    blocks = near_blocks[0]
    places = jnp.concatenate([block_rows, block_cols], axis=0)
    other_blocks = lax.ppermute(blocks, AXES, partner)
    other_places = lax.ppermute(places, AXES, partner)
    near = (blocks, other_blocks, places, other_places)
    near_specs = [VMEM, VMEM, SMEM, SMEM]
    vector = (devices, ROWS, BLOCK)
    chunk = (chips, 2, ROWS, BLOCK)
    turned = (2, owners, ROWS, BLOCK)

    def exchanged(chunks):
        got = lax.all_to_all(chunks, AXES, 0, 0, axis_index_groups=same_core)
        return got.reshape(vector)

    [chunks] = call(start_kernel, [vector], [VMEM, VMEM], name="start")(sources[0], mirror_rows)
    got = lax.all_to_all(chunks, AXES, 0, 0)
    chunks, zero = call(
        functools.partial(first_kernel, total), [chunk, vector], [VMEM] + near_specs, [turned],
        name="first",
    )(got, *near)
    got = exchanged(chunks)
    chunks, one, coeff = call(
        functools.partial(middle_kernel, total), [chunk, vector, (ROWS, BLOCK)],
        [VMEM, VMEM] + near_specs, [turned], name="middle",
    )(got, zero, *near)
    got = exchanged(chunks)
    kept = (2 * ITERS, ROWS, BLOCK)
    chunks, mine, theirs = call(
        functools.partial(last_kernel, total), [(devices, 2, ROWS, BLOCK), kept, kept],
        [VMEM] * 4 + near_specs, [vector, turned], name="last",
    )(got, zero, one, coeff, *near)
    returned = lax.ppermute(theirs, AXES, partner)
    got = lax.all_to_all(chunks, AXES, 0, 0)
    basis, hessenberg = call(
        functools.partial(final_kernel, total),
        [(ITERS + 1, ROWS, panels), (ROWS, ITERS + 1, ITERS)], [VMEM] * 4, name="final",
    )(got, mine, returned, mirror_rows)
    return basis[:, None], hessenberg


def solution(mesh):
    placed = (
        P("side", None, ("grp", "dev")),
        P("side", ("grp", "dev"), None, None),
        P("side", ("grp", "dev")),
        P("side", ("grp", "dev")),
        P(("grp", "dev")),
    )
    return jax.shard_map(
        on_device,
        mesh=mesh,
        in_specs=placed,
        out_specs=(P(None, "side", None, ("grp", "dev")), P()),
        check_vma=False,
    )
```

time: 404 us -> 63.5 us (0.16)
  blocking collectives: 288 us -> 21.4 us
  starting transfers between devices: 63.3 us -> 10.6 us
  waiting for transfers between devices: 32 us -> 18 us
  Pallas kernels: 0 us -> 9.17 us
  other arithmetic: 5.01 us -> 0.01 us
  local copies, waits for them, and re-layouts: 7.85 us -> 3.3 us
  matrix products: 4.45 us -> 0 us
    psum x7 -> x0, blocking collectives: 288 us -> none  [the longest x3 125 us: on_device(): dot_sums = lax.psum(products_local, ('side', 'grp', 'dev'))]
    ppermute x30 -> x3, starting transfers between devices: 63.3 us -> 1.01 us  [the longest x1 0.52 us: on_device(): other_blocks = lax.ppermute(blocks, AXES, partner)]
    ppermute x30 -> x3, waiting for transfers between devices: 32 us -> 1.97 us  [the longest x1 1.08 us: on_device(): returned = lax.ppermute(theirs, AXES, partner)]
    all_to_all x0 -> x2, blocking collectives: none -> 21.4 us  [exchanged(): got = lax.all_to_all(chunks, AXES, 0, 0, axis_index_groups=same_core)]
    all_to_all x0 -> x2, waiting for transfers between devices: none -> 16.1 us  [on_device(): got = lax.all_to_all(chunks, AXES, 0, 0)]
    all_to_all x0 -> x2, starting transfers between devices: none -> 9.54 us  [on_device(): got = lax.all_to_all(chunks, AXES, 0, 0)]
    pallas_call x0 -> x5, Pallas kernels: none -> 9.17 us  [the longest x1 3.02 us: on_device(): call(functools.partial(last_kernel, total), [(devices, 2, ROWS, BLOCK), k...]
    dot_general x14 -> x0, matrix products: 4.45 us -> none  [the longest x3 1.9 us: on_device(): jnp.einsum('rkj,kij->rki', picked, blocks, preferred_element_type=jnp.flo...]
  transfers between devices with their start and end apart: 30 -> 5, of which waited for: 15 -> 4; matrix products, arithmetic and copies ran while one was open for 1% -> 0% of each run, Pallas kernels for 0% -> 1%
where the time goes in v1:
time: 63.5 us; the launch traced here: 63.1 us
  blocking collectives  21.4 us (34%)
  waiting for transfers between devices  18 us (28%)
  starting transfers between devices  10.6 us (17%)
  Pallas kernels  9.17 us (14%)
  local copies, waits for them, and re-layouts  3.3 us (5%)
  between operations  0.7 us (1%)
    all_to_all x2, blocking collectives, exchanged(): got = lax.all_to_all(chunks, AXES, 0, 0, axis_index_groups=same_core)  21.4 us
    all_to_all x2, waiting for transfers between devices, on_device(): got = lax.all_to_all(chunks, AXES, 0, 0)  16.1 us
    all_to_all x2, starting transfers between devices, on_device(): got = lax.all_to_all(chunks, AXES, 0, 0)  9.54 us
    unnamed x13, local copies, waits for them, and re-layouts  3.3 us
    pallas_call x1, Pallas kernels, on_device(): call(functools.partial(last_kernel, total), [(devices, 2, ROWS, BLOCK), k...  3.02 us
    pallas_call x1, Pallas kernels, on_device(): call(functools.partial(middle_kernel, total), [chunk, vector, (ROWS, BLOC...  2.15 us
    pallas_call x1, Pallas kernels, on_device(): call(functools.partial(first_kernel, total), [chunk, vector], [VMEM] + ne...  1.93 us
  transfers between devices with their start and end apart: 5, of which 4 were waited for; matrix products, arithmetic and copies ran while one was open for 0% of the time, Pallas kernels for 1%

profile of v1, /device:TPU:0, one launch (start us, length us, event | category | flops | bytes accessed | tf_op | source)
XLA Modules:
  0.0 63.1 jit_solution(14544931257139648111)
XLA Ops:
  0.6 0.5 collective-permute-start
  1.1 0.0 copy-start.3
  1.1 0.7 %copy-done.3 = s32[256]{0:T(256)S(1)} copy-done((s32[256]{0:T(256)S(1)}, s32[256]{0:T(256)}, u32[]{:S(2)}) %copy-start.3) | copy-done | bytes 1048
  1.8 0.0 copy-start.2
  1.8 0.7 %copy-done.2 = f32[1,8,256]{2,1,0:T(8,128)S(1)} copy-done((f32[1,8,256]{2,1,0:T(8,128)S(1)}, f32[1,8,256]{2,1,0:T(8,128)}, u32[]{:S(2)}) %copy-start.2) | copy-done | bytes 8216
  2.5 0.9 %start.1 = f32[32,8,128]{2,1,0:T(8,128)} custom-call(f32[8,256]{1,0:T(8,128)S(1)} %bitcast.14, s32[2,128]{1,0:T(2,128)S(1)} %bitcast.15), custom_call_target="tpu_custom_call" | custom-call | tf_op jit(solution)/shard_map/start/pallas_call | solution.py:298
  3.4 0.0 copy-start.4
  3.4 0.0 copy-start.5
  3.4 7.0 %all-to-all-start = ((f32[32,8,128]{2,1,0:T(8,128)}), f32[32,8,128]{2,1,0:T(8,128)S(1)}, u32[]{:S(2)}, u32[]{:S(2)}) async-start(f32[32,8,128]{2,1,0:T(8,128)} %start.1), calls=%async_computation | async-start | bytes 262144 | tf_op jit(solution)/shard_map/all_to_all | solution.py:299
  10.4 0.0 copy-done.4
  10.4 0.0 copy-done.5
  10.4 0.3 collective-permute-start.1
  10.7 0.9 %collective-permute-done.1.other_places = s32[2,32]{1,0:T(2,128)S(1)} collective-permute-done((s32[2,32]{1,0:T(2,128)S(1)}, s32[2,32]{1,0:T(2,128)S(1)}, u32[]{:S(2)}, u32[]{:S(2)}) %collective-permute-start.1) | collective-permute-done | bytes 288 | tf_op jit(solution)/shard_map/ppermute | solution.py:287
  11.6 6.9 %all-to-all-done.got_ref = f32[32,8,128]{2,1,0:T(8,128)S(1)} async-done(((f32[32,8,128]{2,1,0:T(8,128)}), f32[32,8,128]{2,1,0:T(8,128)S(1)}, u32[]{:S(2)}, u32[]{:S(2)}) %all-to-all-start) | async-done | bytes 131104 | tf_op jit(solution)/shard_map/all_to_all | solution.py:299
  18.6 0.0 collective-permute-done.other_ref
  18.6 0.0 copy-start
  18.6 1.2 %copy-done = bf16[1,32,128,128]{3,2,1,0:T(8,128)(2,1)S(1)} copy-done((bf16[1,32,128,128]{3,2,1,0:T(8,128)(2,1)S(1)}, bf16[1,32,128,128]{3,2,1,0:T(8,128)(2,1)}, u32[]{:S(2)}) %copy-start) | copy-done | bytes 1048600
  19.8 0.0 copy-start.1
  19.8 1.9 %first.1 = (f32[16,2,8,128]{3,2,1,0:T(8,128)S(1)}, f32[32,8,128]{2,1,0:T(8,128)S(1)}) custom-call(f32[32,8,128]{2,1,0:T(8,128)S(1)} %all-to-all-done.got_ref, bf16[32,128,128]{2,1,0:T(8,128)(2,1)S(1)} %bitcast.9, bf16[32,128,128]{2,1,0:T(8,128)(2,1)S(1)} %collective-permute-done.other_ref, s32[2,32]{1,0:T(2,128)S(1)} %pad_add_fusion.own_places, ...), custom_call_target="tpu_custom_call" | custom-call | tf_op jit(solution)/shard_map/first/pallas_call | solution.py:300
  21.7 11.0 %all_to_all.20 = f32[16,2,8,128]{3,2,1,0:T(8,128)S(1)} all-to-all(f32[16,2,8,128]{3,2,1,0:T(8,128)S(1)} %get-tuple-element.12), channel_id=1, replica_groups={{0,2,4,6,8,10,12,14,16,18,20,22,24,26,28,30},{1,3,5,7,9,11,13,15,17,19,..., dimensions={0} | all-to-all | bytes 262144 | tf_op jit(solution)/shard_map/all_to_all | solution.py:295
  32.7 0.0 copy-done.1
  32.8 2.1 %middle.1 = (f32[16,2,8,128]{3,2,1,0:T(8,128)S(1)}, f32[32,8,128]{2,1,0:T(8,128)S(1)}, f32[8,128]{1,0:T(8,128)S(1)}) custom-call(f32[32,8,128]{2,1,0:T(8,128)S(1)} %bitcast.13, f32[32,8,128]{2,1,0:T(8,128)S(1)} %get-tuple-element.13.basis_ref.zero_ref, bf16[32,128,128]{2,1,0:T(8,128)(2,1)S(1)} %bitcast.10, ...), custom_call_target="tpu_custom_call" | custom-call | tf_op jit(solution)/shard_map/middle/pallas_call | solution.py:305
  34.9 10.3 %all_to_all.21 = f32[16,2,8,128]{3,2,1,0:T(8,128)S(1)} all-to-all(f32[16,2,8,128]{3,2,1,0:T(8,128)S(1)} %get-tuple-element.14), channel_id=1, replica_groups={{0,2,4,6,8,10,12,14,16,18,20,22,24,26,28,30},{1,3,5,7,9,11,13,15,17,19,..., dimensions={0} | all-to-all | bytes 262144 | tf_op jit(solution)/shard_map/all_to_all | solution.py:295
  45.3 3.0 %last.1 = (f32[32,2,8,128]{3,2,1,0:T(8,128)}, f32[6,8,128]{2,1,0:T(8,128)S(1)}, f32[6,8,128]{2,1,0:T(8,128)S(1)}) custom-call(f32[32,8,128]{2,1,0:T(8,128)S(1)} %bitcast.12, f32[32,8,128]{2,1,0:T(8,128)S(1)} %get-tuple-element.13.basis_ref.zero_ref, f32[32,8,128]{2,1,0:T(8,128)S(1)} %get-tuple-element.15.one_ref, f32[8,128]{1,0:T(8,128)S(1)} %get-tuple-element.16.coeff_ref, ...), custom_call_target="tpu_custom_call" | custom-call | tf_op jit(solution)/shard_map/last/pallas_call | solution.py:311
  48.3 2.6 %all-to-all-start.3 = ((f32[32,2,8,128]{3,2,1,0:T(8,128)}), f32[32,2,8,128]{3,2,1,0:T(8,128)S(1)}, u32[]{:S(2)}, u32[]{:S(2)}) async-start(f32[32,2,8,128]{3,2,1,0:T(8,128)} %get-tuple-element.17), calls=%async_computation.3 | async-start | bytes 524288 | tf_op jit(solution)/shard_map/all_to_all | solution.py:316
  50.9 0.2 collective-permute-start.2
  51.0 1.1 %collective-permute-done.2.theirs_ref = f32[6,8,128]{2,1,0:T(8,128)S(1)} collective-permute-done((f32[6,8,128]{2,1,0:T(8,128)S(1)}, f32[6,8,128]{2,1,0:T(8,128)S(1)}, u32[]{:S(2)}, u32[]{:S(2)}) %collective-permute-start.2) | collective-permute-done | bytes 24608 | tf_op jit(solution)/shard_map/ppermute | solution.py:315
  52.1 9.1 %all-to-all-done.3.got_ref = f32[32,2,8,128]{3,2,1,0:T(8,128)S(1)} async-done(((f32[32,2,8,128]{3,2,1,0:T(8,128)}), f32[32,2,8,128]{3,2,1,0:T(8,128)S(1)}, u32[]{:S(2)}, u32[]{:S(2)}) %all-to-all-start.3) | async-done | bytes 262176 | tf_op jit(solution)/shard_map/all_to_all | solution.py:316
  61.2 1.2 %final.1 = (f32[4,8,256]{2,1,0:T(8,128)}, f32[8,4,3]{2,1,0:T(4,128)S(1)}) custom-call(f32[32,2,8,128]{3,2,1,0:T(8,128)S(1)} %all-to-all-done.3.got_ref, f32[6,8,128]{2,1,0:T(8,128)S(1)} %get-tuple-element.18.mine_ref, f32[6,8,128]{2,1,0:T(8,128)S(1)} %collective-permute-done.2.theirs_ref, s32[2,128]{1,0:T(2,128)S(1)} %bitcast.16), custom_call_target="tpu_custom_call" | custom-call | tf_op jit(solution)/shard_map/final/pallas_call | solution.py:317
  62.4 0.7 %copy.8 = f32[8,4,3]{0,1,2:T(4,128)} copy(f32[8,4,3]{2,1,0:T(4,128)S(1)} %get-tuple-element.23) | data formatting | bytes 768
  (1 shorter events, 0.0 us)
Async XLA Ops:
  0.6 17.9 %collective-permute-start = (bf16[32,128,128]{2,1,0:T(8,128)(2,1)}, bf16[32,128,128]{2,1,0:T(8,128)(2,1)S(1)}, u32[]{:S(2)}, u32[]{:S(2)}) collective-permute-start(bf16[32,128,128]{2,1,0:T(8,128)(2,1)} %bitcast.8), channel_id=1, source_target_pairs={{0,1},{1,0},{2,3},{3,2},{4,5},{5,4},{6,7},{7,6},{8,9},{9,8},{10,11... | collective-permute-start | bytes 3145736 | tf_op jit(solution)/shard_map/ppermute | solution.py:286
  1.1 0.7 %copy-start.3 = (s32[256]{0:T(256)S(1)}, s32[256]{0:T(256)}, u32[]{:S(2)}) copy-start(s32[256]{0:T(256)} %param.9) | copy-start | bytes 3076
  1.8 0.7 %copy-start.2 = (f32[1,8,256]{2,1,0:T(8,128)S(1)}, f32[1,8,256]{2,1,0:T(8,128)}, u32[]{:S(2)}) copy-start(f32[1,8,256]{2,1,0:T(8,128)} %param.5) | copy-start | bytes 24580
  3.4 7.0 %copy-start.4 = (s32[1,32]{1,0:T(1,128)S(1)}, s32[1,32]{1,0:T(1,128)}, u32[]{:S(2)}) copy-start(s32[1,32]{1,0:T(1,128)} %param.8) | copy-start | bytes 388
  3.4 7.0 %copy-start.5 = (s32[1,32]{1,0:T(1,128)S(1)}, s32[1,32]{1,0:T(1,128)}, u32[]{:S(2)}) copy-start(s32[1,32]{1,0:T(1,128)} %param.7) | copy-start | bytes 388
  3.4 15.1 %all-to-all-start = ((f32[32,8,128]{2,1,0:T(8,128)}), f32[32,8,128]{2,1,0:T(8,128)S(1)}, u32[]{:S(2)}, u32[]{:S(2)}) async-start(f32[32,8,128]{2,1,0:T(8,128)} %start.1), calls=%async_computation | async-start | bytes 262144 | tf_op jit(solution)/shard_map/all_to_all | solution.py:299
  10.4 1.2 %collective-permute-start.1 = (s32[2,32]{1,0:T(2,128)S(1)}, s32[2,32]{1,0:T(2,128)S(1)}, u32[]{:S(2)}, u32[]{:S(2)}) collective-permute-start(s32[2,32]{1,0:T(2,128)S(1)} %pad_add_fusion.own_places), channel_id=1, source_target_pairs={{0,1},{1,0},{2,3},{3,2},{4,5},{5,4},{6,7},{7,6},{8,9},{9,8},{10,11... | collective-permute-start | bytes 776 | tf_op jit(solution)/shard_map/ppermute | solution.py:287
  18.6 1.2 %copy-start = (bf16[1,32,128,128]{3,2,1,0:T(8,128)(2,1)S(1)}, bf16[1,32,128,128]{3,2,1,0:T(8,128)(2,1)}, u32[]{:S(2)}) copy-start(bf16[1,32,128,128]{3,2,1,0:T(8,128)(2,1)} %param.6) | copy-start | bytes 3145732
  19.8 13.0 %copy-start.1 = (bf16[1,32,128,128]{3,2,1,0:T(8,128)(2,1)S(1)}, bf16[1,32,128,128]{3,2,1,0:T(8,128)(2,1)}, u32[]{:S(2)}) copy-start(bf16[1,32,128,128]{3,2,1,0:T(8,128)(2,1)} %param.6) | copy-start | bytes 3145732
  48.3 13.0 %all-to-all-start.3 = ((f32[32,2,8,128]{3,2,1,0:T(8,128)}), f32[32,2,8,128]{3,2,1,0:T(8,128)S(1)}, u32[]{:S(2)}, u32[]{:S(2)}) async-start(f32[32,2,8,128]{3,2,1,0:T(8,128)} %get-tuple-element.17), calls=%async_computation.3 | async-start | bytes 524288 | tf_op jit(solution)/shard_map/all_to_all | solution.py:316
  50.9 1.3 %collective-permute-start.2 = (f32[6,8,128]{2,1,0:T(8,128)S(1)}, f32[6,8,128]{2,1,0:T(8,128)S(1)}, u32[]{:S(2)}, u32[]{:S(2)}) collective-permute-start(f32[6,8,128]{2,1,0:T(8,128)S(1)} %get-tuple-element.19), channel_id=1, source_target_pairs={{0,1},{1,0},{2,3},{3,2},{4,5},{5,4},{6,7},{7,6},{8,9},{9,8},{10,11... | collective-permute-start | bytes 73736 | tf_op jit(solution)/shard_map/ppermute | solution.py:315

commit v2 on v0

v2 whole, which is shorter than its diff:
```python
import functools

import jax
import jax.numpy as jnp
from jax import lax
from jax.experimental import pallas as pl
from jax.experimental.pallas import tpu as pltpu
from jax.sharding import PartitionSpec as P

BLOCK = 128
BLK_DEV = 2
ITERS = 3
ROWS = 8
HALF_RHS = 4
EPSILON = 1e-06
AXES = ("side", "grp", "dev")
VMEM_LIMIT = 48 * 2**20
PAIRS = [(i, j) for i in range(ITERS) for j in range(i, ITERS)]


def position():
    side = lax.axis_index("side")
    dev = lax.axis_index("dev")
    owner = lax.axis_index("grp") * lax.axis_size("dev") + dev
    return side, owner, lax.rem(dev, 2)


def iota(shape, axis):
    return lax.broadcasted_iota(jnp.int32, shape, axis)


def per_rhs(tile):
    column = jnp.sum(tile, axis=1, keepdims=True)
    return column + jnp.concatenate([column[HALF_RHS:], column[:HALF_RHS]], axis=0)


def dot(left, right):
    return per_rhs(jnp.sum(left * right, axis=0))


def columns(values):
    lane = iota((ROWS, BLOCK), 1)
    tile = jnp.zeros((ROWS, BLOCK), jnp.float32)
    for index, value in values.items():
        tile = jnp.where(lane == index, value, tile)
    return tile


def mirror_onehot(mirror_ref, block):
    return (iota((BLOCK, BLOCK), 0) == mirror_ref[block : block + 1, :]).astype(jnp.float32)


def exact_dot(left, right, dims):
    return lax.dot_general(
        left, right, (dims, ((), ())),
        precision=lax.Precision.HIGHEST, preferred_element_type=jnp.float32,
    )


def start_kernel(sources_hbm, mirror_hbm, chunk_ref, sources_ref, mirror_ref, sems):
    copies = [
        pltpu.make_async_copy(sources_hbm, sources_ref, sems.at[0]),
        pltpu.make_async_copy(mirror_hbm, mirror_ref, sems.at[1]),
    ]
    for copy in copies:
        copy.start()
    for copy in copies:
        copy.wait()
    side, _, _ = position()
    pieces = []
    for block in range(BLK_DEV):
        part = sources_ref[:, block * BLOCK : (block + 1) * BLOCK]
        moved = exact_dot(part, mirror_onehot(mirror_ref, block), ((1,), (0,)))
        pieces.append(jnp.where(side == 0, part, moved))
    tiles = [
        jnp.concatenate([piece[HALF_RHS * c : HALF_RHS * (c + 1)] for piece in pieces], axis=0)
        for c in range(2)
    ]
    chips = chunk_ref.shape[0] // 2

    def store(chip, carry):
        chunk_ref[2 * chip] = tiles[0]
        chunk_ref[2 * chip + 1] = tiles[1]
        return carry

    lax.fori_loop(0, chips, store, 0, unroll=chips <= 32)


def prepare_kernel(blocks_hbm, own_places, other_places, blocks_ref, pick_ref, sem):
    copy = pltpu.make_async_copy(blocks_hbm, blocks_ref, sem)
    copy.start()
    width = pick_ref.shape[1]
    half_of_row = iota((ROWS, width), 0) // HALF_RHS
    rhs_of_row = iota((ROWS, width), 0) % HALF_RHS
    lane = iota((ROWS, width), 1)
    for entry in range(blocks_ref.shape[0]):
        picks = []
        for places in (own_places, other_places):
            place = jnp.where(
                half_of_row == places[0, entry], HALF_RHS * places[1, entry] + rhs_of_row, -1
            )
            picks.append((lane == place).astype(jnp.float32))
        first = 2 * ROWS * entry
        pick_ref[first : first + 2 * ROWS, :] = jnp.concatenate(picks, axis=0).astype(jnp.bfloat16)
    copy.wait()


def image(vector_ref, pick_ref, own_ref, other_ref):
    side, owner, core = position()
    owners = vector_ref.shape[0] // 2
    half = vector_ref[pl.ds(side * owners, owners)]
    rounded = half.reshape(owners * ROWS, BLOCK).astype(jnp.bfloat16)
    picked = lax.dot_general(
        pick_ref[...], rounded, (((1,), (0,)), ((), ())), preferred_element_type=jnp.float32
    ).astype(jnp.bfloat16)
    sums = [jnp.zeros((2 * ROWS, 2 * BLOCK), jnp.float32) for _ in range(2)]
    for entry in range(0, own_ref.shape[0], 2):
        first = 2 * ROWS * entry
        left = jnp.concatenate(
            [picked[first : first + 2 * ROWS], picked[first + 2 * ROWS : first + 4 * ROWS]], axis=1
        )
        right = jnp.concatenate(
            [jnp.concatenate([ref[entry], ref[entry + 1]], axis=1) for ref in (own_ref, other_ref)],
            axis=0,
        )
        sums[entry // 2 % 2] += lax.dot_general(
            left, right, (((1,), (1,)), ((), ())), preferred_element_type=jnp.float32
        )
    total = sums[0] + sums[1]
    own = total[:ROWS, :BLOCK]
    other = total[ROWS:, BLOCK:]
    base = side * owners + owner - core
    low = jnp.where(core == 0, own, other) + 0.5 * vector_ref[base]
    high = jnp.where(core == 0, other, own) + 0.5 * vector_ref[base + 1]
    return low, high


def spread(chunk_ref, low, high):
    chips = chunk_ref.shape[0]

    def store(chip, carry):
        chunk_ref[chip, 0] = low
        chunk_ref[chip, 1] = high
        return carry

    lax.fori_loop(0, chips, store, 0, unroll=chips <= 32)


def first_kernel(total, got_ref, pick_ref, own_ref, other_ref, chunk_ref, basis_ref):
    owners = got_ref.shape[0] // 2
    port = got_ref[:owners]
    star = got_ref[owners:]
    squares = per_rhs(jnp.sum(port * port + star * star, axis=0))
    scale = 1.0 / jnp.sqrt(squares * (1.0 / total) + EPSILON)
    basis_ref[:owners] = (port + star) * scale
    basis_ref[owners:] = (port - star) * scale
    spread(chunk_ref, *image(basis_ref, pick_ref, own_ref, other_ref))


def orthogonalized(total, got, basis_refs):
    inner = 0.5 / total
    coeffs = [dot(got, ref[...]) * inner for ref in basis_refs]
    rest = got
    for coeff, ref in zip(coeffs, basis_refs):
        rest = rest - coeff * ref[...]
    norm = jnp.sqrt(dot(rest, rest) * inner + EPSILON)
    return coeffs + [norm], rest * (1.0 / norm)


def middle_kernel(total, got_ref, basis_ref, pick_ref, own_ref, other_ref, chunk_ref, next_ref,
                  coeff_ref):
    coeffs, next_ref[...] = orthogonalized(total, got_ref[...], [basis_ref])
    coeff_ref[...] = columns(dict(enumerate(coeffs)))
    spread(chunk_ref, *image(next_ref, pick_ref, own_ref, other_ref))


def last_kernel(total, got_ref, zero_ref, one_ref, coeff_ref, pick_ref, own_ref, other_ref,
                chunk_ref, mine_ref, theirs_ref, two_ref):
    side, owner, core = position()
    owners = got_ref.shape[0] // 2
    coeffs, two_ref[...] = orthogonalized(total, got_ref[...], [zero_ref, one_ref])
    refs = [zero_ref, one_ref, two_ref]
    tiles = image(two_ref, pick_ref, own_ref, other_ref)
    base = side * owners + owner - core
    basis = [[ref[base], ref[base + 1]] for ref in refs]
    products = [(tiles, part) for part in basis] + [(tiles, tiles)]
    products += [(basis[i], basis[j]) for i, j in PAIRS]
    rhs = iota((ROWS, BLOCK), 0)
    lane = iota((ROWS, BLOCK), 1)
    spots = jnp.zeros((ROWS, BLOCK), jnp.float32)
    for index, (left, right) in enumerate(products):
        value = per_rhs(left[0] * right[0] + left[1] * right[1])
        here = (lane == HALF_RHS * index + rhs) & (rhs < HALF_RHS)
        spots = jnp.where(here, value, spots)
    row = jnp.sum(spots, axis=0, keepdims=True)
    chunk_ref[...] = jnp.broadcast_to(row, chunk_ref.shape)
    known = columns(
        {place + ITERS + 1: value for place, value in enumerate(coeffs)}
    ) + coeff_ref[...]
    for out_ref, which in ((mine_ref, core), (theirs_ref, 1 - core)):
        for index, ref in enumerate(refs):
            for half in range(2):
                out_ref[2 * index + half] = ref[half * owners + owner - core + which]
        out_ref[2 * ITERS] = jnp.where(which == 0, tiles[0], tiles[1])
        out_ref[2 * ITERS + 1] = known


def keep_kernel(mine_ref, theirs_ref, across_ref, flipped_ref, mirror_hbm, kept_ref, known_ref,
                mirror_ref, sem):
    copy = pltpu.make_async_copy(mirror_hbm, mirror_ref, sem)
    copy.start()
    side, _, core = position()

    def both(index):
        mine, theirs = mine_ref[index], theirs_ref[index]
        return [jnp.where(core == 0, mine, theirs), jnp.where(core == 0, theirs, mine)]

    pairs = [(both(2 * index), both(2 * index + 1)) for index in range(ITERS)]
    here = both(2 * ITERS)
    there = [
        jnp.where(core == 0, across_ref[...], flipped_ref[...]),
        jnp.where(core == 0, flipped_ref[...], across_ref[...]),
    ]
    pairs.append(
        (
            [jnp.where(side == 0, h, t) for h, t in zip(here, there)],
            [jnp.where(side == 0, t, h) for h, t in zip(here, there)],
        )
    )
    known = both(2 * ITERS + 1)
    known_ref[...] = jnp.concatenate([tile[:HALF_RHS] for tile in known], axis=0)
    copy.wait()
    for block in range(BLK_DEV):
        rows = slice(block * HALF_RHS, (block + 1) * HALF_RHS)
        ports, stars = [], []
        for sym, anti in pairs:
            sym = jnp.concatenate([tile[rows] for tile in sym], axis=0)
            anti = jnp.concatenate([tile[rows] for tile in anti], axis=0)
            ports.append(0.5 * (sym + anti))
            stars.append(0.5 * (sym - anti))
        back = exact_dot(
            jnp.concatenate(stars, axis=0), mirror_onehot(mirror_ref, block), ((1,), (1,))
        )
        for index, port in enumerate(ports):
            kept_ref[index, :, block * BLOCK : (block + 1) * BLOCK] = jnp.where(
                side == 0, port, back[index * ROWS : (index + 1) * ROWS]
            )


def final_kernel(total, got_ref, kept_ref, known_ref, basis_ref, hessenberg_ref):
    inner = 0.5 / total
    sums = jnp.sum(got_ref[...].reshape(-1, ROWS, BLOCK), axis=0)
    even = iota((ROWS, BLOCK), 0) % 2 == 0
    lower = jnp.sum(jnp.where(even, sums, 0.0), axis=0, keepdims=True)
    upper = jnp.sum(jnp.where(even, 0.0, sums), axis=0, keepdims=True)
    rhs = iota((ROWS, BLOCK), 0)
    lane = iota((ROWS, BLOCK), 1)
    spots = jnp.where(rhs < HALF_RHS, lower, upper) * inner
    values = [
        jnp.sum(
            jnp.where(lane == HALF_RHS * index + rhs % HALF_RHS, spots, 0.0), axis=1, keepdims=True
        )
        for index in range(ITERS + 1 + len(PAIRS))
    ]
    coeffs = values[:ITERS]
    gram = {}
    for (i, j), value in zip(PAIRS, values[ITERS + 1 :]):
        gram[i, j] = gram[j, i] = value
    squares = values[ITERS]
    for i in range(ITERS):
        weight = -2.0 * coeffs[i]
        for j in range(ITERS):
            weight = weight + coeffs[j] * gram[i, j]
        squares = squares + coeffs[i] * weight
    norm = jnp.sqrt(jnp.maximum(squares, 0.0) + EPSILON)
    rest = kept_ref[ITERS]
    for j in range(ITERS):
        rest = rest - coeffs[j] * kept_ref[j]
    basis_ref[:ITERS] = kept_ref[:ITERS]
    basis_ref[ITERS] = rest * (1.0 / norm)
    place = 2 * (ITERS + 1)
    whole = known_ref[...] + columns(
        {place + index: value for index, value in enumerate(coeffs + [norm])}
    )
    turned = whole.T
    for k in range(ITERS):
        hessenberg_ref[k] = turned[k * (ITERS + 1) : (k + 1) * (ITERS + 1), :]


VMEM = pl.BlockSpec(memory_space=pltpu.VMEM)
SMEM = pl.BlockSpec(memory_space=pltpu.SMEM)
HBM = pl.BlockSpec(memory_space=pl.ANY)


def shaped(*shape, dtype=jnp.float32):
    return jax.ShapeDtypeStruct(shape, dtype)


def call(kernel, outs, specs, scratch=(), name=None):
    return pl.pallas_call(
        kernel,
        out_shape=outs,
        in_specs=specs,
        out_specs=[VMEM] * len(outs),
        scratch_shapes=scratch,
        compiler_params=pltpu.CompilerParams(vmem_limit_bytes=VMEM_LIMIT),
        name=name,
    )


def on_device(sources, near_blocks, block_rows, block_cols, mirror):
    devices = lax.axis_size(AXES)
    owners = devices // 2
    chips = devices // 2
    panels = sources.shape[2]
    total = 1.0 * panels * devices
    same_core = [[i for i in range(devices) if i % 2 == core] for core in range(2)]
    mirror_rows = mirror.reshape(BLK_DEV, BLOCK)
    blocks = near_blocks[0]
    vector = shaped(devices, ROWS, BLOCK)
    chunk = shaped(chips, 2, ROWS, BLOCK)
    tile = shaped(ROWS, BLOCK)

    def swapped(value, bits):
        return lax.ppermute(value, AXES, [(i, i ^ bits) for i in range(devices)])

    def exchanged(chunks):
        got = lax.all_to_all(chunks, AXES, 0, 0, axis_index_groups=same_core)
        return got.reshape(vector.shape)

    places = jnp.concatenate([block_rows, block_cols], axis=0)
    other_blocks = swapped(blocks, 1)
    other_places = swapped(places, 1)
    [chunks] = call(
        start_kernel, [vector], [HBM, HBM],
        [
            pltpu.VMEM(sources.shape[1:], jnp.float32),
            pltpu.VMEM(mirror_rows.shape, jnp.int32),
            pltpu.SemaphoreType.DMA((2,)),
        ],
        name="start",
    )(sources[0], mirror_rows)
    got = lax.all_to_all(chunks, AXES, 0, 0)
    own_blocks, pick = call(
        prepare_kernel,
        [
            shaped(*blocks.shape, dtype=blocks.dtype),
            shaped(2 * ROWS * blocks.shape[0], owners * ROWS, dtype=jnp.bfloat16),
        ],
        [HBM, SMEM, SMEM], [pltpu.SemaphoreType.DMA], name="prepare",
    )(blocks, places, other_places)
    near = (pick, own_blocks, other_blocks)
    chunks, zero = call(
        functools.partial(first_kernel, total), [chunk, vector], [VMEM] * 4, name="first"
    )(got, *near)
    got = exchanged(chunks)
    chunks, one, coeff = call(
        functools.partial(middle_kernel, total), [chunk, vector, tile], [VMEM] * 5, name="middle"
    )(got, zero, *near)
    got = exchanged(chunks)
    kept = shaped(2 * ITERS + 2, ROWS, BLOCK)
    chunks, mine, theirs = call(
        functools.partial(last_kernel, total), [shaped(devices, BLOCK), kept, kept], [VMEM] * 7,
        [pltpu.VMEM(vector.shape, jnp.float32)], name="last",
    )(got, zero, one, coeff, *near)
    got = lax.all_to_all(chunks.reshape(devices, 1, BLOCK), AXES, 0, 0)
    partner = swapped(theirs, 1)
    across = swapped(mine[2 * ITERS], devices // 2)
    flipped = swapped(theirs[2 * ITERS], devices // 2 ^ 1)
    kept, known = call(
        keep_kernel, [shaped(ITERS + 1, ROWS, panels), tile], [VMEM] * 4 + [HBM],
        [pltpu.VMEM(mirror_rows.shape, jnp.int32), pltpu.SemaphoreType.DMA], name="keep",
    )(mine, partner, across, flipped, mirror_rows)
    basis, hessenberg = call(
        functools.partial(final_kernel, total),
        [shaped(ITERS + 1, ROWS, panels), shaped(ITERS, ITERS + 1, ROWS)], [VMEM] * 3,
        name="final",
    )(got.reshape(devices, BLOCK), kept, known)
    return basis[:, None], hessenberg.transpose(2, 1, 0)


def solution(mesh):
    placed = (
        P("side", None, ("grp", "dev")),
        P("side", ("grp", "dev"), None, None),
        P("side", ("grp", "dev")),
        P("side", ("grp", "dev")),
        P(("grp", "dev")),
    )
    return jax.shard_map(
        on_device,
        mesh=mesh,
        in_specs=placed,
        out_specs=(P(None, "side", None, ("grp", "dev")), P()),
        check_vma=False,
    )
```

time: 404 us -> 54.8 us (0.14)
  blocking collectives: 288 us -> 21.4 us
  starting transfers between devices: 63.3 us -> 12.3 us
  waiting for transfers between devices: 32 us -> 10.6 us
  Pallas kernels: 0 us -> 6.82 us
  local copies, waits for them, and re-layouts: 7.85 us -> 2.62 us
  other arithmetic: 5.01 us -> 0.01 us
  matrix products: 4.45 us -> 0 us
    psum x7 -> x0, blocking collectives: 288 us -> none  [the longest x3 125 us: on_device(): dot_sums = lax.psum(products_local, ('side', 'grp', 'dev'))]
    ppermute x30 -> x5, starting transfers between devices: 63.3 us -> 2.78 us  [swapped(): return lax.ppermute(value, AXES, [(i, i ^ bits) for i in range(devices)])]
    ppermute x30 -> x5, waiting for transfers between devices: 32 us -> 4.05 us  [swapped(): return lax.ppermute(value, AXES, [(i, i ^ bits) for i in range(devices)])]
    all_to_all x0 -> x2, blocking collectives: none -> 21.4 us  [exchanged(): got = lax.all_to_all(chunks, AXES, 0, 0, axis_index_groups=same_core)]
    all_to_all x0 -> x2, starting transfers between devices: none -> 9.51 us  [the longest x1 6.97 us: on_device(): got = lax.all_to_all(chunks, AXES, 0, 0)]
    pallas_call x0 -> x7, Pallas kernels: none -> 6.82 us  [the longest x1 1.94 us: on_device(): call(functools.partial(last_kernel, total), [shaped(devices, BLOCK), kept...]
    all_to_all x0 -> x2, waiting for transfers between devices: none -> 6.59 us  [the longest x1 4.99 us: on_device(): got = lax.all_to_all(chunks, AXES, 0, 0)]
    dot_general x14 -> x0, matrix products: 4.45 us -> none  [the longest x3 1.9 us: on_device(): jnp.einsum('rkj,kij->rki', picked, blocks, preferred_element_type=jnp.flo...]
  transfers between devices with their start and end apart: 30 -> 7, of which waited for: 15 -> 5; matrix products, arithmetic and copies ran while one was open for 1% -> 0% of each run, Pallas kernels for 0% -> 4%
where the time goes in v2:
time: 54.8 us; the launch traced here: 54.5 us
  blocking collectives  21.4 us (39%)
  starting transfers between devices  12.3 us (22%)
  waiting for transfers between devices  10.6 us (19%)
  Pallas kernels  6.82 us (12%)
  local copies, waits for them, and re-layouts  2.62 us (5%)
  between operations  0.74 us (1%)
    all_to_all x2, blocking collectives, exchanged(): got = lax.all_to_all(chunks, AXES, 0, 0, axis_index_groups=same_core)  21.4 us
    all_to_all x1, starting transfers between devices, on_device(): got = lax.all_to_all(chunks, AXES, 0, 0)  6.97 us
    all_to_all x1, waiting for transfers between devices, on_device(): got = lax.all_to_all(chunks, AXES, 0, 0)  4.99 us
    ppermute x5, waiting for transfers between devices, swapped(): return lax.ppermute(value, AXES, [(i, i ^ bits) for i in range(devices)])  4.05 us
    ppermute x5, starting transfers between devices, swapped(): return lax.ppermute(value, AXES, [(i, i ^ bits) for i in range(devices)])  2.78 us
    unnamed x10, local copies, waits for them, and re-layouts  2.61 us
    all_to_all x1, starting transfers between devices, on_device(): got = lax.all_to_all(chunks.reshape(devices, 1, BLOCK), AXES, 0, 0)  2.54 us
    pallas_call x1, Pallas kernels, on_device(): call(functools.partial(last_kernel, total), [shaped(devices, BLOCK), kept...  1.94 us
  transfers between devices with their start and end apart: 7, of which 5 were waited for; matrix products, arithmetic and copies ran while one was open for 0% of the time, Pallas kernels for 4%

profile of v2, /device:TPU:0, one launch (start us, length us, event | category | flops | bytes accessed | tf_op | source)
XLA Modules:
  0.0 54.5 jit_solution(15521641107772960714)
XLA Ops:
  0.6 0.5 collective-permute-start.1
  1.1 0.0 copy-start.2
  1.1 0.7 %copy-done.2 = s32[256]{0:T(256)S(1)} copy-done((s32[256]{0:T(256)S(1)}, s32[256]{0:T(256)}, u32[]{:S(2)}) %copy-start.2) | copy-done | bytes 1048
  1.8 0.0 copy-start.1
  1.8 0.7 %copy-done.1 = f32[1,8,256]{2,1,0:T(8,128)S(1)} copy-done((f32[1,8,256]{2,1,0:T(8,128)S(1)}, f32[1,8,256]{2,1,0:T(8,128)}, u32[]{:S(2)}) %copy-start.1) | copy-done | bytes 8216
  2.5 0.9 %start.1 = f32[32,8,128]{2,1,0:T(8,128)} custom-call(f32[8,256]{1,0:T(8,128)S(1)} %bitcast.22, s32[2,128]{1,0:T(2,128)S(1)} %bitcast.23), custom_call_target="tpu_custom_call" | custom-call | tf_op jit(solution)/shard_map/start/pallas_call | solution.py:334
  3.4 0.0 copy-start.3
  3.5 0.0 copy-start.4
  3.5 7.0 %all-to-all-start = ((f32[32,8,128]{2,1,0:T(8,128)}), f32[32,8,128]{2,1,0:T(8,128)S(1)}, u32[]{:S(2)}, u32[]{:S(2)}) async-start(f32[32,8,128]{2,1,0:T(8,128)} %start.1), calls=%async_computation | async-start | bytes 262144 | tf_op jit(solution)/shard_map/all_to_all | solution.py:343
  10.4 0.0 copy-done.3
  10.5 0.0 copy-done.4
  10.5 0.3 collective-permute-start
  10.8 0.9 %collective-permute-done.other_places = s32[2,32]{1,0:T(2,128)S(1)} collective-permute-done((s32[2,32]{1,0:T(2,128)S(1)}, s32[2,32]{1,0:T(2,128)S(1)}, u32[]{:S(2)}, u32[]{:S(2)}) %collective-permute-start) | collective-permute-done | bytes 288 | tf_op jit(solution)/shard_map/ppermute | solution.py:325
  11.7 0.0 copy-start
  11.7 1.2 %copy-done = bf16[1,32,128,128]{3,2,1,0:T(8,128)(2,1)S(1)} copy-done((bf16[1,32,128,128]{3,2,1,0:T(8,128)(2,1)S(1)}, bf16[1,32,128,128]{3,2,1,0:T(8,128)(2,1)}, u32[]{:S(2)}) %copy-start) | copy-done | bytes 1048600
  12.9 0.7 %prepare.1 = (bf16[32,128,128]{2,1,0:T(8,128)(2,1)S(1)}, bf16[512,128]{1,0:T(8,128)(2,1)S(1)}) custom-call(bf16[32,128,128]{2,1,0:T(8,128)(2,1)S(1)} %bitcast.18, s32[2,32]{1,0:T(2,128)S(1)} %pad_add_fusion.own_places, s32[2,32]{1,0:T(2,128)S(1)} %collective-permute-done.other_places), custom_call_target="tpu_custom_call" | custom-call | tf_op jit(solution)/shard_map/prepare/pallas_call | solution.py:344
  13.6 5.0 %all-to-all-done.got_ref = f32[32,8,128]{2,1,0:T(8,128)S(1)} async-done(((f32[32,8,128]{2,1,0:T(8,128)}), f32[32,8,128]{2,1,0:T(8,128)S(1)}, u32[]{:S(2)}, u32[]{:S(2)}) %all-to-all-start) | async-done | bytes 131104 | tf_op jit(solution)/shard_map/all_to_all | solution.py:343
  18.6 0.0 collective-permute-done.1.other_ref
  18.6 1.0 %first.1 = (f32[16,2,8,128]{3,2,1,0:T(8,128)S(1)}, f32[32,8,128]{2,1,0:T(8,128)S(1)}) custom-call(f32[32,8,128]{2,1,0:T(8,128)S(1)} %all-to-all-done.got_ref, bf16[512,128]{1,0:T(8,128)(2,1)S(1)} %get-tuple-element.16.pick_ref, bf16[32,128,128]{2,1,0:T(8,128)(2,1)S(1)} %get-tuple-element.17.own_ref, bf16[32,128,128]{2,1,0:T(8,128)(2,1)S(1)} %collective-permute-done.1.other_ref), custom_call_target="tpu_custom_call" | custom-call | tf_op jit(solution)/shard_map/first/pallas_call | solution.py:353
  19.6 11.0 %all_to_all.20 = f32[16,2,8,128]{3,2,1,0:T(8,128)S(1)} all-to-all(f32[16,2,8,128]{3,2,1,0:T(8,128)S(1)} %get-tuple-element.18), channel_id=1, replica_groups={{0,2,4,6,8,10,12,14,16,18,20,22,24,26,28,30},{1,3,5,7,9,11,13,15,17,19,..., dimensions={0} | all-to-all | bytes 262144 | tf_op jit(solution)/shard_map/all_to_all | solution.py:328
  30.6 1.2 %middle.1 = (f32[16,2,8,128]{3,2,1,0:T(8,128)S(1)}, f32[32,8,128]{2,1,0:T(8,128)S(1)}, f32[8,128]{1,0:T(8,128)S(1)}) custom-call(f32[32,8,128]{2,1,0:T(8,128)S(1)} %bitcast.20, f32[32,8,128]{2,1,0:T(8,128)S(1)} %get-tuple-element.19.basis_ref.zero_ref, bf16[512,128]{1,0:T(8,128)(2,1)S(1)} %get-tuple-element.16.pick_ref, ...), custom_call_target="tpu_custom_call" | custom-call | tf_op jit(solution)/shard_map/middle/pallas_call | solution.py:357
  31.8 10.4 %all_to_all.21 = f32[16,2,8,128]{3,2,1,0:T(8,128)S(1)} all-to-all(f32[16,2,8,128]{3,2,1,0:T(8,128)S(1)} %get-tuple-element.20), channel_id=1, replica_groups={{0,2,4,6,8,10,12,14,16,18,20,22,24,26,28,30},{1,3,5,7,9,11,13,15,17,19,..., dimensions={0} | all-to-all | bytes 262144 | tf_op jit(solution)/shard_map/all_to_all | solution.py:328
  42.1 1.9 %last.1 = (f32[32,128]{1,0:T(8,128)}, f32[8,8,128]{2,1,0:T(8,128)S(1)}, f32[8,8,128]{2,1,0:T(8,128)S(1)}) custom-call(f32[32,8,128]{2,1,0:T(8,128)S(1)} %bitcast.19, f32[32,8,128]{2,1,0:T(8,128)S(1)} %get-tuple-element.19.basis_ref.zero_ref, f32[32,8,128]{2,1,0:T(8,128)S(1)} %get-tuple-element.21.one_ref, f32[8,128]{1,0:T(8,128)S(1)} %get-tuple-element.22.coeff_ref, ...), custom_call_target="tpu_custom_call" | custom-call | tf_op jit(solution)/shard_map/last/pallas_call | solution.py:362
  44.1 0.0 collective-permute-start.2
  44.1 2.5 %all-to-all-start.3 = ((f32[32,1,128]{2,1,0:T(1,128)}), f32[32,1,128]{2,1,0:T(1,128)S(1)}, u32[]{:S(2)}, u32[]{:S(2)}) async-start(f32[32,1,128]{2,1,0:T(1,128)} %bitcast.6), calls=%async_computation.3 | async-start | bytes 32768 | tf_op jit(solution)/shard_map/all_to_all | solution.py:366
  46.6 1.5 %collective-permute-start.4 = (f32[8,128]{1,0:T(8,128)S(1)}, f32[8,128]{1,0:T(8,128)S(1)}, u32[]{:S(2)}, u32[]{:S(2)}) collective-permute-start(f32[8,128]{1,0:T(8,128)S(1)} %slice_bitcast_fusion), channel_id=1, source_target_pairs={{0,17},{1,16},{2,19},{3,18},{4,21},{5,20},{6,23},{7,22},{8,25},{9,... | collective-permute-start | bytes 12296 | tf_op jit(solution)/shard_map/ppermute | solution.py:325
  48.1 0.5 collective-permute-start.3
  48.6 1.2 %collective-permute-done.4.flipped_ref = f32[8,128]{1,0:T(8,128)S(1)} collective-permute-done((f32[8,128]{1,0:T(8,128)S(1)}, f32[8,128]{1,0:T(8,128)S(1)}, u32[]{:S(2)}, u32[]{:S(2)}) %collective-permute-start.4) | collective-permute-done | bytes 4128 | tf_op jit(solution)/shard_map/ppermute | solution.py:325
  49.7 2.0 %collective-permute-done.3.across_ref = f32[8,128]{1,0:T(8,128)S(1)} collective-permute-done((f32[8,128]{1,0:T(8,128)S(1)}, f32[8,128]{1,0:T(8,128)S(1)}, u32[]{:S(2)}, u32[]{:S(2)}) %collective-permute-start.3) | collective-permute-done | bytes 4128 | tf_op jit(solution)/shard_map/ppermute | solution.py:325
  51.7 0.0 collective-permute-done.2.theirs_ref
  51.7 0.3 keep.1
  52.1 1.6 %all-to-all-done.3 = f32[32,1,128]{2,1,0:T(1,128)S(1)} async-done(((f32[32,1,128]{2,1,0:T(1,128)}), f32[32,1,128]{2,1,0:T(1,128)S(1)}, u32[]{:S(2)}, u32[]{:S(2)}) %all-to-all-start.3) | async-done | bytes 16416 | tf_op jit(solution)/shard_map/all_to_all | solution.py:366
  53.7 0.8 %final.1 = (f32[4,8,256]{2,1,0:T(8,128)}, f32[3,4,8]{2,1,0:T(4,128)}) custom-call(f32[32,128]{1,0:T(8,128)S(1)} %bitcast.21, f32[4,8,256]{2,1,0:T(8,128)S(1)} %get-tuple-element.26.kept_ref, f32[8,128]{1,0:T(8,128)S(1)} %get-tuple-element.27.known_ref), custom_call_target="tpu_custom_call" | custom-call | tf_op jit(solution)/shard_map/final/pallas_call | solution.py:374
  (3 shorter events, 0.0 us)
Async XLA Ops:
  0.6 18.0 %collective-permute-start.1 = (bf16[32,128,128]{2,1,0:T(8,128)(2,1)}, bf16[32,128,128]{2,1,0:T(8,128)(2,1)S(1)}, u32[]{:S(2)}, u32[]{:S(2)}) collective-permute-start(bf16[32,128,128]{2,1,0:T(8,128)(2,1)} %bitcast.17), channel_id=1, source_target_pairs={{0,1},{1,0},{2,3},{3,2},{4,5},{5,4},{6,7},{7,6},{8,9},{9,8},{10,11... | collective-permute-start | bytes 3145736 | tf_op jit(solution)/shard_map/ppermute | solution.py:325
  1.1 0.7 %copy-start.2 = (s32[256]{0:T(256)S(1)}, s32[256]{0:T(256)}, u32[]{:S(2)}) copy-start(s32[256]{0:T(256)} %param.9) | copy-start | bytes 3076
  1.8 0.7 %copy-start.1 = (f32[1,8,256]{2,1,0:T(8,128)S(1)}, f32[1,8,256]{2,1,0:T(8,128)}, u32[]{:S(2)}) copy-start(f32[1,8,256]{2,1,0:T(8,128)} %param.5) | copy-start | bytes 24580
  3.4 7.0 %copy-start.3 = (s32[1,32]{1,0:T(1,128)S(1)}, s32[1,32]{1,0:T(1,128)}, u32[]{:S(2)}) copy-start(s32[1,32]{1,0:T(1,128)} %param.8) | copy-start | bytes 388
  3.5 7.0 %copy-start.4 = (s32[1,32]{1,0:T(1,128)S(1)}, s32[1,32]{1,0:T(1,128)}, u32[]{:S(2)}) copy-start(s32[1,32]{1,0:T(1,128)} %param.7) | copy-start | bytes 388
  3.5 15.1 %all-to-all-start = ((f32[32,8,128]{2,1,0:T(8,128)}), f32[32,8,128]{2,1,0:T(8,128)S(1)}, u32[]{:S(2)}, u32[]{:S(2)}) async-start(f32[32,8,128]{2,1,0:T(8,128)} %start.1), calls=%async_computation | async-start | bytes 262144 | tf_op jit(solution)/shard_map/all_to_all | solution.py:343
  10.5 1.2 %collective-permute-start = (s32[2,32]{1,0:T(2,128)S(1)}, s32[2,32]{1,0:T(2,128)S(1)}, u32[]{:S(2)}, u32[]{:S(2)}) collective-permute-start(s32[2,32]{1,0:T(2,128)S(1)} %pad_add_fusion.own_places), channel_id=1, source_target_pairs={{0,1},{1,0},{2,3},{3,2},{4,5},{5,4},{6,7},{7,6},{8,9},{9,8},{10,11... | collective-permute-start | bytes 776 | tf_op jit(solution)/shard_map/ppermute | solution.py:325
  11.7 1.2 %copy-start = (bf16[1,32,128,128]{3,2,1,0:T(8,128)(2,1)S(1)}, bf16[1,32,128,128]{3,2,1,0:T(8,128)(2,1)}, u32[]{:S(2)}) copy-start(bf16[1,32,128,128]{3,2,1,0:T(8,128)(2,1)} %param.6) | copy-start | bytes 3145732
  44.1 7.7 %collective-permute-start.2 = (f32[8,8,128]{2,1,0:T(8,128)S(1)}, f32[8,8,128]{2,1,0:T(8,128)S(1)}, u32[]{:S(2)}, u32[]{:S(2)}) collective-permute-start(f32[8,8,128]{2,1,0:T(8,128)S(1)} %get-tuple-element.25), channel_id=1, source_target_pairs={{0,1},{1,0},{2,3},{3,2},{4,5},{5,4},{6,7},{7,6},{8,9},{9,8},{10,11... | collective-permute-start | bytes 98312 | tf_op jit(solution)/shard_map/ppermute | solution.py:325
  44.1 9.6 %all-to-all-start.3 = ((f32[32,1,128]{2,1,0:T(1,128)}), f32[32,1,128]{2,1,0:T(1,128)S(1)}, u32[]{:S(2)}, u32[]{:S(2)}) async-start(f32[32,1,128]{2,1,0:T(1,128)} %bitcast.6), calls=%async_computation.3 | async-start | bytes 32768 | tf_op jit(solution)/shard_map/all_to_all | solution.py:366
  46.6 3.1 %collective-permute-start.4 = (f32[8,128]{1,0:T(8,128)S(1)}, f32[8,128]{1,0:T(8,128)S(1)}, u32[]{:S(2)}, u32[]{:S(2)}) collective-permute-start(f32[8,128]{1,0:T(8,128)S(1)} %slice_bitcast_fusion), channel_id=1, source_target_pairs={{0,17},{1,16},{2,19},{3,18},{4,21},{5,20},{6,23},{7,22},{8,25},{9,... | collective-permute-start | bytes 12296 | tf_op jit(solution)/shard_map/ppermute | solution.py:325
  48.1 3.6 %collective-permute-start.3 = (f32[8,128]{1,0:T(8,128)S(1)}, f32[8,128]{1,0:T(8,128)S(1)}, u32[]{:S(2)}, u32[]{:S(2)}) collective-permute-start(f32[8,128]{1,0:T(8,128)S(1)} %slice_bitcast_fusion.1), channel_id=1, source_target_pairs={{0,16},{1,17},{2,18},{3,19},{4,20},{5,21},{6,22},{7,23},{8,24},{9,... | collective-permute-start | bytes 12296 | tf_op jit(solution)/shard_map/ppermute | solution.py:325

commit v3 on v2

--- a/solution.py
+++ b/solution.py
@@ -15,7 +15,7 @@
 EPSILON = 1e-06
 AXES = ("side", "grp", "dev")
 VMEM_LIMIT = 48 * 2**20
-PAIRS = [(i, j) for i in range(ITERS) for j in range(i, ITERS)]
+LENGTH_LANE = ITERS * (ITERS + 1)
 
 
 def position():
@@ -86,7 +86,8 @@
     lax.fori_loop(0, chips, store, 0, unroll=chips <= 32)
 
 
-def prepare_kernel(blocks_hbm, own_places, other_places, blocks_ref, pick_ref, sem):
+def prepare_kernel(blocks_hbm, own_rows, own_cols, other_rows, other_cols, blocks_ref, pick_ref,
+                   sem):
     copy = pltpu.make_async_copy(blocks_hbm, blocks_ref, sem)
     copy.start()
     width = pick_ref.shape[1]
@@ -95,9 +96,9 @@
     lane = iota((ROWS, width), 1)
     for entry in range(blocks_ref.shape[0]):
         picks = []
-        for places in (own_places, other_places):
+        for rows, cols in ((own_rows, own_cols), (other_rows, other_cols)):
             place = jnp.where(
-                half_of_row == places[0, entry], HALF_RHS * places[1, entry] + rhs_of_row, -1
+                half_of_row == rows[0, entry], HALF_RHS * cols[0, entry] + rhs_of_row, -1
             )
             picks.append((lane == place).astype(jnp.float32))
         first = 2 * ROWS * entry
@@ -146,19 +147,24 @@
     lax.fori_loop(0, chips, store, 0, unroll=chips <= 32)
 
 
-def first_kernel(total, got_ref, pick_ref, own_ref, other_ref, chunk_ref, basis_ref):
+def first_kernel(total, got_ref, pick_ref, own_ref, other_ref, chunk_ref, basis_ref, coeff_ref):
     owners = got_ref.shape[0] // 2
     port = got_ref[:owners]
     star = got_ref[owners:]
     squares = per_rhs(jnp.sum(port * port + star * star, axis=0))
-    scale = 1.0 / jnp.sqrt(squares * (1.0 / total) + EPSILON)
+    length = jnp.sqrt(squares * (1.0 / total) + EPSILON)
+    scale = 1.0 / length
+    coeff_ref[...] = columns({LENGTH_LANE: length})
     basis_ref[:owners] = (port + star) * scale
     basis_ref[owners:] = (port - star) * scale
     spread(chunk_ref, *image(basis_ref, pick_ref, own_ref, other_ref))
 
 
-def orthogonalized(total, got, basis_refs):
+def orthogonalized(total, shift, got_ref, basis_refs):
     inner = 0.5 / total
+    chips = got_ref.shape[0]
+    got = jnp.concatenate([got_ref[chips - shift :], got_ref[: chips - shift]], axis=0)
+    got = got.reshape(basis_refs[0].shape)
     coeffs = [dot(got, ref[...]) * inner for ref in basis_refs]
     rest = got
     for coeff, ref in zip(coeffs, basis_refs):
@@ -167,68 +173,84 @@
     return coeffs + [norm], rest * (1.0 / norm)
 
 
-def middle_kernel(total, got_ref, basis_ref, pick_ref, own_ref, other_ref, chunk_ref, next_ref,
-                  coeff_ref):
-    coeffs, next_ref[...] = orthogonalized(total, got_ref[...], [basis_ref])
-    coeff_ref[...] = columns(dict(enumerate(coeffs)))
+def middle_kernel(total, shift, got_ref, basis_ref, known_ref, pick_ref, own_ref, other_ref,
+                  chunk_ref, next_ref, coeff_ref):
+    coeffs, next_ref[...] = orthogonalized(total, shift, got_ref, [basis_ref])
+    coeff_ref[...] = columns(dict(enumerate(coeffs))) + known_ref[...]
     spread(chunk_ref, *image(next_ref, pick_ref, own_ref, other_ref))
 
 
-def last_kernel(total, got_ref, zero_ref, one_ref, coeff_ref, pick_ref, own_ref, other_ref,
-                chunk_ref, mine_ref, theirs_ref, two_ref):
+def last_kernel(total, shift, got_ref, zero_ref, one_ref, known_ref, pick_ref, own_ref, other_ref,
+                chunk_ref, two_ref, coeff_ref, same_ref, flip_ref, theirs_ref):
     side, owner, core = position()
-    owners = got_ref.shape[0] // 2
-    coeffs, two_ref[...] = orthogonalized(total, got_ref[...], [zero_ref, one_ref])
+    owners = two_ref.shape[0] // 2
     refs = [zero_ref, one_ref, two_ref]
+    coeffs, two_ref[...] = orthogonalized(total, shift, got_ref, refs[:2])
     tiles = image(two_ref, pick_ref, own_ref, other_ref)
     base = side * owners + owner - core
-    basis = [[ref[base], ref[base + 1]] for ref in refs]
-    products = [(tiles, part) for part in basis] + [(tiles, tiles)]
-    products += [(basis[i], basis[j]) for i, j in PAIRS]
     rhs = iota((ROWS, BLOCK), 0)
     lane = iota((ROWS, BLOCK), 1)
     spots = jnp.zeros((ROWS, BLOCK), jnp.float32)
-    for index, (left, right) in enumerate(products):
-        value = per_rhs(left[0] * right[0] + left[1] * right[1])
+    for index in range(ITERS + 1):
+        if index < ITERS:
+            product = tiles[0] * refs[index][base] + tiles[1] * refs[index][base + 1]
+        else:
+            product = tiles[0] * tiles[0] + tiles[1] * tiles[1]
         here = (lane == HALF_RHS * index + rhs) & (rhs < HALF_RHS)
-        spots = jnp.where(here, value, spots)
+        spots = jnp.where(here, per_rhs(product), spots)
     row = jnp.sum(spots, axis=0, keepdims=True)
     chunk_ref[...] = jnp.broadcast_to(row, chunk_ref.shape)
-    known = columns(
-        {place + ITERS + 1: value for place, value in enumerate(coeffs)}
-    ) + coeff_ref[...]
-    for out_ref, which in ((mine_ref, core), (theirs_ref, 1 - core)):
-        for index, ref in enumerate(refs):
-            for half in range(2):
-                out_ref[2 * index + half] = ref[half * owners + owner - core + which]
-        out_ref[2 * ITERS] = jnp.where(which == 0, tiles[0], tiles[1])
-        out_ref[2 * ITERS + 1] = known
-
-
-def keep_kernel(mine_ref, theirs_ref, across_ref, flipped_ref, mirror_hbm, kept_ref, known_ref,
-                mirror_ref, sem):
+    coeffs = columns({place + ITERS + 1: value for place, value in enumerate(coeffs)})
+    coeff_ref[...] = coeffs + known_ref[...]
+    same_ref[...] = jnp.where(core == 0, tiles[0], tiles[1])
+    flip_ref[...] = jnp.where(core == 0, tiles[1], tiles[0])
+    for index, ref in enumerate(refs):
+        for half in range(2):
+            theirs_ref[2 * index + half] = ref[half * owners + owner + 1 - 2 * core]
+    theirs_ref[2 * ITERS] = flip_ref[...]
+    theirs_ref[2 * ITERS + 1] = coeff_ref[...]
+
+
+def keep_kernel(zero_ref, one_ref, two_ref, coeff_ref, same_ref, theirs_ref, across_ref,
+                flipped_ref, mirror_hbm, kept_ref, known_ref, gram_ref, mirror_ref, sem):
     copy = pltpu.make_async_copy(mirror_hbm, mirror_ref, sem)
     copy.start()
-    side, _, core = position()
-
-    def both(index):
-        mine, theirs = mine_ref[index], theirs_ref[index]
+    side, owner, core = position()
+    owners = zero_ref.shape[0] // 2
+
+    def by_core(mine, theirs):
         return [jnp.where(core == 0, mine, theirs), jnp.where(core == 0, theirs, mine)]
 
-    pairs = [(both(2 * index), both(2 * index + 1)) for index in range(ITERS)]
-    here = both(2 * ITERS)
-    there = [
-        jnp.where(core == 0, across_ref[...], flipped_ref[...]),
-        jnp.where(core == 0, flipped_ref[...], across_ref[...]),
-    ]
+    pairs = []
+    for index, ref in enumerate((zero_ref, one_ref, two_ref)):
+        pairs.append(
+            [
+                by_core(ref[half * owners + owner], theirs_ref[2 * index + half])
+                for half in range(2)
+            ]
+        )
+    here = by_core(same_ref[...], theirs_ref[2 * ITERS])
+    there = by_core(across_ref[...], flipped_ref[...])
     pairs.append(
-        (
+        [
             [jnp.where(side == 0, h, t) for h, t in zip(here, there)],
             [jnp.where(side == 0, t, h) for h, t in zip(here, there)],
-        )
-    )
-    known = both(2 * ITERS + 1)
-    known_ref[...] = jnp.concatenate([tile[:HALF_RHS] for tile in known], axis=0)
+        ]
+    )
+    known = by_core(coeff_ref[...], theirs_ref[2 * ITERS + 1])
+    known = jnp.concatenate([tile[:HALF_RHS] for tile in known], axis=0)
+    known_ref[...] = jnp.where(iota((ROWS, BLOCK), 1) < LENGTH_LANE, known, 0.0)
+
+    def entry(j, k):
+        place = k * (ITERS + 1) + j
+        return known[:, place : place + 1]
+
+    norms = [known[:, LENGTH_LANE : LENGTH_LANE + 1], entry(1, 0), entry(2, 1)]
+    short = [EPSILON / (norm * norm) for norm in norms]
+    zero_one = entry(0, 0) * short[0] / norms[1]
+    zero_two = (entry(0, 1) * short[0] - entry(1, 1) * zero_one) / norms[2]
+    one_two = (entry(1, 1) * short[1] - entry(0, 1) * zero_one) / norms[2]
+    gram_ref[...] = columns(dict(enumerate(short + [zero_one, zero_two, one_two])))
     copy.wait()
     for block in range(BLK_DEV):
         rows = slice(block * HALF_RHS, (block + 1) * HALF_RHS)
@@ -247,7 +269,7 @@
             )
 
 
-def final_kernel(total, got_ref, kept_ref, known_ref, basis_ref, hessenberg_ref):
+def final_kernel(total, got_ref, kept_ref, known_ref, gram_ref, basis_ref, hessenberg_ref):
     inner = 0.5 / total
     sums = jnp.sum(got_ref[...].reshape(-1, ROWS, BLOCK), axis=0)
     even = iota((ROWS, BLOCK), 0) % 2 == 0
@@ -260,18 +282,15 @@
         jnp.sum(
             jnp.where(lane == HALF_RHS * index + rhs % HALF_RHS, spots, 0.0), axis=1, keepdims=True
         )
-        for index in range(ITERS + 1 + len(PAIRS))
+        for index in range(ITERS + 1)
     ]
     coeffs = values[:ITERS]
-    gram = {}
-    for (i, j), value in zip(PAIRS, values[ITERS + 1 :]):
-        gram[i, j] = gram[j, i] = value
+    gram = gram_ref[...]
     squares = values[ITERS]
-    for i in range(ITERS):
-        weight = -2.0 * coeffs[i]
-        for j in range(ITERS):
-            weight = weight + coeffs[j] * gram[i, j]
-        squares = squares + coeffs[i] * weight
+    for j in range(ITERS):
+        squares = squares - coeffs[j] * coeffs[j] * (1.0 + gram[:, j : j + 1])
+    for place, (i, j) in enumerate(((0, 1), (0, 2), (1, 2))):
+        squares = squares + 2.0 * coeffs[i] * coeffs[j] * gram[:, ITERS + place : ITERS + place + 1]
     norm = jnp.sqrt(jnp.maximum(squares, 0.0) + EPSILON)
     rest = kept_ref[ITERS]
     for j in range(ITERS):
@@ -289,7 +308,7 @@
 
 VMEM = pl.BlockSpec(memory_space=pltpu.VMEM)
 SMEM = pl.BlockSpec(memory_space=pltpu.SMEM)
-HBM = pl.BlockSpec(memory_space=pl.ANY)
+HBM = pl.BlockSpec(memory_space=pltpu.HBM)
 
 
 def shaped(*shape, dtype=jnp.float32):
@@ -314,7 +333,11 @@
     chips = devices // 2
     panels = sources.shape[2]
     total = 1.0 * panels * devices
-    same_core = [[i for i in range(devices) if i % 2 == core] for core in range(2)]
+    dev = lax.axis_size("dev")
+    shift = (dev + dev // 2) // 2 % chips
+    same_core = [
+        [(2 * (chip + shift) + core) % devices for chip in range(chips)] for core in range(2)
+    ]
     mirror_rows = mirror.reshape(BLK_DEV, BLOCK)
     blocks = near_blocks[0]
     vector = shaped(devices, ROWS, BLOCK)
@@ -325,12 +348,8 @@
         return lax.ppermute(value, AXES, [(i, i ^ bits) for i in range(devices)])
 
     def exchanged(chunks):
-        got = lax.all_to_all(chunks, AXES, 0, 0, axis_index_groups=same_core)
-        return got.reshape(vector.shape)
-
-    places = jnp.concatenate([block_rows, block_cols], axis=0)
-    other_blocks = swapped(blocks, 1)
-    other_places = swapped(places, 1)
+        return lax.all_to_all(chunks, AXES, 0, 0, axis_index_groups=same_core)
+
     [chunks] = call(
         start_kernel, [vector], [HBM, HBM],
         [
@@ -340,42 +359,47 @@
         ],
         name="start",
     )(sources[0], mirror_rows)
+    chunks, blocks, block_rows, block_cols = lax.optimization_barrier(
+        (chunks, blocks, block_rows, block_cols)
+    )
     got = lax.all_to_all(chunks, AXES, 0, 0)
+    other_blocks = swapped(blocks, 1)
     own_blocks, pick = call(
         prepare_kernel,
         [
             shaped(*blocks.shape, dtype=blocks.dtype),
             shaped(2 * ROWS * blocks.shape[0], owners * ROWS, dtype=jnp.bfloat16),
         ],
-        [HBM, SMEM, SMEM], [pltpu.SemaphoreType.DMA], name="prepare",
-    )(blocks, places, other_places)
+        [HBM] + [SMEM] * 4, [pltpu.SemaphoreType.DMA], name="prepare",
+    )(blocks, block_rows, block_cols, swapped(block_rows, 1), swapped(block_cols, 1))
     near = (pick, own_blocks, other_blocks)
-    chunks, zero = call(
-        functools.partial(first_kernel, total), [chunk, vector], [VMEM] * 4, name="first"
+    chunks, zero, coeff = call(
+        functools.partial(first_kernel, total), [chunk, vector, tile], [VMEM] * 4, name="first"
     )(got, *near)
     got = exchanged(chunks)
     chunks, one, coeff = call(
-        functools.partial(middle_kernel, total), [chunk, vector, tile], [VMEM] * 5, name="middle"
-    )(got, zero, *near)
+        functools.partial(middle_kernel, total, shift), [chunk, vector, tile], [VMEM] * 6,
+        name="middle",
+    )(got, zero, coeff, *near)
     got = exchanged(chunks)
-    kept = shaped(2 * ITERS + 2, ROWS, BLOCK)
-    chunks, mine, theirs = call(
-        functools.partial(last_kernel, total), [shaped(devices, BLOCK), kept, kept], [VMEM] * 7,
-        [pltpu.VMEM(vector.shape, jnp.float32)], name="last",
+    theirs = shaped(2 * ITERS + 2, ROWS, BLOCK)
+    chunks, two, coeff, same, flip, theirs = call(
+        functools.partial(last_kernel, total, shift),
+        [shaped(devices, BLOCK), vector, tile, tile, tile, theirs], [VMEM] * 7, name="last",
     )(got, zero, one, coeff, *near)
     got = lax.all_to_all(chunks.reshape(devices, 1, BLOCK), AXES, 0, 0)
-    partner = swapped(theirs, 1)
-    across = swapped(mine[2 * ITERS], devices // 2)
-    flipped = swapped(theirs[2 * ITERS], devices // 2 ^ 1)
-    kept, known = call(
-        keep_kernel, [shaped(ITERS + 1, ROWS, panels), tile], [VMEM] * 4 + [HBM],
+    kept, known, gram = call(
+        keep_kernel, [shaped(ITERS + 1, ROWS, panels), tile, tile], [VMEM] * 8 + [HBM],
         [pltpu.VMEM(mirror_rows.shape, jnp.int32), pltpu.SemaphoreType.DMA], name="keep",
-    )(mine, partner, across, flipped, mirror_rows)
+    )(
+        zero, one, two, coeff, same, swapped(theirs, 1), swapped(same, devices // 2),
+        swapped(flip, devices // 2 ^ 1), mirror_rows,
+    )
     basis, hessenberg = call(
         functools.partial(final_kernel, total),
-        [shaped(ITERS + 1, ROWS, panels), shaped(ITERS, ITERS + 1, ROWS)], [VMEM] * 3,
+        [shaped(ITERS + 1, ROWS, panels), shaped(ITERS, ITERS + 1, ROWS)], [VMEM] * 4,
         name="final",
-    )(got.reshape(devices, BLOCK), kept, known)
+    )(got.reshape(devices, BLOCK), kept, known, gram)
     return basis[:, None], hessenberg.transpose(2, 1, 0)
 
 

time: 54.8 us -> 55 us (level)
  starting transfers between devices: 12.3 us -> 14.2 us
  blocking collectives: 21.4 us -> 19.8 us
    all_to_all x1, starting transfers between devices: 2.54 us -> 4.18 us  [on_device(): got = lax.all_to_all(chunks.reshape(devices, 1, BLOCK), AXES, 0, 0)]
    all_to_all x2, blocking collectives: 21.4 us -> 19.8 us  [exchanged(): return lax.all_to_all(chunks, AXES, 0, 0, axis_index_groups=same_core)]
    ppermute x5 -> x6, starting transfers between devices: 2.78 us -> 3.04 us  [swapped(): return lax.ppermute(value, AXES, [(i, i ^ bits) for i in range(devices)])]
    ppermute x5 -> x6, waiting for transfers between devices: 4.05 us -> 4.13 us  [swapped(): return lax.ppermute(value, AXES, [(i, i ^ bits) for i in range(devices)])]
  transfers between devices with their start and end apart: 7 -> 8, of which waited for: 5 -> 6; matrix products, arithmetic and copies ran while one was open for 0% -> 0% of each run, Pallas kernels for 4% -> 2%
where the time goes in v3:
time: 55 us; the launch traced here: 54.7 us
  blocking collectives  19.8 us (36%)
  starting transfers between devices  14.2 us (26%)
  waiting for transfers between devices  10.1 us (18%)
  Pallas kernels  7.23 us (13%)
  local copies, waits for them, and re-layouts  2.61 us (5%)
  between operations  0.73 us (1%)
    all_to_all x2, blocking collectives, exchanged(): return lax.all_to_all(chunks, AXES, 0, 0, axis_index_groups=same_core)  19.8 us
    all_to_all x1, starting transfers between devices, on_device(): got = lax.all_to_all(chunks, AXES, 0, 0)  6.96 us
    all_to_all x1, waiting for transfers between devices, on_device(): got = lax.all_to_all(chunks, AXES, 0, 0)  4.78 us
    all_to_all x1, starting transfers between devices, on_device(): got = lax.all_to_all(chunks.reshape(devices, 1, BLOCK), AXES, 0, 0)  4.18 us
    ppermute x6, waiting for transfers between devices, swapped(): return lax.ppermute(value, AXES, [(i, i ^ bits) for i in range(devices)])  4.13 us
    ppermute x6, starting transfers between devices, swapped(): return lax.ppermute(value, AXES, [(i, i ^ bits) for i in range(devices)])  3.04 us
    unnamed x10, local copies, waits for them, and re-layouts  2.61 us
    pallas_call x1, Pallas kernels, on_device(): call(functools.partial(last_kernel, total, shift), [shaped(devices, BLOCK...  1.93 us
  transfers between devices with their start and end apart: 8, of which 6 were waited for; matrix products, arithmetic and copies ran while one was open for 0% of the time, Pallas kernels for 2%

profile of v3, /device:TPU:0, one launch (start us, length us, event | category | flops | bytes accessed | tf_op | source)
XLA Modules:
  0.0 54.7 jit_solution(2268477588883904852)
XLA Ops:
  0.6 0.0 copy-start.2
  0.6 0.7 %copy-done.2 = s32[256]{0:T(256)S(1)} copy-done((s32[256]{0:T(256)S(1)}, s32[256]{0:T(256)}, u32[]{:S(2)}) %copy-start.2) | copy-done | bytes 1048
  1.3 0.0 copy-start.1
  1.3 0.7 %copy-done.1 = f32[1,8,256]{2,1,0:T(8,128)S(1)} copy-done((f32[1,8,256]{2,1,0:T(8,128)S(1)}, f32[1,8,256]{2,1,0:T(8,128)}, u32[]{:S(2)}) %copy-start.1) | copy-done | bytes 8216
  2.0 0.9 %start.1 = f32[32,8,128]{2,1,0:T(8,128)} custom-call(f32[8,256]{1,0:T(8,128)S(1)} %bitcast.14, s32[2,128]{1,0:T(2,128)S(1)} %bitcast.15), custom_call_target="tpu_custom_call" | custom-call | tf_op jit(solution)/shard_map/start/pallas_call | solution.py:353
  2.9 0.0 copy-start.3
  2.9 0.0 copy-start.4
  2.9 0.5 collective-permute-start.2
  3.5 7.0 %all-to-all-start = ((f32[32,8,128]{2,1,0:T(8,128)}), f32[32,8,128]{2,1,0:T(8,128)S(1)}, u32[]{:S(2)}, u32[]{:S(2)}) async-start(f32[32,8,128]{2,1,0:T(8,128)} %start.1), calls=%async_computation | async-start | bytes 262144 | tf_op jit(solution)/shard_map/all_to_all | solution.py:365
  10.4 0.0 copy-done.3
  10.4 0.3 collective-permute-start
  10.8 0.0 copy-done.4
  10.8 0.3 collective-permute-start.1
  11.0 0.6 %collective-permute-done.other_rows = s32[1,32]{1,0:T(1,128)S(1)} collective-permute-done((s32[1,32]{1,0:T(1,128)S(1)}, s32[1,32]{1,0:T(1,128)S(1)}, u32[]{:S(2)}, u32[]{:S(2)}) %collective-permute-start) | collective-permute-done | bytes 160 | tf_op jit(solution)/shard_map/ppermute | solution.py:348
  11.6 0.3 collective-permute-done.1.other_cols
  11.9 0.0 copy-start
  11.9 1.2 %copy-done = bf16[1,32,128,128]{3,2,1,0:T(8,128)(2,1)S(1)} copy-done((bf16[1,32,128,128]{3,2,1,0:T(8,128)(2,1)S(1)}, bf16[1,32,128,128]{3,2,1,0:T(8,128)(2,1)}, u32[]{:S(2)}) %copy-start) | copy-done | bytes 1048600
  13.1 0.7 %prepare.1 = (bf16[32,128,128]{2,1,0:T(8,128)(2,1)S(1)}, bf16[512,128]{1,0:T(8,128)(2,1)S(1)}) custom-call(bf16[32,128,128]{2,1,0:T(8,128)(2,1)S(1)} %bitcast.12, s32[1,32]{1,0:T(1,128)S(1)} %copy-done.3, s32[1,32]{1,0:T(1,128)S(1)} %copy-done.4, s32[1,32]{1,0:T(1,128)S(1)} %collective-permute-done.other_rows, s32[1,32]{1,0:T(1,128)S(1)} %collective-permute-done.1.other_cols), custom_call_target="tpu_custom_call" | custom-call | tf_op jit(solution)/shard_map/prepare/pallas_call | solution.py:367
  13.8 4.8 %all-to-all-done.got_ref = f32[32,8,128]{2,1,0:T(8,128)S(1)} async-done(((f32[32,8,128]{2,1,0:T(8,128)}), f32[32,8,128]{2,1,0:T(8,128)S(1)}, u32[]{:S(2)}, u32[]{:S(2)}) %all-to-all-start) | async-done | bytes 131104 | tf_op jit(solution)/shard_map/all_to_all | solution.py:365
  18.6 0.0 collective-permute-done.2.other_ref
  18.6 1.0 %first.1 = (f32[16,2,8,128]{3,2,1,0:T(8,128)S(1)}, f32[32,8,128]{2,1,0:T(8,128)S(1)}, f32[8,128]{1,0:T(8,128)S(1)}) custom-call(f32[32,8,128]{2,1,0:T(8,128)S(1)} %all-to-all-done.got_ref, bf16[512,128]{1,0:T(8,128)(2,1)S(1)} %get-tuple-element.29.pick_ref, bf16[32,128,128]{2,1,0:T(8,128)(2,1)S(1)} %get-tuple-element.30.own_ref, ...), custom_call_target="tpu_custom_call" | custom-call | tf_op jit(solution)/shard_map/first/pallas_call | solution.py:376
  19.6 10.0 %all_to_all.20.got_ref = f32[16,2,8,128]{3,2,1,0:T(8,128)S(1)} all-to-all(f32[16,2,8,128]{3,2,1,0:T(8,128)S(1)} %get-tuple-element.31), channel_id=1, replica_groups={{12,14,16,18,20,22,24,26,28,30,0,2,4,6,8,10},{13,15,17,19,21,23,25,27,2..., dimensions={0} | all-to-all | bytes 262144 | tf_op jit(solution)/shard_map/all_to_all | solution.py:351
  29.6 1.2 %middle.1 = (f32[16,2,8,128]{3,2,1,0:T(8,128)S(1)}, f32[32,8,128]{2,1,0:T(8,128)S(1)}, f32[8,128]{1,0:T(8,128)S(1)}) custom-call(f32[16,2,8,128]{3,2,1,0:T(8,128)S(1)} %all_to_all.20.got_ref, f32[32,8,128]{2,1,0:T(8,128)S(1)} %get-tuple-element.32.basis_ref.zero_ref, f32[8,128]{1,0:T(8,128)S(1)} %get-tuple-element.33.known_ref, ...), custom_call_target="tpu_custom_call" | custom-call | tf_op jit(solution)/shard_map/middle/pallas_call | solution.py:380
  30.8 9.8 %all_to_all.21.got_ref = f32[16,2,8,128]{3,2,1,0:T(8,128)S(1)} all-to-all(f32[16,2,8,128]{3,2,1,0:T(8,128)S(1)} %get-tuple-element.34), channel_id=1, replica_groups={{12,14,16,18,20,22,24,26,28,30,0,2,4,6,8,10},{13,15,17,19,21,23,25,27,2..., dimensions={0} | all-to-all | bytes 262144 | tf_op jit(solution)/shard_map/all_to_all | solution.py:351
  40.5 1.9 %last.1 = (f32[32,128]{1,0:T(8,128)}, f32[32,8,128]{2,1,0:T(8,128)S(1)}, f32[8,128]{1,0:T(8,128)S(1)}, f32[8,128]{1,0:T(8,128)S(1)}, f32[8,128]{1,0:T(8,128)S(1)}, /*index=5*/f32[8,8,128]{2,1,0:T(8,128)S(1)}) custom-call(f32[16,2,8,128]{3,2,1,0:T(8,128)S(1)} %all_to_all.21.got_ref, f32[32,8,128]{2,1,0:T(8,128)S(1)} %get-tuple-element.32.basis_ref.zero_ref, ...), custom_call_target="tpu_custom_call" | custom-call | tf_op jit(solution)/shard_map/last/pallas_call | solution.py:386
  42.5 0.0 collective-permute-start.3
  42.5 4.2 %all-to-all-start.3 = ((f32[32,1,128]{2,1,0:T(1,128)}), f32[32,1,128]{2,1,0:T(1,128)S(1)}, u32[]{:S(2)}, u32[]{:S(2)}) async-start(f32[32,1,128]{2,1,0:T(1,128)} %bitcast.4), calls=%async_computation.3 | async-start | bytes 32768 | tf_op jit(solution)/shard_map/all_to_all | solution.py:390
  46.7 1.6 %collective-permute-start.5 = (f32[8,128]{1,0:T(8,128)S(1)}, f32[8,128]{1,0:T(8,128)S(1)}, u32[]{:S(2)}, u32[]{:S(2)}) collective-permute-start(f32[8,128]{1,0:T(8,128)S(1)} %get-tuple-element.42), channel_id=1, source_target_pairs={{0,17},{1,16},{2,19},{3,18},{4,21},{5,20},{6,23},{7,22},{8,25},{9,... | collective-permute-start | bytes 12296 | tf_op jit(solution)/shard_map/ppermute | solution.py:348
  48.3 0.4 collective-permute-start.4
  48.6 1.1 %collective-permute-done.5.flipped_ref = f32[8,128]{1,0:T(8,128)S(1)} collective-permute-done((f32[8,128]{1,0:T(8,128)S(1)}, f32[8,128]{1,0:T(8,128)S(1)}, u32[]{:S(2)}, u32[]{:S(2)}) %collective-permute-start.5) | collective-permute-done | bytes 4128 | tf_op jit(solution)/shard_map/ppermute | solution.py:348
  49.8 2.1 %collective-permute-done.4.across_ref = f32[8,128]{1,0:T(8,128)S(1)} collective-permute-done((f32[8,128]{1,0:T(8,128)S(1)}, f32[8,128]{1,0:T(8,128)S(1)}, u32[]{:S(2)}, u32[]{:S(2)}) %collective-permute-start.4) | collective-permute-done | bytes 4128 | tf_op jit(solution)/shard_map/ppermute | solution.py:348
  51.9 0.0 collective-permute-done.3.theirs_ref
  51.9 0.6 %keep.1 = (f32[4,8,256]{2,1,0:T(8,128)S(1)}, f32[8,128]{1,0:T(8,128)S(1)}, f32[8,128]{1,0:T(8,128)S(1)}) custom-call(f32[32,8,128]{2,1,0:T(8,128)S(1)} %get-tuple-element.32.basis_ref.zero_ref, f32[32,8,128]{2,1,0:T(8,128)S(1)} %get-tuple-element.35.one_ref, f32[32,8,128]{2,1,0:T(8,128)S(1)} %get-tuple-element.38.two_ref, ...), custom_call_target="tpu_custom_call" | custom-call | tf_op jit(solution)/shard_map/keep/pallas_call | solution.py:391
  52.5 1.2 %all-to-all-done.3 = f32[32,1,128]{2,1,0:T(1,128)S(1)} async-done(((f32[32,1,128]{2,1,0:T(1,128)}), f32[32,1,128]{2,1,0:T(1,128)S(1)}, u32[]{:S(2)}, u32[]{:S(2)}) %all-to-all-start.3) | async-done | bytes 16416 | tf_op jit(solution)/shard_map/all_to_all | solution.py:390
  53.7 0.9 %final.1 = (f32[4,8,256]{2,1,0:T(8,128)}, f32[3,4,8]{2,1,0:T(4,128)}) custom-call(f32[32,128]{1,0:T(8,128)S(1)} %bitcast.13, f32[4,8,256]{2,1,0:T(8,128)S(1)} %get-tuple-element.43.kept_ref, f32[8,128]{1,0:T(8,128)S(1)} %get-tuple-element.44.known_ref, f32[8,128]{1,0:T(8,128)S(1)} %get-tuple-element.45.gram_ref), custom_call_target="tpu_custom_call" | custom-call | tf_op jit(solution)/shard_map/final/pallas_call | solution.py:398
Async XLA Ops:
  0.6 0.7 %copy-start.2 = (s32[256]{0:T(256)S(1)}, s32[256]{0:T(256)}, u32[]{:S(2)}) copy-start(s32[256]{0:T(256)} %param.9) | copy-start | bytes 3076
  1.3 0.7 %copy-start.1 = (f32[1,8,256]{2,1,0:T(8,128)S(1)}, f32[1,8,256]{2,1,0:T(8,128)}, u32[]{:S(2)}) copy-start(f32[1,8,256]{2,1,0:T(8,128)} %param.5) | copy-start | bytes 24580
  2.9 7.5 %copy-start.3 = (s32[1,32]{1,0:T(1,128)S(1)}, s32[1,32]{1,0:T(1,128)}, u32[]{:S(2)}) copy-start(s32[1,32]{1,0:T(1,128)} %own_rows) | copy-start | bytes 388
  2.9 7.8 %copy-start.4 = (s32[1,32]{1,0:T(1,128)S(1)}, s32[1,32]{1,0:T(1,128)}, u32[]{:S(2)}) copy-start(s32[1,32]{1,0:T(1,128)} %own_cols) | copy-start | bytes 388
  2.9 15.7 %collective-permute-start.2 = (bf16[32,128,128]{2,1,0:T(8,128)(2,1)}, bf16[32,128,128]{2,1,0:T(8,128)(2,1)S(1)}, u32[]{:S(2)}, u32[]{:S(2)}) collective-permute-start(bf16[32,128,128]{2,1,0:T(8,128)(2,1)} %bitcast.11), channel_id=1, source_target_pairs={{0,1},{1,0},{2,3},{3,2},{4,5},{5,4},{6,7},{7,6},{8,9},{9,8},{10,11... | collective-permute-start | bytes 3145736 | tf_op jit(solution)/shard_map/ppermute | solution.py:348
  3.5 15.1 %all-to-all-start = ((f32[32,8,128]{2,1,0:T(8,128)}), f32[32,8,128]{2,1,0:T(8,128)S(1)}, u32[]{:S(2)}, u32[]{:S(2)}) async-start(f32[32,8,128]{2,1,0:T(8,128)} %start.1), calls=%async_computation | async-start | bytes 262144 | tf_op jit(solution)/shard_map/all_to_all | solution.py:365
  10.4 1.2 %collective-permute-start = (s32[1,32]{1,0:T(1,128)S(1)}, s32[1,32]{1,0:T(1,128)S(1)}, u32[]{:S(2)}, u32[]{:S(2)}) collective-permute-start(s32[1,32]{1,0:T(1,128)S(1)} %copy-done.3), channel_id=1, source_target_pairs={{0,1},{1,0},{2,3},{3,2},{4,5},{5,4},{6,7},{7,6},{8,9},{9,8},{10,11... | collective-permute-start | bytes 392 | tf_op jit(solution)/shard_map/ppermute | solution.py:348
  10.8 1.1 %collective-permute-start.1 = (s32[1,32]{1,0:T(1,128)S(1)}, s32[1,32]{1,0:T(1,128)S(1)}, u32[]{:S(2)}, u32[]{:S(2)}) collective-permute-start(s32[1,32]{1,0:T(1,128)S(1)} %copy-done.4), channel_id=1, source_target_pairs={{0,1},{1,0},{2,3},{3,2},{4,5},{5,4},{6,7},{7,6},{8,9},{9,8},{10,11... | collective-permute-start | bytes 392 | tf_op jit(solution)/shard_map/ppermute | solution.py:348
  11.9 1.2 %copy-start = (bf16[1,32,128,128]{3,2,1,0:T(8,128)(2,1)S(1)}, bf16[1,32,128,128]{3,2,1,0:T(8,128)(2,1)}, u32[]{:S(2)}) copy-start(bf16[1,32,128,128]{3,2,1,0:T(8,128)(2,1)} %param.6) | copy-start | bytes 3145732
  42.5 9.4 %collective-permute-start.3 = (f32[8,8,128]{2,1,0:T(8,128)S(1)}, f32[8,8,128]{2,1,0:T(8,128)S(1)}, u32[]{:S(2)}, u32[]{:S(2)}) collective-permute-start(f32[8,8,128]{2,1,0:T(8,128)S(1)} %get-tuple-element.41), channel_id=1, source_target_pairs={{0,1},{1,0},{2,3},{3,2},{4,5},{5,4},{6,7},{7,6},{8,9},{9,8},{10,11... | collective-permute-start | bytes 98312 | tf_op jit(solution)/shard_map/ppermute | solution.py:348
  42.5 11.3 %all-to-all-start.3 = ((f32[32,1,128]{2,1,0:T(1,128)}), f32[32,1,128]{2,1,0:T(1,128)S(1)}, u32[]{:S(2)}, u32[]{:S(2)}) async-start(f32[32,1,128]{2,1,0:T(1,128)} %bitcast.4), calls=%async_computation.3 | async-start | bytes 32768 | tf_op jit(solution)/shard_map/all_to_all | solution.py:390
  46.7 3.1 %collective-permute-start.5 = (f32[8,128]{1,0:T(8,128)S(1)}, f32[8,128]{1,0:T(8,128)S(1)}, u32[]{:S(2)}, u32[]{:S(2)}) collective-permute-start(f32[8,128]{1,0:T(8,128)S(1)} %get-tuple-element.42), channel_id=1, source_target_pairs={{0,17},{1,16},{2,19},{3,18},{4,21},{5,20},{6,23},{7,22},{8,25},{9,... | collective-permute-start | bytes 12296 | tf_op jit(solution)/shard_map/ppermute | solution.py:348
  48.3 3.6 %collective-permute-start.4 = (f32[8,128]{1,0:T(8,128)S(1)}, f32[8,128]{1,0:T(8,128)S(1)}, u32[]{:S(2)}, u32[]{:S(2)}) collective-permute-start(f32[8,128]{1,0:T(8,128)S(1)} %get-tuple-element.40.same_ref), channel_id=1, source_target_pairs={{0,16},{1,17},{2,18},{3,19},{4,20},{5,21},{6,22},{7,23},{8,24},{9,... | collective-permute-start | bytes 12296 | tf_op jit(solution)/shard_map/ppermute | solution.py:348

commit v4 on v3

--- a/solution.py
+++ b/solution.py
@@ -152,9 +152,9 @@
     port = got_ref[:owners]
     star = got_ref[owners:]
     squares = per_rhs(jnp.sum(port * port + star * star, axis=0))
-    length = jnp.sqrt(squares * (1.0 / total) + EPSILON)
-    scale = 1.0 / length
-    coeff_ref[...] = columns({LENGTH_LANE: length})
+    squares = squares * (1.0 / total) + EPSILON
+    scale = lax.rsqrt(squares)
+    coeff_ref[...] = columns({LENGTH_LANE: jnp.sqrt(squares)})
     basis_ref[:owners] = (port + star) * scale
     basis_ref[owners:] = (port - star) * scale
     spread(chunk_ref, *image(basis_ref, pick_ref, own_ref, other_ref))
@@ -169,8 +169,8 @@
     rest = got
     for coeff, ref in zip(coeffs, basis_refs):
         rest = rest - coeff * ref[...]
-    norm = jnp.sqrt(dot(rest, rest) * inner + EPSILON)
-    return coeffs + [norm], rest * (1.0 / norm)
+    squares = dot(rest, rest) * inner + EPSILON
+    return coeffs + [jnp.sqrt(squares)], rest * lax.rsqrt(squares)
 
 
 def middle_kernel(total, shift, got_ref, basis_ref, known_ref, pick_ref, own_ref, other_ref,
@@ -181,7 +181,7 @@
 
 
 def last_kernel(total, shift, got_ref, zero_ref, one_ref, known_ref, pick_ref, own_ref, other_ref,
-                chunk_ref, two_ref, coeff_ref, same_ref, flip_ref, theirs_ref):
+                chunk_ref, two_ref, coeff_ref, same_ref, flip_ref):
     side, owner, core = position()
     owners = two_ref.shape[0] // 2
     refs = [zero_ref, one_ref, two_ref]
@@ -204,7 +204,12 @@
     coeff_ref[...] = coeffs + known_ref[...]
     same_ref[...] = jnp.where(core == 0, tiles[0], tiles[1])
     flip_ref[...] = jnp.where(core == 0, tiles[1], tiles[0])
-    for index, ref in enumerate(refs):
+
+
+def pack_kernel(zero_ref, one_ref, two_ref, coeff_ref, flip_ref, theirs_ref):
+    _, owner, core = position()
+    owners = zero_ref.shape[0] // 2
+    for index, ref in enumerate((zero_ref, one_ref, two_ref)):
         for half in range(2):
             theirs_ref[2 * index + half] = ref[half * owners + owner + 1 - 2 * core]
     theirs_ref[2 * ITERS] = flip_ref[...]
@@ -291,12 +296,13 @@
         squares = squares - coeffs[j] * coeffs[j] * (1.0 + gram[:, j : j + 1])
     for place, (i, j) in enumerate(((0, 1), (0, 2), (1, 2))):
         squares = squares + 2.0 * coeffs[i] * coeffs[j] * gram[:, ITERS + place : ITERS + place + 1]
-    norm = jnp.sqrt(jnp.maximum(squares, 0.0) + EPSILON)
+    squares = jnp.maximum(squares, 0.0) + EPSILON
+    norm = jnp.sqrt(squares)
     rest = kept_ref[ITERS]
     for j in range(ITERS):
         rest = rest - coeffs[j] * kept_ref[j]
     basis_ref[:ITERS] = kept_ref[:ITERS]
-    basis_ref[ITERS] = rest * (1.0 / norm)
+    basis_ref[ITERS] = rest * lax.rsqrt(squares)
     place = 2 * (ITERS + 1)
     whole = known_ref[...] + columns(
         {place + index: value for index, value in enumerate(coeffs + [norm])}
@@ -313,6 +319,10 @@
 
 def shaped(*shape, dtype=jnp.float32):
     return jax.ShapeDtypeStruct(shape, dtype)
+
+
+def in_hbm(value):
+    return pltpu.with_memory_space_constraint(value, pltpu.HBM)
 
 
 def call(kernel, outs, specs, scratch=(), name=None):
@@ -351,14 +361,14 @@
         return lax.all_to_all(chunks, AXES, 0, 0, axis_index_groups=same_core)
 
     [chunks] = call(
-        start_kernel, [vector], [HBM, HBM],
+        start_kernel, [pltpu.VMEM(vector.shape, jnp.float32)], [HBM, HBM],
         [
             pltpu.VMEM(sources.shape[1:], jnp.float32),
             pltpu.VMEM(mirror_rows.shape, jnp.int32),
             pltpu.SemaphoreType.DMA((2,)),
         ],
         name="start",
-    )(sources[0], mirror_rows)
+    )(in_hbm(sources[0]), in_hbm(mirror_rows))
     chunks, blocks, block_rows, block_cols = lax.optimization_barrier(
         (chunks, blocks, block_rows, block_cols)
     )
@@ -371,7 +381,7 @@
             shaped(2 * ROWS * blocks.shape[0], owners * ROWS, dtype=jnp.bfloat16),
         ],
         [HBM] + [SMEM] * 4, [pltpu.SemaphoreType.DMA], name="prepare",
-    )(blocks, block_rows, block_cols, swapped(block_rows, 1), swapped(block_cols, 1))
+    )(in_hbm(blocks), block_rows, block_cols, swapped(block_rows, 1), swapped(block_cols, 1))
     near = (pick, own_blocks, other_blocks)
     chunks, zero, coeff = call(
         functools.partial(first_kernel, total), [chunk, vector, tile], [VMEM] * 4, name="first"
@@ -382,18 +392,21 @@
         name="middle",
     )(got, zero, coeff, *near)
     got = exchanged(chunks)
-    theirs = shaped(2 * ITERS + 2, ROWS, BLOCK)
-    chunks, two, coeff, same, flip, theirs = call(
+    chunks, two, coeff, same, flip = call(
         functools.partial(last_kernel, total, shift),
-        [shaped(devices, BLOCK), vector, tile, tile, tile, theirs], [VMEM] * 7, name="last",
+        [pltpu.VMEM((devices, BLOCK), jnp.float32), vector, tile, tile, tile], [VMEM] * 7,
+        name="last",
     )(got, zero, one, coeff, *near)
     got = lax.all_to_all(chunks.reshape(devices, 1, BLOCK), AXES, 0, 0)
+    [theirs] = call(
+        pack_kernel, [shaped(2 * ITERS + 2, ROWS, BLOCK)], [VMEM] * 5, name="pack"
+    )(zero, one, two, coeff, flip)
     kept, known, gram = call(
         keep_kernel, [shaped(ITERS + 1, ROWS, panels), tile, tile], [VMEM] * 8 + [HBM],
         [pltpu.VMEM(mirror_rows.shape, jnp.int32), pltpu.SemaphoreType.DMA], name="keep",
     )(
         zero, one, two, coeff, same, swapped(theirs, 1), swapped(same, devices // 2),
-        swapped(flip, devices // 2 ^ 1), mirror_rows,
+        swapped(flip, devices // 2 ^ 1), in_hbm(mirror_rows),
     )
     basis, hessenberg = call(
         functools.partial(final_kernel, total),

time: 55 us -> 54.3 us (0.987)
  local copies, waits for them, and re-layouts: 2.61 us -> 0.01 us
  Pallas kernels: 7.23 us -> 9.38 us
    unnamed x10 -> x4, local copies, waits for them, and re-layouts: 2.61 us -> 0.01 us
    pallas_call x1, Pallas kernels: 0.71 us -> 1.79 us  [on_device(): call(prepare_kernel, [shaped(*blocks.shape, dtype=blocks.dtype), shaped(2...]
    pallas_call x2 -> x3, Pallas kernels: 2.84 us -> 3.53 us  [the longest x1 1.92 us: on_device(): call(functools.partial(last_kernel, total, shift), [pltpu.VMEM((devices,...]
  transfers between devices with their start and end apart: 8 -> 8, of which waited for: 6 -> 6; matrix products, arithmetic and copies ran while one was open for 0% -> 0% of each run, Pallas kernels for 2% -> 5%
where the time goes in v4:
time: 54.3 us; the launch traced here: 54 us
  blocking collectives  19.8 us (36%)
  starting transfers between devices  14.1 us (26%)
  waiting for transfers between devices  9.99 us (18%)
  Pallas kernels  9.38 us (17%)
  between operations  0.72 us (1%)
    all_to_all x2, blocking collectives, exchanged(): return lax.all_to_all(chunks, AXES, 0, 0, axis_index_groups=same_core)  19.8 us
    all_to_all x1, starting transfers between devices, on_device(): got = lax.all_to_all(chunks, AXES, 0, 0)  6.96 us
    all_to_all x1, waiting for transfers between devices, on_device(): got = lax.all_to_all(chunks, AXES, 0, 0)  4.92 us
    all_to_all x1, starting transfers between devices, on_device(): got = lax.all_to_all(chunks.reshape(devices, 1, BLOCK), AXES, 0, 0)  4.17 us
    ppermute x6, waiting for transfers between devices, swapped(): return lax.ppermute(value, AXES, [(i, i ^ bits) for i in range(devices)])  3.9 us
    ppermute x6, starting transfers between devices, swapped(): return lax.ppermute(value, AXES, [(i, i ^ bits) for i in range(devices)])  2.93 us
    pallas_call x1, Pallas kernels, on_device(): call(functools.partial(last_kernel, total, shift), [pltpu.VMEM((devices,...  1.92 us
    pallas_call x1, Pallas kernels, on_device(): call(prepare_kernel, [shaped(*blocks.shape, dtype=blocks.dtype), shaped(2...  1.79 us
  transfers between devices with their start and end apart: 8, of which 6 were waited for; matrix products, arithmetic and copies ran while one was open for 0% of the time, Pallas kernels for 5%

profile of v4, /device:TPU:0, one launch (start us, length us, event | category | flops | bytes accessed | tf_op | source)
XLA Modules:
  0.0 54.0 jit_solution(14109946765985366442)
XLA Ops:
  0.6 1.6 %start.1 = f32[32,8,128]{2,1,0:T(8,128)} custom-call(f32[8,256]{1,0:T(8,128)} %bitcast.14, s32[2,128]{1,0:T(2,128)} %bitcast.15), custom_call_target="tpu_custom_call" | custom-call | tf_op jit(solution)/shard_map/start/pallas_call | solution.py:363
  2.2 0.0 copy-start
  2.3 0.0 copy-start.1
  2.3 0.5 collective-permute-start.2
  2.8 7.0 %all-to-all-start = ((f32[32,8,128]{2,1,0:T(8,128)}), f32[32,8,128]{2,1,0:T(8,128)S(1)}, u32[]{:S(2)}, u32[]{:S(2)}) async-start(f32[32,8,128]{2,1,0:T(8,128)} %start.1), calls=%async_computation | async-start | bytes 262144 | tf_op jit(solution)/shard_map/all_to_all | solution.py:375
  9.7 0.0 copy-done
  9.8 0.3 collective-permute-start
  10.1 0.0 copy-done.1
  10.1 0.3 collective-permute-start.1
  10.3 0.6 %collective-permute-done.other_rows = s32[1,32]{1,0:T(1,128)S(1)} collective-permute-done((s32[1,32]{1,0:T(1,128)S(1)}, s32[1,32]{1,0:T(1,128)S(1)}, u32[]{:S(2)}, u32[]{:S(2)}) %collective-permute-start) | collective-permute-done | bytes 160 | tf_op jit(solution)/shard_map/ppermute | solution.py:358
  10.9 0.3 collective-permute-done.1.other_cols
  11.2 1.8 %prepare.1 = (bf16[32,128,128]{2,1,0:T(8,128)(2,1)S(1)}, bf16[512,128]{1,0:T(8,128)(2,1)S(1)}) custom-call(bf16[32,128,128]{2,1,0:T(8,128)(2,1)} %bitcast.13, s32[1,32]{1,0:T(1,128)S(1)} %copy-done, s32[1,32]{1,0:T(1,128)S(1)} %copy-done.1, s32[1,32]{1,0:T(1,128)S(1)} %collective-permute-done.other_rows, s32[1,32]{1,0:T(1,128)S(1)} %collective-permute-done.1.other_cols), custom_call_target="tpu_custom_call" | custom-call | tf_op jit(solution)/shard_map/prepare/pallas_call | solution.py:377
  13.0 4.9 %all-to-all-done.got_ref = f32[32,8,128]{2,1,0:T(8,128)S(1)} async-done(((f32[32,8,128]{2,1,0:T(8,128)}), f32[32,8,128]{2,1,0:T(8,128)S(1)}, u32[]{:S(2)}, u32[]{:S(2)}) %all-to-all-start) | async-done | bytes 131104 | tf_op jit(solution)/shard_map/all_to_all | solution.py:375
  17.9 0.0 collective-permute-done.2.other_ref
  17.9 1.0 %first.1 = (f32[16,2,8,128]{3,2,1,0:T(8,128)S(1)}, f32[32,8,128]{2,1,0:T(8,128)S(1)}, f32[8,128]{1,0:T(8,128)S(1)}) custom-call(f32[32,8,128]{2,1,0:T(8,128)S(1)} %all-to-all-done.got_ref, bf16[512,128]{1,0:T(8,128)(2,1)S(1)} %get-tuple-element.28.pick_ref, bf16[32,128,128]{2,1,0:T(8,128)(2,1)S(1)} %get-tuple-element.29.own_ref, ...), custom_call_target="tpu_custom_call" | custom-call | tf_op jit(solution)/shard_map/first/pallas_call | solution.py:386
  18.9 10.0 %all_to_all.20.got_ref = f32[16,2,8,128]{3,2,1,0:T(8,128)S(1)} all-to-all(f32[16,2,8,128]{3,2,1,0:T(8,128)S(1)} %get-tuple-element.30), channel_id=1, replica_groups={{12,14,16,18,20,22,24,26,28,30,0,2,4,6,8,10},{13,15,17,19,21,23,25,27,2..., dimensions={0} | all-to-all | bytes 262144 | tf_op jit(solution)/shard_map/all_to_all | solution.py:361
  28.9 1.2 %middle.1 = (f32[16,2,8,128]{3,2,1,0:T(8,128)S(1)}, f32[32,8,128]{2,1,0:T(8,128)S(1)}, f32[8,128]{1,0:T(8,128)S(1)}) custom-call(f32[16,2,8,128]{3,2,1,0:T(8,128)S(1)} %all_to_all.20.got_ref, f32[32,8,128]{2,1,0:T(8,128)S(1)} %get-tuple-element.31.basis_ref.zero_ref, f32[8,128]{1,0:T(8,128)S(1)} %get-tuple-element.32.known_ref, ...), custom_call_target="tpu_custom_call" | custom-call | tf_op jit(solution)/shard_map/middle/pallas_call | solution.py:390
  30.1 9.8 %all_to_all.21.got_ref = f32[16,2,8,128]{3,2,1,0:T(8,128)S(1)} all-to-all(f32[16,2,8,128]{3,2,1,0:T(8,128)S(1)} %get-tuple-element.33), channel_id=1, replica_groups={{12,14,16,18,20,22,24,26,28,30,0,2,4,6,8,10},{13,15,17,19,21,23,25,27,2..., dimensions={0} | all-to-all | bytes 262144 | tf_op jit(solution)/shard_map/all_to_all | solution.py:361
  39.9 1.9 %last.1 = (f32[32,128]{1,0:T(8,128)}, f32[32,8,128]{2,1,0:T(8,128)S(1)}, f32[8,128]{1,0:T(8,128)S(1)}, f32[8,128]{1,0:T(8,128)S(1)}, f32[8,128]{1,0:T(8,128)S(1)}) custom-call(f32[16,2,8,128]{3,2,1,0:T(8,128)S(1)} %all_to_all.21.got_ref, f32[32,8,128]{2,1,0:T(8,128)S(1)} %get-tuple-element.31.basis_ref.zero_ref, ...), custom_call_target="tpu_custom_call" | custom-call | tf_op jit(solution)/shard_map/last/pallas_call | solution.py:395
  41.8 0.0 collective-permute-start.3
  41.8 4.2 %all-to-all-start.3 = ((f32[32,1,128]{2,1,0:T(1,128)}), f32[32,1,128]{2,1,0:T(1,128)S(1)}, u32[]{:S(2)}, u32[]{:S(2)}) async-start(f32[32,1,128]{2,1,0:T(1,128)} %bitcast.4), calls=%async_computation.3 | async-start | bytes 32768 | tf_op jit(solution)/shard_map/all_to_all | solution.py:400
  46.0 1.8 %collective-permute-start.4 = (f32[8,128]{1,0:T(8,128)S(1)}, f32[8,128]{1,0:T(8,128)S(1)}, u32[]{:S(2)}, u32[]{:S(2)}) collective-permute-start(f32[8,128]{1,0:T(8,128)S(1)} %get-tuple-element.39.same_ref), channel_id=1, source_target_pairs={{0,16},{1,17},{2,18},{3,19},{4,20},{5,21},{6,22},{7,23},{8,24},{9,... | collective-permute-start | bytes 12296 | tf_op jit(solution)/shard_map/ppermute | solution.py:358
  47.8 0.0 collective-permute-start.5
  47.8 1.8 %collective-permute-done.4.across_ref = f32[8,128]{1,0:T(8,128)S(1)} collective-permute-done((f32[8,128]{1,0:T(8,128)S(1)}, f32[8,128]{1,0:T(8,128)S(1)}, u32[]{:S(2)}, u32[]{:S(2)}) %collective-permute-start.4) | collective-permute-done | bytes 4128 | tf_op jit(solution)/shard_map/ppermute | solution.py:358
  49.6 1.2 %collective-permute-done.5.flipped_ref = f32[8,128]{1,0:T(8,128)S(1)} collective-permute-done((f32[8,128]{1,0:T(8,128)S(1)}, f32[8,128]{1,0:T(8,128)S(1)}, u32[]{:S(2)}, u32[]{:S(2)}) %collective-permute-start.5) | collective-permute-done | bytes 4128 | tf_op jit(solution)/shard_map/ppermute | solution.py:358
  50.8 0.0 collective-permute-done.3.theirs_ref
  50.8 1.0 %keep.1 = (f32[4,8,256]{2,1,0:T(8,128)S(1)}, f32[8,128]{1,0:T(8,128)S(1)}, f32[8,128]{1,0:T(8,128)S(1)}) custom-call(f32[32,8,128]{2,1,0:T(8,128)S(1)} %get-tuple-element.31.basis_ref.zero_ref, f32[32,8,128]{2,1,0:T(8,128)S(1)} %get-tuple-element.34.one_ref, f32[32,8,128]{2,1,0:T(8,128)S(1)} %get-tuple-element.37.two_ref, ...), custom_call_target="tpu_custom_call" | custom-call | tf_op jit(solution)/shard_map/keep/pallas_call | solution.py:404
  51.9 1.2 %all-to-all-done.3 = f32[32,1,128]{2,1,0:T(1,128)S(1)} async-done(((f32[32,1,128]{2,1,0:T(1,128)}), f32[32,1,128]{2,1,0:T(1,128)S(1)}, u32[]{:S(2)}, u32[]{:S(2)}) %all-to-all-start.3) | async-done | bytes 16416 | tf_op jit(solution)/shard_map/all_to_all | solution.py:400
  53.0 0.9 %final.1 = (f32[4,8,256]{2,1,0:T(8,128)}, f32[3,4,8]{2,1,0:T(4,128)}) custom-call(f32[32,128]{1,0:T(8,128)S(1)} %bitcast.11, f32[4,8,256]{2,1,0:T(8,128)S(1)} %get-tuple-element.41.kept_ref, f32[8,128]{1,0:T(8,128)S(1)} %get-tuple-element.42.known_ref, f32[8,128]{1,0:T(8,128)S(1)} %get-tuple-element.43.gram_ref), custom_call_target="tpu_custom_call" | custom-call | tf_op jit(solution)/shard_map/final/pallas_call | solution.py:411
  (1 shorter events, 0.0 us)
Async XLA Ops:
  2.2 7.5 %copy-start = (s32[1,32]{1,0:T(1,128)S(1)}, s32[1,32]{1,0:T(1,128)}, u32[]{:S(2)}) copy-start(s32[1,32]{1,0:T(1,128)} %own_rows) | copy-start | bytes 388
  2.3 7.8 %copy-start.1 = (s32[1,32]{1,0:T(1,128)S(1)}, s32[1,32]{1,0:T(1,128)}, u32[]{:S(2)}) copy-start(s32[1,32]{1,0:T(1,128)} %own_cols) | copy-start | bytes 388
  2.3 15.7 %collective-permute-start.2 = (bf16[32,128,128]{2,1,0:T(8,128)(2,1)}, bf16[32,128,128]{2,1,0:T(8,128)(2,1)S(1)}, u32[]{:S(2)}, u32[]{:S(2)}) collective-permute-start(bf16[32,128,128]{2,1,0:T(8,128)(2,1)} %bitcast.12), channel_id=1, source_target_pairs={{0,1},{1,0},{2,3},{3,2},{4,5},{5,4},{6,7},{7,6},{8,9},{9,8},{10,11... | collective-permute-start | bytes 3145736 | tf_op jit(solution)/shard_map/ppermute | solution.py:358
  2.8 15.1 %all-to-all-start = ((f32[32,8,128]{2,1,0:T(8,128)}), f32[32,8,128]{2,1,0:T(8,128)S(1)}, u32[]{:S(2)}, u32[]{:S(2)}) async-start(f32[32,8,128]{2,1,0:T(8,128)} %start.1), calls=%async_computation | async-start | bytes 262144 | tf_op jit(solution)/shard_map/all_to_all | solution.py:375
  9.8 1.2 %collective-permute-start = (s32[1,32]{1,0:T(1,128)S(1)}, s32[1,32]{1,0:T(1,128)S(1)}, u32[]{:S(2)}, u32[]{:S(2)}) collective-permute-start(s32[1,32]{1,0:T(1,128)S(1)} %copy-done), channel_id=1, source_target_pairs={{0,1},{1,0},{2,3},{3,2},{4,5},{5,4},{6,7},{7,6},{8,9},{9,8},{10,11... | collective-permute-start | bytes 392 | tf_op jit(solution)/shard_map/ppermute | solution.py:358
  10.1 1.1 %collective-permute-start.1 = (s32[1,32]{1,0:T(1,128)S(1)}, s32[1,32]{1,0:T(1,128)S(1)}, u32[]{:S(2)}, u32[]{:S(2)}) collective-permute-start(s32[1,32]{1,0:T(1,128)S(1)} %copy-done.1), channel_id=1, source_target_pairs={{0,1},{1,0},{2,3},{3,2},{4,5},{5,4},{6,7},{7,6},{8,9},{9,8},{10,11... | collective-permute-start | bytes 392 | tf_op jit(solution)/shard_map/ppermute | solution.py:358
  41.8 9.1 %collective-permute-start.3 = (f32[8,8,128]{2,1,0:T(8,128)S(1)}, f32[8,8,128]{2,1,0:T(8,128)S(1)}, u32[]{:S(2)}, u32[]{:S(2)}) collective-permute-start(f32[8,8,128]{2,1,0:T(8,128)S(1)} %pack.1), channel_id=1, source_target_pairs={{0,1},{1,0},{2,3},{3,2},{4,5},{5,4},{6,7},{7,6},{8,9},{9,8},{10,11... | collective-permute-start | bytes 98312 | tf_op jit(solution)/shard_map/ppermute | solution.py:358
  41.8 11.2 %all-to-all-start.3 = ((f32[32,1,128]{2,1,0:T(1,128)}), f32[32,1,128]{2,1,0:T(1,128)S(1)}, u32[]{:S(2)}, u32[]{:S(2)}) async-start(f32[32,1,128]{2,1,0:T(1,128)} %bitcast.4), calls=%async_computation.3 | async-start | bytes 32768 | tf_op jit(solution)/shard_map/all_to_all | solution.py:400
  46.0 3.7 %collective-permute-start.4 = (f32[8,128]{1,0:T(8,128)S(1)}, f32[8,128]{1,0:T(8,128)S(1)}, u32[]{:S(2)}, u32[]{:S(2)}) collective-permute-start(f32[8,128]{1,0:T(8,128)S(1)} %get-tuple-element.39.same_ref), channel_id=1, source_target_pairs={{0,16},{1,17},{2,18},{3,19},{4,20},{5,21},{6,22},{7,23},{8,24},{9,... | collective-permute-start | bytes 12296 | tf_op jit(solution)/shard_map/ppermute | solution.py:358
  47.8 3.0 %collective-permute-start.5 = (f32[8,128]{1,0:T(8,128)S(1)}, f32[8,128]{1,0:T(8,128)S(1)}, u32[]{:S(2)}, u32[]{:S(2)}) collective-permute-start(f32[8,128]{1,0:T(8,128)S(1)} %get-tuple-element.40.flip_ref), channel_id=1, source_target_pairs={{0,17},{1,16},{2,19},{3,18},{4,21},{5,20},{6,23},{7,22},{8,25},{9,... | collective-permute-start | bytes 12296 | tf_op jit(solution)/shard_map/ppermute | solution.py:358

commit v5 on v4

--- a/solution.py
+++ b/solution.py
@@ -57,7 +57,7 @@
     )
 
 
-def start_kernel(sources_hbm, mirror_hbm, chunk_ref, sources_ref, mirror_ref, sems):
+def start_kernel(sources_hbm, mirror_hbm, chunk_ref, mirror_ref, sources_ref, sems):
     copies = [
         pltpu.make_async_copy(sources_hbm, sources_ref, sems.at[0]),
         pltpu.make_async_copy(mirror_hbm, mirror_ref, sems.at[1]),
@@ -70,7 +70,8 @@
     pieces = []
     for block in range(BLK_DEV):
         part = sources_ref[:, block * BLOCK : (block + 1) * BLOCK]
-        moved = exact_dot(part, mirror_onehot(mirror_ref, block), ((1,), (0,)))
+        places = jnp.broadcast_to(mirror_ref[block : block + 1, :], part.shape)
+        moved = jnp.take_along_axis(part, places, axis=1, mode="promise_in_bounds")
         pieces.append(jnp.where(side == 0, part, moved))
     tiles = [
         jnp.concatenate([piece[HALF_RHS * c : HALF_RHS * (c + 1)] for piece in pieces], axis=0)
@@ -196,8 +197,8 @@
             product = tiles[0] * refs[index][base] + tiles[1] * refs[index][base + 1]
         else:
             product = tiles[0] * tiles[0] + tiles[1] * tiles[1]
-        here = (lane == HALF_RHS * index + rhs) & (rhs < HALF_RHS)
-        spots = jnp.where(here, per_rhs(product), spots)
+        column = jnp.sum(product, axis=1, keepdims=True)
+        spots = jnp.where(lane == ROWS * index + rhs, column, spots)
     row = jnp.sum(spots, axis=0, keepdims=True)
     chunk_ref[...] = jnp.broadcast_to(row, chunk_ref.shape)
     coeffs = columns({place + ITERS + 1: value for place, value in enumerate(coeffs)})
@@ -217,9 +218,7 @@
 
 
 def keep_kernel(zero_ref, one_ref, two_ref, coeff_ref, same_ref, theirs_ref, across_ref,
-                flipped_ref, mirror_hbm, kept_ref, known_ref, gram_ref, mirror_ref, sem):
-    copy = pltpu.make_async_copy(mirror_hbm, mirror_ref, sem)
-    copy.start()
+                flipped_ref, mirror_ref, kept_ref, known_ref, gram_ref):
     side, owner, core = position()
     owners = zero_ref.shape[0] // 2
 
@@ -256,7 +255,6 @@
     zero_two = (entry(0, 1) * short[0] - entry(1, 1) * zero_one) / norms[2]
     one_two = (entry(1, 1) * short[1] - entry(0, 1) * zero_one) / norms[2]
     gram_ref[...] = columns(dict(enumerate(short + [zero_one, zero_two, one_two])))
-    copy.wait()
     for block in range(BLK_DEV):
         rows = slice(block * HALF_RHS, (block + 1) * HALF_RHS)
         ports, stars = [], []
@@ -285,7 +283,9 @@
     spots = jnp.where(rhs < HALF_RHS, lower, upper) * inner
     values = [
         jnp.sum(
-            jnp.where(lane == HALF_RHS * index + rhs % HALF_RHS, spots, 0.0), axis=1, keepdims=True
+            jnp.where((lane // ROWS == index) & (lane % HALF_RHS == rhs % HALF_RHS), spots, 0.0),
+            axis=1,
+            keepdims=True,
         )
         for index in range(ITERS + 1)
     ]
@@ -343,8 +343,7 @@
     chips = devices // 2
     panels = sources.shape[2]
     total = 1.0 * panels * devices
-    dev = lax.axis_size("dev")
-    shift = (dev + dev // 2) // 2 % chips
+    shift = 1
     same_core = [
         [(2 * (chip + shift) + core) % devices for chip in range(chips)] for core in range(2)
     ]
@@ -360,13 +359,11 @@
     def exchanged(chunks):
         return lax.all_to_all(chunks, AXES, 0, 0, axis_index_groups=same_core)
 
-    [chunks] = call(
-        start_kernel, [pltpu.VMEM(vector.shape, jnp.float32)], [HBM, HBM],
-        [
-            pltpu.VMEM(sources.shape[1:], jnp.float32),
-            pltpu.VMEM(mirror_rows.shape, jnp.int32),
-            pltpu.SemaphoreType.DMA((2,)),
-        ],
+    chunks, mirror_rows = call(
+        start_kernel,
+        [pltpu.VMEM(vector.shape, jnp.float32), shaped(*mirror_rows.shape, dtype=jnp.int32)],
+        [HBM, HBM],
+        [pltpu.VMEM(sources.shape[1:], jnp.float32), pltpu.SemaphoreType.DMA((2,))],
         name="start",
     )(in_hbm(sources[0]), in_hbm(mirror_rows))
     chunks, blocks, block_rows, block_cols = lax.optimization_barrier(
@@ -402,11 +399,10 @@
         pack_kernel, [shaped(2 * ITERS + 2, ROWS, BLOCK)], [VMEM] * 5, name="pack"
     )(zero, one, two, coeff, flip)
     kept, known, gram = call(
-        keep_kernel, [shaped(ITERS + 1, ROWS, panels), tile, tile], [VMEM] * 8 + [HBM],
-        [pltpu.VMEM(mirror_rows.shape, jnp.int32), pltpu.SemaphoreType.DMA], name="keep",
+        keep_kernel, [shaped(ITERS + 1, ROWS, panels), tile, tile], [VMEM] * 9, name="keep"
     )(
         zero, one, two, coeff, same, swapped(theirs, 1), swapped(same, devices // 2),
-        swapped(flip, devices // 2 ^ 1), in_hbm(mirror_rows),
+        swapped(flip, devices // 2 ^ 1), mirror_rows,
     )
     basis, hessenberg = call(
         functools.partial(final_kernel, total),

time: 54.3 us -> 52.5 us (0.967)
  starting transfers between devices: 14.1 us -> 12.4 us
  Pallas kernels: 9.38 us -> 8.48 us
  waiting for transfers between devices: 9.99 us -> 10.7 us
    all_to_all x1, starting transfers between devices: 4.17 us -> 2.57 us  [on_device(): got = lax.all_to_all(chunks.reshape(devices, 1, BLOCK), AXES, 0, 0)]
    all_to_all x1, waiting for transfers between devices: 1.17 us -> 1.9 us  [on_device(): got = lax.all_to_all(chunks.reshape(devices, 1, BLOCK), AXES, 0, 0)]
    pallas_call x1, Pallas kernels: 1.02 us -> 0.31 us  [on_device(): call(keep_kernel, [shaped(ITERS + 1, ROWS, panels), tile, tile], [VMEM] *...]
  transfers between devices with their start and end apart: 8 -> 8, of which waited for: 6 -> 6; matrix products, arithmetic and copies ran while one was open for 0% -> 0% of each run, Pallas kernels for 5% -> 4%
where the time goes in v5:
time: 52.5 us; the launch traced here: 52.2 us
  blocking collectives  19.8 us (38%)
  starting transfers between devices  12.4 us (24%)
  waiting for transfers between devices  10.7 us (20%)
  Pallas kernels  8.48 us (16%)
  between operations  0.72 us (1%)
    all_to_all x2, blocking collectives, exchanged(): return lax.all_to_all(chunks, AXES, 0, 0, axis_index_groups=same_core)  19.8 us
    all_to_all x1, starting transfers between devices, on_device(): got = lax.all_to_all(chunks, AXES, 0, 0)  6.96 us
    all_to_all x1, waiting for transfers between devices, on_device(): got = lax.all_to_all(chunks, AXES, 0, 0)  4.92 us
    ppermute x6, waiting for transfers between devices, swapped(): return lax.ppermute(value, AXES, [(i, i ^ bits) for i in range(devices)])  3.9 us
    ppermute x6, starting transfers between devices, swapped(): return lax.ppermute(value, AXES, [(i, i ^ bits) for i in range(devices)])  2.92 us
    all_to_all x1, starting transfers between devices, on_device(): got = lax.all_to_all(chunks.reshape(devices, 1, BLOCK), AXES, 0, 0)  2.57 us
    all_to_all x1, waiting for transfers between devices, on_device(): got = lax.all_to_all(chunks.reshape(devices, 1, BLOCK), AXES, 0, 0)  1.9 us
    pallas_call x1, Pallas kernels, on_device(): call(functools.partial(last_kernel, total, shift), [pltpu.VMEM((devices,...  1.86 us
  transfers between devices with their start and end apart: 8, of which 6 were waited for; matrix products, arithmetic and copies ran while one was open for 0% of the time, Pallas kernels for 4%

profile of v5, /device:TPU:0, one launch (start us, length us, event | category | flops | bytes accessed | tf_op | source)
XLA Modules:
  0.0 52.2 jit_solution(10837453513461931678)
XLA Ops:
  0.6 1.5 %start.1 = (f32[32,8,128]{2,1,0:T(8,128)}, s32[2,128]{1,0:T(2,128)S(1)}) custom-call(f32[8,256]{1,0:T(8,128)} %bitcast.14, s32[2,128]{1,0:T(2,128)} %bitcast.15), custom_call_target="tpu_custom_call" | custom-call | tf_op jit(solution)/shard_map/start/pallas_call | solution.py:362
  2.1 0.0 copy-start
  2.1 0.0 copy-start.1
  2.1 0.5 collective-permute-start.2
  2.6 7.0 %all-to-all-start = ((f32[32,8,128]{2,1,0:T(8,128)}), f32[32,8,128]{2,1,0:T(8,128)S(1)}, u32[]{:S(2)}, u32[]{:S(2)}) async-start(f32[32,8,128]{2,1,0:T(8,128)} %get-tuple-element.27), calls=%async_computation | async-start | bytes 262144 | tf_op jit(solution)/shard_map/all_to_all | solution.py:372
  9.6 0.0 copy-done
  9.6 0.3 collective-permute-start
  9.9 0.0 copy-done.1
  9.9 0.3 collective-permute-start.1
  10.2 0.6 %collective-permute-done.other_rows = s32[1,32]{1,0:T(1,128)S(1)} collective-permute-done((s32[1,32]{1,0:T(1,128)S(1)}, s32[1,32]{1,0:T(1,128)S(1)}, u32[]{:S(2)}, u32[]{:S(2)}) %collective-permute-start) | collective-permute-done | bytes 160 | tf_op jit(solution)/shard_map/ppermute | solution.py:357
  10.8 0.3 collective-permute-done.1.other_cols
  11.1 1.8 %prepare.1 = (bf16[32,128,128]{2,1,0:T(8,128)(2,1)S(1)}, bf16[512,128]{1,0:T(8,128)(2,1)S(1)}) custom-call(bf16[32,128,128]{2,1,0:T(8,128)(2,1)} %bitcast.13, s32[1,32]{1,0:T(1,128)S(1)} %copy-done, s32[1,32]{1,0:T(1,128)S(1)} %copy-done.1, s32[1,32]{1,0:T(1,128)S(1)} %collective-permute-done.other_rows, s32[1,32]{1,0:T(1,128)S(1)} %collective-permute-done.1.other_cols), custom_call_target="tpu_custom_call" | custom-call | tf_op jit(solution)/shard_map/prepare/pallas_call | solution.py:374
  12.9 4.9 %all-to-all-done.got_ref = f32[32,8,128]{2,1,0:T(8,128)S(1)} async-done(((f32[32,8,128]{2,1,0:T(8,128)}), f32[32,8,128]{2,1,0:T(8,128)S(1)}, u32[]{:S(2)}, u32[]{:S(2)}) %all-to-all-start) | async-done | bytes 131104 | tf_op jit(solution)/shard_map/all_to_all | solution.py:372
  17.8 0.0 collective-permute-done.2.other_ref
  17.8 1.0 %first.1 = (f32[16,2,8,128]{3,2,1,0:T(8,128)S(1)}, f32[32,8,128]{2,1,0:T(8,128)S(1)}, f32[8,128]{1,0:T(8,128)S(1)}) custom-call(f32[32,8,128]{2,1,0:T(8,128)S(1)} %all-to-all-done.got_ref, bf16[512,128]{1,0:T(8,128)(2,1)S(1)} %get-tuple-element.31.pick_ref, bf16[32,128,128]{2,1,0:T(8,128)(2,1)S(1)} %get-tuple-element.32.own_ref, ...), custom_call_target="tpu_custom_call" | custom-call | tf_op jit(solution)/shard_map/first/pallas_call | solution.py:383
  18.8 10.0 %all_to_all.20.got_ref = f32[16,2,8,128]{3,2,1,0:T(8,128)S(1)} all-to-all(f32[16,2,8,128]{3,2,1,0:T(8,128)S(1)} %get-tuple-element.33), channel_id=1, replica_groups={{2,4,6,8,10,12,14,16,18,20,22,24,26,28,30,0},{3,5,7,9,11,13,15,17,19,21..., dimensions={0} | all-to-all | bytes 262144 | tf_op jit(solution)/shard_map/all_to_all | solution.py:360
  28.8 1.2 %middle.1 = (f32[16,2,8,128]{3,2,1,0:T(8,128)S(1)}, f32[32,8,128]{2,1,0:T(8,128)S(1)}, f32[8,128]{1,0:T(8,128)S(1)}) custom-call(f32[16,2,8,128]{3,2,1,0:T(8,128)S(1)} %all_to_all.20.got_ref, f32[32,8,128]{2,1,0:T(8,128)S(1)} %get-tuple-element.34.basis_ref.zero_ref, f32[8,128]{1,0:T(8,128)S(1)} %get-tuple-element.35.known_ref, ...), custom_call_target="tpu_custom_call" | custom-call | tf_op jit(solution)/shard_map/middle/pallas_call | solution.py:387
  29.9 9.8 %all_to_all.21.got_ref = f32[16,2,8,128]{3,2,1,0:T(8,128)S(1)} all-to-all(f32[16,2,8,128]{3,2,1,0:T(8,128)S(1)} %get-tuple-element.36), channel_id=1, replica_groups={{2,4,6,8,10,12,14,16,18,20,22,24,26,28,30,0},{3,5,7,9,11,13,15,17,19,21..., dimensions={0} | all-to-all | bytes 262144 | tf_op jit(solution)/shard_map/all_to_all | solution.py:360
  39.7 1.9 %last.1 = (f32[32,128]{1,0:T(8,128)}, f32[32,8,128]{2,1,0:T(8,128)S(1)}, f32[8,128]{1,0:T(8,128)S(1)}, f32[8,128]{1,0:T(8,128)S(1)}, f32[8,128]{1,0:T(8,128)S(1)}) custom-call(f32[16,2,8,128]{3,2,1,0:T(8,128)S(1)} %all_to_all.21.got_ref, f32[32,8,128]{2,1,0:T(8,128)S(1)} %get-tuple-element.34.basis_ref.zero_ref, ...), custom_call_target="tpu_custom_call" | custom-call | tf_op jit(solution)/shard_map/last/pallas_call | solution.py:392
  41.6 0.0 collective-permute-start.3
  41.6 2.6 %all-to-all-start.3 = ((f32[32,1,128]{2,1,0:T(1,128)}), f32[32,1,128]{2,1,0:T(1,128)S(1)}, u32[]{:S(2)}, u32[]{:S(2)}) async-start(f32[32,1,128]{2,1,0:T(1,128)} %bitcast.4), calls=%async_computation.3 | async-start | bytes 32768 | tf_op jit(solution)/shard_map/all_to_all | solution.py:397
  44.2 1.8 %collective-permute-start.4 = (f32[8,128]{1,0:T(8,128)S(1)}, f32[8,128]{1,0:T(8,128)S(1)}, u32[]{:S(2)}, u32[]{:S(2)}) collective-permute-start(f32[8,128]{1,0:T(8,128)S(1)} %get-tuple-element.42.same_ref), channel_id=1, source_target_pairs={{0,16},{1,17},{2,18},{3,19},{4,20},{5,21},{6,22},{7,23},{8,24},{9,... | collective-permute-start | bytes 12296 | tf_op jit(solution)/shard_map/ppermute | solution.py:357
  46.0 0.0 collective-permute-start.5
  46.0 1.8 %collective-permute-done.4.across_ref = f32[8,128]{1,0:T(8,128)S(1)} collective-permute-done((f32[8,128]{1,0:T(8,128)S(1)}, f32[8,128]{1,0:T(8,128)S(1)}, u32[]{:S(2)}, u32[]{:S(2)}) %collective-permute-start.4) | collective-permute-done | bytes 4128 | tf_op jit(solution)/shard_map/ppermute | solution.py:357
  47.8 1.2 %collective-permute-done.5.flipped_ref = f32[8,128]{1,0:T(8,128)S(1)} collective-permute-done((f32[8,128]{1,0:T(8,128)S(1)}, f32[8,128]{1,0:T(8,128)S(1)}, u32[]{:S(2)}, u32[]{:S(2)}) %collective-permute-start.5) | collective-permute-done | bytes 4128 | tf_op jit(solution)/shard_map/ppermute | solution.py:357
  49.0 0.0 collective-permute-done.3.theirs_ref
  49.0 0.3 keep.1
  49.3 1.9 %all-to-all-done.3 = f32[32,1,128]{2,1,0:T(1,128)S(1)} async-done(((f32[32,1,128]{2,1,0:T(1,128)}), f32[32,1,128]{2,1,0:T(1,128)S(1)}, u32[]{:S(2)}, u32[]{:S(2)}) %all-to-all-start.3) | async-done | bytes 16416 | tf_op jit(solution)/shard_map/all_to_all | solution.py:397
  51.2 0.9 %final.1 = (f32[4,8,256]{2,1,0:T(8,128)}, f32[3,4,8]{2,1,0:T(4,128)}) custom-call(f32[32,128]{1,0:T(8,128)S(1)} %bitcast.11, f32[4,8,256]{2,1,0:T(8,128)S(1)} %get-tuple-element.45.kept_ref, f32[8,128]{1,0:T(8,128)S(1)} %get-tuple-element.46.known_ref, f32[8,128]{1,0:T(8,128)S(1)} %get-tuple-element.47.gram_ref), custom_call_target="tpu_custom_call" | custom-call | tf_op jit(solution)/shard_map/final/pallas_call | solution.py:407
  (1 shorter events, 0.0 us)
Async XLA Ops:
  2.1 7.5 %copy-start = (s32[1,32]{1,0:T(1,128)S(1)}, s32[1,32]{1,0:T(1,128)}, u32[]{:S(2)}) copy-start(s32[1,32]{1,0:T(1,128)} %own_rows) | copy-start | bytes 388
  2.1 7.8 %copy-start.1 = (s32[1,32]{1,0:T(1,128)S(1)}, s32[1,32]{1,0:T(1,128)}, u32[]{:S(2)}) copy-start(s32[1,32]{1,0:T(1,128)} %own_cols) | copy-start | bytes 388
  2.1 15.7 %collective-permute-start.2 = (bf16[32,128,128]{2,1,0:T(8,128)(2,1)}, bf16[32,128,128]{2,1,0:T(8,128)(2,1)S(1)}, u32[]{:S(2)}, u32[]{:S(2)}) collective-permute-start(bf16[32,128,128]{2,1,0:T(8,128)(2,1)} %bitcast.12), channel_id=1, source_target_pairs={{0,1},{1,0},{2,3},{3,2},{4,5},{5,4},{6,7},{7,6},{8,9},{9,8},{10,11... | collective-permute-start | bytes 3145736 | tf_op jit(solution)/shard_map/ppermute | solution.py:357
  2.6 15.1 %all-to-all-start = ((f32[32,8,128]{2,1,0:T(8,128)}), f32[32,8,128]{2,1,0:T(8,128)S(1)}, u32[]{:S(2)}, u32[]{:S(2)}) async-start(f32[32,8,128]{2,1,0:T(8,128)} %get-tuple-element.27), calls=%async_computation | async-start | bytes 262144 | tf_op jit(solution)/shard_map/all_to_all | solution.py:372
  9.6 1.2 %collective-permute-start = (s32[1,32]{1,0:T(1,128)S(1)}, s32[1,32]{1,0:T(1,128)S(1)}, u32[]{:S(2)}, u32[]{:S(2)}) collective-permute-start(s32[1,32]{1,0:T(1,128)S(1)} %copy-done), channel_id=1, source_target_pairs={{0,1},{1,0},{2,3},{3,2},{4,5},{5,4},{6,7},{7,6},{8,9},{9,8},{10,11... | collective-permute-start | bytes 392 | tf_op jit(solution)/shard_map/ppermute | solution.py:357
  9.9 1.1 %collective-permute-start.1 = (s32[1,32]{1,0:T(1,128)S(1)}, s32[1,32]{1,0:T(1,128)S(1)}, u32[]{:S(2)}, u32[]{:S(2)}) collective-permute-start(s32[1,32]{1,0:T(1,128)S(1)} %copy-done.1), channel_id=1, source_target_pairs={{0,1},{1,0},{2,3},{3,2},{4,5},{5,4},{6,7},{7,6},{8,9},{9,8},{10,11... | collective-permute-start | bytes 392 | tf_op jit(solution)/shard_map/ppermute | solution.py:357
  41.6 7.4 %collective-permute-start.3 = (f32[8,8,128]{2,1,0:T(8,128)S(1)}, f32[8,8,128]{2,1,0:T(8,128)S(1)}, u32[]{:S(2)}, u32[]{:S(2)}) collective-permute-start(f32[8,8,128]{2,1,0:T(8,128)S(1)} %pack.1), channel_id=1, source_target_pairs={{0,1},{1,0},{2,3},{3,2},{4,5},{5,4},{6,7},{7,6},{8,9},{9,8},{10,11... | collective-permute-start | bytes 98312 | tf_op jit(solution)/shard_map/ppermute | solution.py:357
  41.6 9.6 %all-to-all-start.3 = ((f32[32,1,128]{2,1,0:T(1,128)}), f32[32,1,128]{2,1,0:T(1,128)S(1)}, u32[]{:S(2)}, u32[]{:S(2)}) async-start(f32[32,1,128]{2,1,0:T(1,128)} %bitcast.4), calls=%async_computation.3 | async-start | bytes 32768 | tf_op jit(solution)/shard_map/all_to_all | solution.py:397
  44.2 3.7 %collective-permute-start.4 = (f32[8,128]{1,0:T(8,128)S(1)}, f32[8,128]{1,0:T(8,128)S(1)}, u32[]{:S(2)}, u32[]{:S(2)}) collective-permute-start(f32[8,128]{1,0:T(8,128)S(1)} %get-tuple-element.42.same_ref), channel_id=1, source_target_pairs={{0,16},{1,17},{2,18},{3,19},{4,20},{5,21},{6,22},{7,23},{8,24},{9,... | collective-permute-start | bytes 12296 | tf_op jit(solution)/shard_map/ppermute | solution.py:357
  46.0 3.0 %collective-permute-start.5 = (f32[8,128]{1,0:T(8,128)S(1)}, f32[8,128]{1,0:T(8,128)S(1)}, u32[]{:S(2)}, u32[]{:S(2)}) collective-permute-start(f32[8,128]{1,0:T(8,128)S(1)} %get-tuple-element.43.flip_ref), channel_id=1, source_target_pairs={{0,17},{1,16},{2,19},{3,18},{4,21},{5,20},{6,23},{7,22},{8,25},{9,... | collective-permute-start | bytes 12296 | tf_op jit(solution)/shard_map/ppermute | solution.py:357

commit v6 on v5

--- a/solution.py
+++ b/solution.py
@@ -107,19 +107,23 @@
     copy.wait()
 
 
-def image(vector_ref, pick_ref, own_ref, other_ref):
-    side, owner, core = position()
-    owners = vector_ref.shape[0] // 2
-    half = vector_ref[pl.ds(side * owners, owners)]
-    rounded = half.reshape(owners * ROWS, BLOCK).astype(jnp.bfloat16)
+def near(half, pick_ref, own_ref, other_ref):
+    flat = half.reshape(-1, BLOCK)
+    coarse = flat.astype(jnp.bfloat16)
+    fine = (flat - coarse.astype(jnp.float32)).astype(jnp.bfloat16)
     picked = lax.dot_general(
-        pick_ref[...], rounded, (((1,), (0,)), ((), ())), preferred_element_type=jnp.float32
+        pick_ref[...], jnp.concatenate([coarse, fine], axis=1), (((1,), (0,)), ((), ())),
+        preferred_element_type=jnp.float32,
     ).astype(jnp.bfloat16)
-    sums = [jnp.zeros((2 * ROWS, 2 * BLOCK), jnp.float32) for _ in range(2)]
+    sums = [jnp.zeros((4 * ROWS, 2 * BLOCK), jnp.float32) for _ in range(2)]
     for entry in range(0, own_ref.shape[0], 2):
-        first = 2 * ROWS * entry
+        rows = [slice(2 * ROWS * place, 2 * ROWS * (place + 1)) for place in (entry, entry + 1)]
         left = jnp.concatenate(
-            [picked[first : first + 2 * ROWS], picked[first + 2 * ROWS : first + 4 * ROWS]], axis=1
+            [
+                jnp.concatenate([picked[rows[0], part], picked[rows[1], part]], axis=1)
+                for part in (slice(0, BLOCK), slice(BLOCK, 2 * BLOCK))
+            ],
+            axis=0,
         )
         right = jnp.concatenate(
             [jnp.concatenate([ref[entry], ref[entry + 1]], axis=1) for ref in (own_ref, other_ref)],
@@ -129,12 +133,11 @@
             left, right, (((1,), (1,)), ((), ())), preferred_element_type=jnp.float32
         )
     total = sums[0] + sums[1]
+    total = total[: 2 * ROWS] + total[2 * ROWS :]
+    _, _, core = position()
     own = total[:ROWS, :BLOCK]
     other = total[ROWS:, BLOCK:]
-    base = side * owners + owner - core
-    low = jnp.where(core == 0, own, other) + 0.5 * vector_ref[base]
-    high = jnp.where(core == 0, other, own) + 0.5 * vector_ref[base + 1]
-    return low, high
+    return jnp.where(core == 0, own, other), jnp.where(core == 0, other, own)
 
 
 def spread(chunk_ref, low, high):
@@ -149,45 +152,78 @@
 
 
 def first_kernel(total, got_ref, pick_ref, own_ref, other_ref, chunk_ref, basis_ref, coeff_ref):
+    side, owner, core = position()
     owners = got_ref.shape[0] // 2
+    base = owner - core
     port = got_ref[:owners]
     star = got_ref[owners:]
-    squares = per_rhs(jnp.sum(port * port + star * star, axis=0))
-    squares = squares * (1.0 / total) + EPSILON
+    sym = port + star
+    anti = port - star
+    tiles = near(jnp.where(side == 0, sym, anti), pick_ref, own_ref, other_ref)
+    squares = per_rhs(jnp.sum(port * port + star * star, axis=0)) * (1.0 / total) + EPSILON
     scale = lax.rsqrt(squares)
     coeff_ref[...] = columns({LENGTH_LANE: jnp.sqrt(squares)})
-    basis_ref[:owners] = (port + star) * scale
-    basis_ref[owners:] = (port - star) * scale
-    spread(chunk_ref, *image(basis_ref, pick_ref, own_ref, other_ref))
-
-
-def orthogonalized(total, shift, got_ref, basis_refs):
+    basis_ref[:owners] = sym * scale
+    basis_ref[owners:] = anti * scale
+    images = []
+    for place, tile in enumerate(tiles):
+        here, there = got_ref[base + place], got_ref[owners + base + place]
+        images.append((tile + 0.5 * jnp.where(side == 0, here + there, here - there)) * scale)
+    spread(chunk_ref, *images)
+
+
+def in_order(got_ref, shift):
+    chips = got_ref.shape[0]
+    return jnp.concatenate([got_ref[chips - shift :], got_ref[: chips - shift]], axis=0)
+
+
+def own_tiles(got_ref, shift):
+    side, owner, _ = position()
+    chips = got_ref.shape[0]
+    chip = lax.rem(side * (chips // 2) + owner // 2 + chips - shift, chips)
+    return got_ref[chip, 0], got_ref[chip, 1]
+
+
+def advanced(total, shift, got_refs, basis_refs, pick_ref, own_ref, other_ref):
+    side, _, _ = position()
+    got = in_order(got_refs[-1], shift)
+    half = got.shape[0] // 2
+    tiles = near(jnp.where(side == 0, got[:half], got[half:]), pick_ref, own_ref, other_ref)
+    got = got.reshape(basis_refs[0].shape)
     inner = 0.5 / total
-    chips = got_ref.shape[0]
-    got = jnp.concatenate([got_ref[chips - shift :], got_ref[: chips - shift]], axis=0)
-    got = got.reshape(basis_refs[0].shape)
     coeffs = [dot(got, ref[...]) * inner for ref in basis_refs]
     rest = got
     for coeff, ref in zip(coeffs, basis_refs):
         rest = rest - coeff * ref[...]
     squares = dot(rest, rest) * inner + EPSILON
-    return coeffs + [jnp.sqrt(squares)], rest * lax.rsqrt(squares)
+    scale = lax.rsqrt(squares)
+    owned = [own_tiles(ref, shift) for ref in got_refs]
+    images = []
+    for place, tile in enumerate(tiles):
+        value = tile + 0.5 * owned[-1][place]
+        for coeff, earlier in zip(coeffs, owned):
+            value = value - coeff * earlier[place]
+        images.append(value * scale)
+    return coeffs + [jnp.sqrt(squares)], rest * scale, images
 
 
 def middle_kernel(total, shift, got_ref, basis_ref, known_ref, pick_ref, own_ref, other_ref,
                   chunk_ref, next_ref, coeff_ref):
-    coeffs, next_ref[...] = orthogonalized(total, shift, got_ref, [basis_ref])
+    coeffs, next_ref[...], images = advanced(
+        total, shift, [got_ref], [basis_ref], pick_ref, own_ref, other_ref
+    )
     coeff_ref[...] = columns(dict(enumerate(coeffs))) + known_ref[...]
-    spread(chunk_ref, *image(next_ref, pick_ref, own_ref, other_ref))
-
-
-def last_kernel(total, shift, got_ref, zero_ref, one_ref, known_ref, pick_ref, own_ref, other_ref,
-                chunk_ref, two_ref, coeff_ref, same_ref, flip_ref):
+    spread(chunk_ref, *images)
+
+
+def last_kernel(total, shift, first_got_ref, got_ref, zero_ref, one_ref, known_ref, pick_ref,
+                own_ref, other_ref, chunk_ref, two_ref, coeff_ref, same_ref, flip_ref):
     side, owner, core = position()
     owners = two_ref.shape[0] // 2
     refs = [zero_ref, one_ref, two_ref]
-    coeffs, two_ref[...] = orthogonalized(total, shift, got_ref, refs[:2])
-    tiles = image(two_ref, pick_ref, own_ref, other_ref)
+    coeffs, two_ref[...], tiles = advanced(
+        total, shift, [first_got_ref, got_ref], refs[:2], pick_ref, own_ref, other_ref
+    )
     base = side * owners + owner - core
     rhs = iota((ROWS, BLOCK), 0)
     lane = iota((ROWS, BLOCK), 1)
@@ -379,21 +415,21 @@
         ],
         [HBM] + [SMEM] * 4, [pltpu.SemaphoreType.DMA], name="prepare",
     )(in_hbm(blocks), block_rows, block_cols, swapped(block_rows, 1), swapped(block_cols, 1))
-    near = (pick, own_blocks, other_blocks)
+    near_args = (pick, own_blocks, other_blocks)
     chunks, zero, coeff = call(
         functools.partial(first_kernel, total), [chunk, vector, tile], [VMEM] * 4, name="first"
-    )(got, *near)
+    )(got, *near_args)
     got = exchanged(chunks)
     chunks, one, coeff = call(
         functools.partial(middle_kernel, total, shift), [chunk, vector, tile], [VMEM] * 6,
         name="middle",
-    )(got, zero, coeff, *near)
-    got = exchanged(chunks)
+    )(got, zero, coeff, *near_args)
+    first_got, got = got, exchanged(chunks)
     chunks, two, coeff, same, flip = call(
         functools.partial(last_kernel, total, shift),
-        [pltpu.VMEM((devices, BLOCK), jnp.float32), vector, tile, tile, tile], [VMEM] * 7,
+        [pltpu.VMEM((devices, BLOCK), jnp.float32), vector, tile, tile, tile], [VMEM] * 8,
         name="last",
-    )(got, zero, one, coeff, *near)
+    )(first_got, got, zero, one, coeff, *near_args)
     got = lax.all_to_all(chunks.reshape(devices, 1, BLOCK), AXES, 0, 0)
     [theirs] = call(
         pack_kernel, [shaped(2 * ITERS + 2, ROWS, BLOCK)], [VMEM] * 5, name="pack"

time: 52.5 us -> 51.9 us (0.989)
  Pallas kernels: 8.48 us -> 7.85 us
where the time goes in v6:
time: 51.9 us; the launch traced here: 51.5 us
  blocking collectives  19.8 us (38%)
  starting transfers between devices  12.4 us (24%)
  waiting for transfers between devices  10.7 us (21%)
  Pallas kernels  7.85 us (15%)
  between operations  0.71 us (1%)
    all_to_all x2, blocking collectives, exchanged(): return lax.all_to_all(chunks, AXES, 0, 0, axis_index_groups=same_core)  19.8 us
    all_to_all x1, starting transfers between devices, on_device(): got = lax.all_to_all(chunks, AXES, 0, 0)  6.96 us
    all_to_all x1, waiting for transfers between devices, on_device(): got = lax.all_to_all(chunks, AXES, 0, 0)  4.92 us
    ppermute x6, waiting for transfers between devices, swapped(): return lax.ppermute(value, AXES, [(i, i ^ bits) for i in range(devices)])  3.9 us
    ppermute x6, starting transfers between devices, swapped(): return lax.ppermute(value, AXES, [(i, i ^ bits) for i in range(devices)])  2.92 us
    all_to_all x1, starting transfers between devices, on_device(): got = lax.all_to_all(chunks.reshape(devices, 1, BLOCK), AXES, 0, 0)  2.57 us
    all_to_all x1, waiting for transfers between devices, on_device(): got = lax.all_to_all(chunks.reshape(devices, 1, BLOCK), AXES, 0, 0)  1.9 us
    pallas_call x1, Pallas kernels, on_device(): call(prepare_kernel, [shaped(*blocks.shape, dtype=blocks.dtype), shaped(2...  1.79 us
  transfers between devices with their start and end apart: 8, of which 6 were waited for; matrix products, arithmetic and copies ran while one was open for 0% of the time, Pallas kernels for 4%

profile of v6, /device:TPU:0, one launch (start us, length us, event | category | flops | bytes accessed | tf_op | source)
XLA Modules:
  0.0 51.5 jit_solution(10704634053715145438)
XLA Ops:
  0.6 1.5 %start.1 = (f32[32,8,128]{2,1,0:T(8,128)}, s32[2,128]{1,0:T(2,128)S(1)}) custom-call(f32[8,256]{1,0:T(8,128)} %bitcast.14, s32[2,128]{1,0:T(2,128)} %bitcast.15), custom_call_target="tpu_custom_call" | custom-call | tf_op jit(solution)/shard_map/start/pallas_call | solution.py:398
  2.1 0.0 copy-start
  2.1 0.0 copy-start.1
  2.1 0.5 %collective-permute-start.2 = (bf16[32,128,128]{2,1,0:T(8,128)(2,1)}, bf16[32,128,128]{2,1,0:T(8,128)(2,1)S(1)}, u32[]{:S(2)}, u32[]{:S(2)}) collective-permute-start(bf16[32,128,128]{2,1,0:T(8,128)(2,1)} %bitcast.12), channel_id=1, source_target_pairs={{0,1},{1,0},{2,3},{3,2},{4,5},{5,4},{6,7},{7,6},{8,9},{9,8},{10,11... | collective-permute-start | bytes 3145736 | tf_op jit(solution)/shard_map/ppermute | solution.py:393
  2.6 7.0 %all-to-all-start = ((f32[32,8,128]{2,1,0:T(8,128)}), f32[32,8,128]{2,1,0:T(8,128)S(1)}, u32[]{:S(2)}, u32[]{:S(2)}) async-start(f32[32,8,128]{2,1,0:T(8,128)} %get-tuple-element.27), calls=%async_computation | async-start | bytes 262144 | tf_op jit(solution)/shard_map/all_to_all | solution.py:408
  9.6 0.0 copy-done
  9.6 0.3 collective-permute-start
  9.9 0.0 copy-done.1
  9.9 0.3 collective-permute-start.1
  10.2 0.6 %collective-permute-done.other_rows = s32[1,32]{1,0:T(1,128)S(1)} collective-permute-done((s32[1,32]{1,0:T(1,128)S(1)}, s32[1,32]{1,0:T(1,128)S(1)}, u32[]{:S(2)}, u32[]{:S(2)}) %collective-permute-start) | collective-permute-done | bytes 160 | tf_op jit(solution)/shard_map/ppermute | solution.py:393
  10.8 0.3 collective-permute-done.1.other_cols
  11.1 1.8 %prepare.1 = (bf16[32,128,128]{2,1,0:T(8,128)(2,1)S(1)}, bf16[512,128]{1,0:T(8,128)(2,1)S(1)}) custom-call(bf16[32,128,128]{2,1,0:T(8,128)(2,1)} %bitcast.13, s32[1,32]{1,0:T(1,128)S(1)} %copy-done, s32[1,32]{1,0:T(1,128)S(1)} %copy-done.1, s32[1,32]{1,0:T(1,128)S(1)} %collective-permute-done.other_rows, s32[1,32]{1,0:T(1,128)S(1)} %collective-permute-done.1.other_cols), custom_call_target="tpu_custom_call" | custom-call | tf_op jit(solution)/shard_map/prepare/pallas_call | solution.py:410
  12.9 4.9 %all-to-all-done.got_ref = f32[32,8,128]{2,1,0:T(8,128)S(1)} async-done(((f32[32,8,128]{2,1,0:T(8,128)}), f32[32,8,128]{2,1,0:T(8,128)S(1)}, u32[]{:S(2)}, u32[]{:S(2)}) %all-to-all-start) | async-done | bytes 131104 | tf_op jit(solution)/shard_map/all_to_all | solution.py:408
  17.8 0.0 collective-permute-done.2.other_ref
  17.8 0.9 %first.1 = (f32[16,2,8,128]{3,2,1,0:T(8,128)S(1)}, f32[32,8,128]{2,1,0:T(8,128)S(1)}, f32[8,128]{1,0:T(8,128)S(1)}) custom-call(f32[32,8,128]{2,1,0:T(8,128)S(1)} %all-to-all-done.got_ref, bf16[512,128]{1,0:T(8,128)(2,1)S(1)} %get-tuple-element.31.pick_ref, bf16[32,128,128]{2,1,0:T(8,128)(2,1)S(1)} %get-tuple-element.32.own_ref, ...), custom_call_target="tpu_custom_call" | custom-call | tf_op jit(solution)/shard_map/first/pallas_call | solution.py:419
  18.7 10.0 %all_to_all.20.got_ref.first_got_ref = f32[16,2,8,128]{3,2,1,0:T(8,128)S(1)} all-to-all(f32[16,2,8,128]{3,2,1,0:T(8,128)S(1)} %get-tuple-element.33), channel_id=1, replica_groups={{2,4,6,8,10,12,14,16,18,20,22,24,26,28,30,0},{3,5,7,9,11,13,15,17,19,21..., dimensions={0} | all-to-all | bytes 262144 | tf_op jit(solution)/shard_map/all_to_all | solution.py:396
  28.7 0.9 %middle.1 = (f32[16,2,8,128]{3,2,1,0:T(8,128)S(1)}, f32[32,8,128]{2,1,0:T(8,128)S(1)}, f32[8,128]{1,0:T(8,128)S(1)}) custom-call(f32[16,2,8,128]{3,2,1,0:T(8,128)S(1)} %all_to_all.20.got_ref.first_got_ref, f32[32,8,128]{2,1,0:T(8,128)S(1)} %get-tuple-element.34.basis_ref.zero_ref, f32[8,128]{1,0:T(8,128)S(1)} %get-tuple-element.35.known_ref, ...), custom_call_target="tpu_custom_call" | custom-call | tf_op jit(solution)/shard_map/middle/pallas_call | solution.py:423
  29.6 9.8 %all_to_all.21.got_ref = f32[16,2,8,128]{3,2,1,0:T(8,128)S(1)} all-to-all(f32[16,2,8,128]{3,2,1,0:T(8,128)S(1)} %get-tuple-element.36), channel_id=1, replica_groups={{2,4,6,8,10,12,14,16,18,20,22,24,26,28,30,0},{3,5,7,9,11,13,15,17,19,21..., dimensions={0} | all-to-all | bytes 262144 | tf_op jit(solution)/shard_map/all_to_all | solution.py:396
  39.4 1.6 %last.1 = (f32[32,128]{1,0:T(8,128)}, f32[32,8,128]{2,1,0:T(8,128)S(1)}, f32[8,128]{1,0:T(8,128)S(1)}, f32[8,128]{1,0:T(8,128)S(1)}, f32[8,128]{1,0:T(8,128)S(1)}) custom-call(f32[16,2,8,128]{3,2,1,0:T(8,128)S(1)} %all_to_all.20.got_ref.first_got_ref, f32[16,2,8,128]{3,2,1,0:T(8,128)S(1)} %all_to_all.21.got_ref, ...), custom_call_target="tpu_custom_call" | custom-call | tf_op jit(solution)/shard_map/last/pallas_call | solution.py:428
  41.0 0.0 collective-permute-start.3
  41.0 2.6 %all-to-all-start.3 = ((f32[32,1,128]{2,1,0:T(1,128)}), f32[32,1,128]{2,1,0:T(1,128)S(1)}, u32[]{:S(2)}, u32[]{:S(2)}) async-start(f32[32,1,128]{2,1,0:T(1,128)} %bitcast.4), calls=%async_computation.3 | async-start | bytes 32768 | tf_op jit(solution)/shard_map/all_to_all | solution.py:433
  43.5 1.8 %collective-permute-start.4 = (f32[8,128]{1,0:T(8,128)S(1)}, f32[8,128]{1,0:T(8,128)S(1)}, u32[]{:S(2)}, u32[]{:S(2)}) collective-permute-start(f32[8,128]{1,0:T(8,128)S(1)} %get-tuple-element.42.same_ref), channel_id=1, source_target_pairs={{0,16},{1,17},{2,18},{3,19},{4,20},{5,21},{6,22},{7,23},{8,24},{9,... | collective-permute-start | bytes 12296 | tf_op jit(solution)/shard_map/ppermute | solution.py:393
  45.4 0.0 collective-permute-start.5
  45.4 1.8 %collective-permute-done.4.across_ref = f32[8,128]{1,0:T(8,128)S(1)} collective-permute-done((f32[8,128]{1,0:T(8,128)S(1)}, f32[8,128]{1,0:T(8,128)S(1)}, u32[]{:S(2)}, u32[]{:S(2)}) %collective-permute-start.4) | collective-permute-done | bytes 4128 | tf_op jit(solution)/shard_map/ppermute | solution.py:393
  47.2 1.2 %collective-permute-done.5.flipped_ref = f32[8,128]{1,0:T(8,128)S(1)} collective-permute-done((f32[8,128]{1,0:T(8,128)S(1)}, f32[8,128]{1,0:T(8,128)S(1)}, u32[]{:S(2)}, u32[]{:S(2)}) %collective-permute-start.5) | collective-permute-done | bytes 4128 | tf_op jit(solution)/shard_map/ppermute | solution.py:393
  48.4 0.0 collective-permute-done.3.theirs_ref
  48.4 0.3 keep.1
  48.7 1.9 %all-to-all-done.3 = f32[32,1,128]{2,1,0:T(1,128)S(1)} async-done(((f32[32,1,128]{2,1,0:T(1,128)}), f32[32,1,128]{2,1,0:T(1,128)S(1)}, u32[]{:S(2)}, u32[]{:S(2)}) %all-to-all-start.3) | async-done | bytes 16416 | tf_op jit(solution)/shard_map/all_to_all | solution.py:433
  50.6 0.9 %final.1 = (f32[4,8,256]{2,1,0:T(8,128)}, f32[3,4,8]{2,1,0:T(4,128)}) custom-call(f32[32,128]{1,0:T(8,128)S(1)} %bitcast.11, f32[4,8,256]{2,1,0:T(8,128)S(1)} %get-tuple-element.45.kept_ref, f32[8,128]{1,0:T(8,128)S(1)} %get-tuple-element.46.known_ref, f32[8,128]{1,0:T(8,128)S(1)} %get-tuple-element.47.gram_ref), custom_call_target="tpu_custom_call" | custom-call | tf_op jit(solution)/shard_map/final/pallas_call | solution.py:443
  (1 shorter events, 0.0 us)
Async XLA Ops:
  2.1 7.5 %copy-start = (s32[1,32]{1,0:T(1,128)S(1)}, s32[1,32]{1,0:T(1,128)}, u32[]{:S(2)}) copy-start(s32[1,32]{1,0:T(1,128)} %own_rows) | copy-start | bytes 388
  2.1 7.8 %copy-start.1 = (s32[1,32]{1,0:T(1,128)S(1)}, s32[1,32]{1,0:T(1,128)}, u32[]{:S(2)}) copy-start(s32[1,32]{1,0:T(1,128)} %own_cols) | copy-start | bytes 388
  2.1 15.7 %collective-permute-start.2 = (bf16[32,128,128]{2,1,0:T(8,128)(2,1)}, bf16[32,128,128]{2,1,0:T(8,128)(2,1)S(1)}, u32[]{:S(2)}, u32[]{:S(2)}) collective-permute-start(bf16[32,128,128]{2,1,0:T(8,128)(2,1)} %bitcast.12), channel_id=1, source_target_pairs={{0,1},{1,0},{2,3},{3,2},{4,5},{5,4},{6,7},{7,6},{8,9},{9,8},{10,11... | collective-permute-start | bytes 3145736 | tf_op jit(solution)/shard_map/ppermute | solution.py:393
  2.6 15.1 %all-to-all-start = ((f32[32,8,128]{2,1,0:T(8,128)}), f32[32,8,128]{2,1,0:T(8,128)S(1)}, u32[]{:S(2)}, u32[]{:S(2)}) async-start(f32[32,8,128]{2,1,0:T(8,128)} %get-tuple-element.27), calls=%async_computation | async-start | bytes 262144 | tf_op jit(solution)/shard_map/all_to_all | solution.py:408
  9.6 1.2 %collective-permute-start = (s32[1,32]{1,0:T(1,128)S(1)}, s32[1,32]{1,0:T(1,128)S(1)}, u32[]{:S(2)}, u32[]{:S(2)}) collective-permute-start(s32[1,32]{1,0:T(1,128)S(1)} %copy-done), channel_id=1, source_target_pairs={{0,1},{1,0},{2,3},{3,2},{4,5},{5,4},{6,7},{7,6},{8,9},{9,8},{10,11... | collective-permute-start | bytes 392 | tf_op jit(solution)/shard_map/ppermute | solution.py:393
  9.9 1.1 %collective-permute-start.1 = (s32[1,32]{1,0:T(1,128)S(1)}, s32[1,32]{1,0:T(1,128)S(1)}, u32[]{:S(2)}, u32[]{:S(2)}) collective-permute-start(s32[1,32]{1,0:T(1,128)S(1)} %copy-done.1), channel_id=1, source_target_pairs={{0,1},{1,0},{2,3},{3,2},{4,5},{5,4},{6,7},{7,6},{8,9},{9,8},{10,11... | collective-permute-start | bytes 392 | tf_op jit(solution)/shard_map/ppermute | solution.py:393
  41.0 7.4 %collective-permute-start.3 = (f32[8,8,128]{2,1,0:T(8,128)S(1)}, f32[8,8,128]{2,1,0:T(8,128)S(1)}, u32[]{:S(2)}, u32[]{:S(2)}) collective-permute-start(f32[8,8,128]{2,1,0:T(8,128)S(1)} %pack.1), channel_id=1, source_target_pairs={{0,1},{1,0},{2,3},{3,2},{4,5},{5,4},{6,7},{7,6},{8,9},{9,8},{10,11... | collective-permute-start | bytes 98312 | tf_op jit(solution)/shard_map/ppermute | solution.py:393
  41.0 9.6 %all-to-all-start.3 = ((f32[32,1,128]{2,1,0:T(1,128)}), f32[32,1,128]{2,1,0:T(1,128)S(1)}, u32[]{:S(2)}, u32[]{:S(2)}) async-start(f32[32,1,128]{2,1,0:T(1,128)} %bitcast.4), calls=%async_computation.3 | async-start | bytes 32768 | tf_op jit(solution)/shard_map/all_to_all | solution.py:433
  43.5 3.7 %collective-permute-start.4 = (f32[8,128]{1,0:T(8,128)S(1)}, f32[8,128]{1,0:T(8,128)S(1)}, u32[]{:S(2)}, u32[]{:S(2)}) collective-permute-start(f32[8,128]{1,0:T(8,128)S(1)} %get-tuple-element.42.same_ref), channel_id=1, source_target_pairs={{0,16},{1,17},{2,18},{3,19},{4,20},{5,21},{6,22},{7,23},{8,24},{9,... | collective-permute-start | bytes 12296 | tf_op jit(solution)/shard_map/ppermute | solution.py:393
  45.4 3.0 %collective-permute-start.5 = (f32[8,128]{1,0:T(8,128)S(1)}, f32[8,128]{1,0:T(8,128)S(1)}, u32[]{:S(2)}, u32[]{:S(2)}) collective-permute-start(f32[8,128]{1,0:T(8,128)S(1)} %get-tuple-element.43.flip_ref), channel_id=1, source_target_pairs={{0,17},{1,16},{2,19},{3,18},{4,21},{5,20},{6,23},{7,22},{8,25},{9,... | collective-permute-start | bytes 12296 | tf_op jit(solution)/shard_map/ppermute | solution.py:393

commit v7 on v6

--- a/solution.py
+++ b/solution.py
@@ -57,10 +57,13 @@
     )
 
 
-def start_kernel(sources_hbm, mirror_hbm, chunk_ref, mirror_ref, sources_ref, sems):
+def start_kernel(sources_hbm, mirror_hbm, rows_hbm, cols_hbm, chunk_ref, mirror_ref, places_ref,
+                 sources_ref, sems):
     copies = [
         pltpu.make_async_copy(sources_hbm, sources_ref, sems.at[0]),
         pltpu.make_async_copy(mirror_hbm, mirror_ref, sems.at[1]),
+        pltpu.make_async_copy(rows_hbm, places_ref.at[0], sems.at[2]),
+        pltpu.make_async_copy(cols_hbm, places_ref.at[1], sems.at[3]),
     ]
     for copy in copies:
         copy.start()
@@ -87,27 +90,34 @@
     lax.fori_loop(0, chips, store, 0, unroll=chips <= 32)
 
 
-def prepare_kernel(blocks_hbm, own_rows, own_cols, other_rows, other_cols, blocks_ref, pick_ref,
+def prepare_kernel(own_hbm, other_ref, own_places, other_places, weights_ref, pick_ref, own_ref,
                    sem):
-    copy = pltpu.make_async_copy(blocks_hbm, blocks_ref, sem)
+    copy = pltpu.make_async_copy(own_hbm, own_ref, sem)
     copy.start()
     width = pick_ref.shape[1]
     half_of_row = iota((ROWS, width), 0) // HALF_RHS
     rhs_of_row = iota((ROWS, width), 0) % HALF_RHS
     lane = iota((ROWS, width), 1)
-    for entry in range(blocks_ref.shape[0]):
+    for entry in range(own_ref.shape[0]):
         picks = []
-        for rows, cols in ((own_rows, own_cols), (other_rows, other_cols)):
+        for places in (own_places, other_places):
             place = jnp.where(
-                half_of_row == rows[0, entry], HALF_RHS * cols[0, entry] + rhs_of_row, -1
+                half_of_row == places[0, 0, entry], HALF_RHS * places[1, 0, entry] + rhs_of_row, -1
             )
             picks.append((lane == place).astype(jnp.float32))
         first = 2 * ROWS * entry
         pick_ref[first : first + 2 * ROWS, :] = jnp.concatenate(picks, axis=0).astype(jnp.bfloat16)
-    copy.wait()
-
-
-def near(half, pick_ref, own_ref, other_ref):
+    for side, ref in ((1, other_ref), (0, own_ref)):
+        if side == 0:
+            copy.wait()
+        for entry in range(own_ref.shape[0]):
+            first = entry % 2 * BLOCK
+            weights_ref[
+                entry // 2, first : first + BLOCK, side * BLOCK : (side + 1) * BLOCK
+            ] = ref[entry].T
+
+
+def near(half, pick_ref, weights_ref):
     flat = half.reshape(-1, BLOCK)
     coarse = flat.astype(jnp.bfloat16)
     fine = (flat - coarse.astype(jnp.float32)).astype(jnp.bfloat16)
@@ -116,8 +126,10 @@
         preferred_element_type=jnp.float32,
     ).astype(jnp.bfloat16)
     sums = [jnp.zeros((4 * ROWS, 2 * BLOCK), jnp.float32) for _ in range(2)]
-    for entry in range(0, own_ref.shape[0], 2):
-        rows = [slice(2 * ROWS * place, 2 * ROWS * (place + 1)) for place in (entry, entry + 1)]
+    for group in range(weights_ref.shape[0]):
+        rows = [
+            slice(2 * ROWS * place, 2 * ROWS * (place + 1)) for place in (2 * group, 2 * group + 1)
+        ]
         left = jnp.concatenate(
             [
                 jnp.concatenate([picked[rows[0], part], picked[rows[1], part]], axis=1)
@@ -125,12 +137,8 @@
             ],
             axis=0,
         )
-        right = jnp.concatenate(
-            [jnp.concatenate([ref[entry], ref[entry + 1]], axis=1) for ref in (own_ref, other_ref)],
-            axis=0,
-        )
-        sums[entry // 2 % 2] += lax.dot_general(
-            left, right, (((1,), (1,)), ((), ())), preferred_element_type=jnp.float32
+        sums[group % 2] += lax.dot_general(
+            left, weights_ref[group], (((1,), (0,)), ((), ())), preferred_element_type=jnp.float32
         )
     total = sums[0] + sums[1]
     total = total[: 2 * ROWS] + total[2 * ROWS :]
@@ -151,7 +159,7 @@
     lax.fori_loop(0, chips, store, 0, unroll=chips <= 32)
 
 
-def first_kernel(total, got_ref, pick_ref, own_ref, other_ref, chunk_ref, basis_ref, coeff_ref):
+def first_kernel(total, got_ref, pick_ref, weights_ref, chunk_ref, basis_ref, coeff_ref):
     side, owner, core = position()
     owners = got_ref.shape[0] // 2
     base = owner - core
@@ -159,7 +167,7 @@
     star = got_ref[owners:]
     sym = port + star
     anti = port - star
-    tiles = near(jnp.where(side == 0, sym, anti), pick_ref, own_ref, other_ref)
+    tiles = near(jnp.where(side == 0, sym, anti), pick_ref, weights_ref)
     squares = per_rhs(jnp.sum(port * port + star * star, axis=0)) * (1.0 / total) + EPSILON
     scale = lax.rsqrt(squares)
     coeff_ref[...] = columns({LENGTH_LANE: jnp.sqrt(squares)})
@@ -184,11 +192,11 @@
     return got_ref[chip, 0], got_ref[chip, 1]
 
 
-def advanced(total, shift, got_refs, basis_refs, pick_ref, own_ref, other_ref):
+def advanced(total, shift, got_refs, basis_refs, pick_ref, weights_ref):
     side, _, _ = position()
     got = in_order(got_refs[-1], shift)
     half = got.shape[0] // 2
-    tiles = near(jnp.where(side == 0, got[:half], got[half:]), pick_ref, own_ref, other_ref)
+    tiles = near(jnp.where(side == 0, got[:half], got[half:]), pick_ref, weights_ref)
     got = got.reshape(basis_refs[0].shape)
     inner = 0.5 / total
     coeffs = [dot(got, ref[...]) * inner for ref in basis_refs]
@@ -207,22 +215,22 @@
     return coeffs + [jnp.sqrt(squares)], rest * scale, images
 
 
-def middle_kernel(total, shift, got_ref, basis_ref, known_ref, pick_ref, own_ref, other_ref,
+def middle_kernel(total, shift, got_ref, basis_ref, known_ref, pick_ref, weights_ref,
                   chunk_ref, next_ref, coeff_ref):
     coeffs, next_ref[...], images = advanced(
-        total, shift, [got_ref], [basis_ref], pick_ref, own_ref, other_ref
+        total, shift, [got_ref], [basis_ref], pick_ref, weights_ref
     )
     coeff_ref[...] = columns(dict(enumerate(coeffs))) + known_ref[...]
     spread(chunk_ref, *images)
 
 
 def last_kernel(total, shift, first_got_ref, got_ref, zero_ref, one_ref, known_ref, pick_ref,
-                own_ref, other_ref, chunk_ref, two_ref, coeff_ref, same_ref, flip_ref):
+                weights_ref, chunk_ref, two_ref, coeff_ref, same_ref, flip_ref):
     side, owner, core = position()
     owners = two_ref.shape[0] // 2
     refs = [zero_ref, one_ref, two_ref]
     coeffs, two_ref[...], tiles = advanced(
-        total, shift, [first_got_ref, got_ref], refs[:2], pick_ref, own_ref, other_ref
+        total, shift, [first_got_ref, got_ref], refs[:2], pick_ref, weights_ref
     )
     base = side * owners + owner - core
     rhs = iota((ROWS, BLOCK), 0)
@@ -395,39 +403,43 @@
     def exchanged(chunks):
         return lax.all_to_all(chunks, AXES, 0, 0, axis_index_groups=same_core)
 
-    chunks, mirror_rows = call(
+    chunks, mirror_rows, places = call(
         start_kernel,
-        [pltpu.VMEM(vector.shape, jnp.float32), shaped(*mirror_rows.shape, dtype=jnp.int32)],
-        [HBM, HBM],
-        [pltpu.VMEM(sources.shape[1:], jnp.float32), pltpu.SemaphoreType.DMA((2,))],
+        [
+            vector,
+            shaped(*mirror_rows.shape, dtype=jnp.int32),
+            shaped(2, *block_rows.shape, dtype=jnp.int32),
+        ],
+        [HBM] * 4,
+        [pltpu.VMEM(sources.shape[1:], jnp.float32), pltpu.SemaphoreType.DMA((4,))],
         name="start",
-    )(in_hbm(sources[0]), in_hbm(mirror_rows))
-    chunks, blocks, block_rows, block_cols = lax.optimization_barrier(
-        (chunks, blocks, block_rows, block_cols)
-    )
+    )(in_hbm(sources[0]), in_hbm(mirror_rows), in_hbm(block_rows), in_hbm(block_cols))
+    chunks, blocks = lax.optimization_barrier((chunks, blocks))
     got = lax.all_to_all(chunks, AXES, 0, 0)
     other_blocks = swapped(blocks, 1)
-    own_blocks, pick = call(
+    weights, pick = call(
         prepare_kernel,
         [
-            shaped(*blocks.shape, dtype=blocks.dtype),
+            shaped(blocks.shape[0] // 2, 2 * BLOCK, 2 * BLOCK, dtype=blocks.dtype),
             shaped(2 * ROWS * blocks.shape[0], owners * ROWS, dtype=jnp.bfloat16),
         ],
-        [HBM] + [SMEM] * 4, [pltpu.SemaphoreType.DMA], name="prepare",
-    )(in_hbm(blocks), block_rows, block_cols, swapped(block_rows, 1), swapped(block_cols, 1))
-    near_args = (pick, own_blocks, other_blocks)
+        [HBM, VMEM, SMEM, SMEM],
+        [pltpu.VMEM(blocks.shape, blocks.dtype), pltpu.SemaphoreType.DMA],
+        name="prepare",
+    )(in_hbm(blocks), other_blocks, places, swapped(places, 1))
+    near_args = (pick, weights)
     chunks, zero, coeff = call(
-        functools.partial(first_kernel, total), [chunk, vector, tile], [VMEM] * 4, name="first"
+        functools.partial(first_kernel, total), [chunk, vector, tile], [VMEM] * 3, name="first"
     )(got, *near_args)
     got = exchanged(chunks)
     chunks, one, coeff = call(
-        functools.partial(middle_kernel, total, shift), [chunk, vector, tile], [VMEM] * 6,
+        functools.partial(middle_kernel, total, shift), [chunk, vector, tile], [VMEM] * 5,
         name="middle",
     )(got, zero, coeff, *near_args)
     first_got, got = got, exchanged(chunks)
     chunks, two, coeff, same, flip = call(
         functools.partial(last_kernel, total, shift),
-        [pltpu.VMEM((devices, BLOCK), jnp.float32), vector, tile, tile, tile], [VMEM] * 8,
+        [shaped(devices, BLOCK), vector, tile, tile, tile], [VMEM] * 7,
         name="last",
     )(first_got, got, zero, one, coeff, *near_args)
     got = lax.all_to_all(chunks.reshape(devices, 1, BLOCK), AXES, 0, 0)

time: 51.9 us -> 51.3 us (0.988)
    ppermute x6 -> x5, starting transfers between devices: 2.92 us -> 2.66 us  [swapped(): return lax.ppermute(value, AXES, [(i, i ^ bits) for i in range(devices)])]
    ppermute x6 -> x5, waiting for transfers between devices: 3.9 us -> 3.92 us  [swapped(): return lax.ppermute(value, AXES, [(i, i ^ bits) for i in range(devices)])]
  transfers between devices with their start and end apart: 8 -> 7, of which waited for: 6 -> 5; matrix products, arithmetic and copies ran while one was open for 0% -> 0% of each run, Pallas kernels for 4% -> 5%
where the time goes in v7:
time: 51.3 us; the launch traced here: 51 us
  blocking collectives  19.8 us (39%)
  starting transfers between devices  12.2 us (24%)
  waiting for transfers between devices  10.7 us (21%)
  Pallas kernels  7.64 us (15%)
  between operations  0.69 us (1%)
    all_to_all x2, blocking collectives, exchanged(): return lax.all_to_all(chunks, AXES, 0, 0, axis_index_groups=same_core)  19.8 us
    all_to_all x1, starting transfers between devices, on_device(): got = lax.all_to_all(chunks, AXES, 0, 0)  6.96 us
    all_to_all x1, waiting for transfers between devices, on_device(): got = lax.all_to_all(chunks, AXES, 0, 0)  4.84 us
    ppermute x5, waiting for transfers between devices, swapped(): return lax.ppermute(value, AXES, [(i, i ^ bits) for i in range(devices)])  3.92 us
    ppermute x5, starting transfers between devices, swapped(): return lax.ppermute(value, AXES, [(i, i ^ bits) for i in range(devices)])  2.66 us
    all_to_all x1, starting transfers between devices, on_device(): got = lax.all_to_all(chunks.reshape(devices, 1, BLOCK), AXES, 0, 0)  2.57 us
    pallas_call x1, Pallas kernels, on_device(): call(prepare_kernel, [shaped(blocks.shape[0] // 2, 2 * BLOCK, 2 * BLOCK,...  2.12 us
    all_to_all x1, waiting for transfers between devices, on_device(): got = lax.all_to_all(chunks.reshape(devices, 1, BLOCK), AXES, 0, 0)  1.9 us
  transfers between devices with their start and end apart: 7, of which 5 were waited for; matrix products, arithmetic and copies ran while one was open for 0% of the time, Pallas kernels for 5%

profile of v7, /device:TPU:0, one launch (start us, length us, event | category | flops | bytes accessed | tf_op | source)
XLA Modules:
  0.0 51.0 jit_solution(12671847369228111946)
XLA Ops:
  0.6 1.5 %start.1 = (f32[32,8,128]{2,1,0:T(8,128)}, s32[2,128]{1,0:T(2,128)S(1)}, s32[2,1,32]{2,1,0:T(1,128)S(1)}) custom-call(f32[8,256]{1,0:T(8,128)} %bitcast.14, s32[2,128]{1,0:T(2,128)} %bitcast.15, s32[1,32]{1,0:T(1,128)} %rows_hbm.1, s32[1,32]{1,0:T(1,128)} %cols_hbm.1), custom_call_target="tpu_custom_call" | custom-call | tf_op jit(solution)/shard_map/start/pallas_call | solution.py:406
  2.1 0.5 %collective-permute-start = (bf16[32,128,128]{2,1,0:T(8,128)(2,1)}, bf16[32,128,128]{2,1,0:T(8,128)(2,1)S(1)}, u32[]{:S(2)}, u32[]{:S(2)}) collective-permute-start(bf16[32,128,128]{2,1,0:T(8,128)(2,1)} %bitcast.12), channel_id=1, source_target_pairs={{0,1},{1,0},{2,3},{3,2},{4,5},{5,4},{6,7},{7,6},{8,9},{9,8},{10,11... | collective-permute-start | bytes 3145736 | tf_op jit(solution)/shard_map/ppermute | solution.py:401
  2.6 7.0 %all-to-all-start = ((f32[32,8,128]{2,1,0:T(8,128)}), f32[32,8,128]{2,1,0:T(8,128)S(1)}, u32[]{:S(2)}, u32[]{:S(2)}) async-start(f32[32,8,128]{2,1,0:T(8,128)} %get-tuple-element.26), calls=%async_computation | async-start | bytes 262144 | tf_op jit(solution)/shard_map/all_to_all | solution.py:418
  9.6 0.3 collective-permute-start.1
  9.9 0.9 %collective-permute-done.1.other_places = s32[2,1,32]{2,1,0:T(1,128)S(1)} collective-permute-done((s32[2,1,32]{2,1,0:T(1,128)S(1)}, s32[2,1,32]{2,1,0:T(1,128)S(1)}, u32[]{:S(2)}, u32[]{:S(2)}) %collective-permute-start.1) | collective-permute-done | bytes 288 | tf_op jit(solution)/shard_map/ppermute | solution.py:401
  10.8 0.0 collective-permute-done.other_ref
  10.8 2.1 %prepare.1 = (bf16[16,256,256]{2,1,0:T(8,128)(2,1)S(1)}, bf16[512,128]{1,0:T(8,128)(2,1)S(1)}) custom-call(bf16[32,128,128]{2,1,0:T(8,128)(2,1)} %bitcast.13, bf16[32,128,128]{2,1,0:T(8,128)(2,1)S(1)} %collective-permute-done.other_ref, s32[2,1,32]{2,1,0:T(1,128)S(1)} %get-tuple-element.28.own_places, s32[2,1,32]{2,1,0:T(1,128)S(1)} %collective-permute-done.1.other_places), custom_call_target="tpu_custom_call" | custom-call | tf_op jit(solution)/shard_map/prepare/pallas_call | solution.py:420
  12.9 4.8 %all-to-all-done.got_ref = f32[32,8,128]{2,1,0:T(8,128)S(1)} async-done(((f32[32,8,128]{2,1,0:T(8,128)}), f32[32,8,128]{2,1,0:T(8,128)S(1)}, u32[]{:S(2)}, u32[]{:S(2)}) %all-to-all-start) | async-done | bytes 131104 | tf_op jit(solution)/shard_map/all_to_all | solution.py:418
  17.8 0.7 %first.1 = (f32[16,2,8,128]{3,2,1,0:T(8,128)S(1)}, f32[32,8,128]{2,1,0:T(8,128)S(1)}, f32[8,128]{1,0:T(8,128)S(1)}) custom-call(f32[32,8,128]{2,1,0:T(8,128)S(1)} %all-to-all-done.got_ref, bf16[512,128]{1,0:T(8,128)(2,1)S(1)} %get-tuple-element.29.pick_ref, bf16[16,256,256]{2,1,0:T(8,128)(2,1)S(1)} %get-tuple-element.30.weights_ref), custom_call_target="tpu_custom_call" | custom-call | tf_op jit(solution)/shard_map/first/pallas_call | solution.py:431
  18.5 10.0 %all_to_all.20.got_ref.first_got_ref = f32[16,2,8,128]{3,2,1,0:T(8,128)S(1)} all-to-all(f32[16,2,8,128]{3,2,1,0:T(8,128)S(1)} %get-tuple-element.31), channel_id=1, replica_groups={{2,4,6,8,10,12,14,16,18,20,22,24,26,28,30,0},{3,5,7,9,11,13,15,17,19,21..., dimensions={0} | all-to-all | bytes 262144 | tf_op jit(solution)/shard_map/all_to_all | solution.py:404
  28.5 0.7 %middle.1 = (f32[16,2,8,128]{3,2,1,0:T(8,128)S(1)}, f32[32,8,128]{2,1,0:T(8,128)S(1)}, f32[8,128]{1,0:T(8,128)S(1)}) custom-call(f32[16,2,8,128]{3,2,1,0:T(8,128)S(1)} %all_to_all.20.got_ref.first_got_ref, f32[32,8,128]{2,1,0:T(8,128)S(1)} %get-tuple-element.32.basis_ref.zero_ref, f32[8,128]{1,0:T(8,128)S(1)} %get-tuple-element.33.known_ref, ...), custom_call_target="tpu_custom_call" | custom-call | tf_op jit(solution)/shard_map/middle/pallas_call | solution.py:435
  29.2 9.8 %all_to_all.21.got_ref = f32[16,2,8,128]{3,2,1,0:T(8,128)S(1)} all-to-all(f32[16,2,8,128]{3,2,1,0:T(8,128)S(1)} %get-tuple-element.34), channel_id=1, replica_groups={{2,4,6,8,10,12,14,16,18,20,22,24,26,28,30,0},{3,5,7,9,11,13,15,17,19,21..., dimensions={0} | all-to-all | bytes 262144 | tf_op jit(solution)/shard_map/all_to_all | solution.py:404
  39.0 1.4 %last.1 = (f32[32,128]{1,0:T(8,128)}, f32[32,8,128]{2,1,0:T(8,128)S(1)}, f32[8,128]{1,0:T(8,128)S(1)}, f32[8,128]{1,0:T(8,128)S(1)}, f32[8,128]{1,0:T(8,128)S(1)}) custom-call(f32[16,2,8,128]{3,2,1,0:T(8,128)S(1)} %all_to_all.20.got_ref.first_got_ref, f32[16,2,8,128]{3,2,1,0:T(8,128)S(1)} %all_to_all.21.got_ref, ...), custom_call_target="tpu_custom_call" | custom-call | tf_op jit(solution)/shard_map/last/pallas_call | solution.py:440
  40.4 0.0 collective-permute-start.2
  40.4 2.6 %all-to-all-start.3 = ((f32[32,1,128]{2,1,0:T(1,128)}), f32[32,1,128]{2,1,0:T(1,128)S(1)}, u32[]{:S(2)}, u32[]{:S(2)}) async-start(f32[32,1,128]{2,1,0:T(1,128)} %bitcast.4), calls=%async_computation.3 | async-start | bytes 32768 | tf_op jit(solution)/shard_map/all_to_all | solution.py:445
  43.0 1.8 %collective-permute-start.3 = (f32[8,128]{1,0:T(8,128)S(1)}, f32[8,128]{1,0:T(8,128)S(1)}, u32[]{:S(2)}, u32[]{:S(2)}) collective-permute-start(f32[8,128]{1,0:T(8,128)S(1)} %get-tuple-element.40.same_ref), channel_id=1, source_target_pairs={{0,16},{1,17},{2,18},{3,19},{4,20},{5,21},{6,22},{7,23},{8,24},{9,... | collective-permute-start | bytes 12296 | tf_op jit(solution)/shard_map/ppermute | solution.py:401
  44.8 0.0 collective-permute-start.4
  44.8 1.8 %collective-permute-done.3.across_ref = f32[8,128]{1,0:T(8,128)S(1)} collective-permute-done((f32[8,128]{1,0:T(8,128)S(1)}, f32[8,128]{1,0:T(8,128)S(1)}, u32[]{:S(2)}, u32[]{:S(2)}) %collective-permute-start.3) | collective-permute-done | bytes 4128 | tf_op jit(solution)/shard_map/ppermute | solution.py:401
  46.6 1.2 %collective-permute-done.4.flipped_ref = f32[8,128]{1,0:T(8,128)S(1)} collective-permute-done((f32[8,128]{1,0:T(8,128)S(1)}, f32[8,128]{1,0:T(8,128)S(1)}, u32[]{:S(2)}, u32[]{:S(2)}) %collective-permute-start.4) | collective-permute-done | bytes 4128 | tf_op jit(solution)/shard_map/ppermute | solution.py:401
  47.8 0.0 collective-permute-done.2.theirs_ref
  47.8 0.3 keep.1
  48.1 1.9 %all-to-all-done.3 = f32[32,1,128]{2,1,0:T(1,128)S(1)} async-done(((f32[32,1,128]{2,1,0:T(1,128)}), f32[32,1,128]{2,1,0:T(1,128)S(1)}, u32[]{:S(2)}, u32[]{:S(2)}) %all-to-all-start.3) | async-done | bytes 16416 | tf_op jit(solution)/shard_map/all_to_all | solution.py:445
  50.0 0.9 %final.1 = (f32[4,8,256]{2,1,0:T(8,128)}, f32[3,4,8]{2,1,0:T(4,128)}) custom-call(f32[32,128]{1,0:T(8,128)S(1)} %bitcast.11, f32[4,8,256]{2,1,0:T(8,128)S(1)} %get-tuple-element.43.kept_ref, f32[8,128]{1,0:T(8,128)S(1)} %get-tuple-element.44.known_ref, f32[8,128]{1,0:T(8,128)S(1)} %get-tuple-element.45.gram_ref), custom_call_target="tpu_custom_call" | custom-call | tf_op jit(solution)/shard_map/final/pallas_call | solution.py:455
  (1 shorter events, 0.0 us)
Async XLA Ops:
  2.1 8.7 %collective-permute-start = (bf16[32,128,128]{2,1,0:T(8,128)(2,1)}, bf16[32,128,128]{2,1,0:T(8,128)(2,1)S(1)}, u32[]{:S(2)}, u32[]{:S(2)}) collective-permute-start(bf16[32,128,128]{2,1,0:T(8,128)(2,1)} %bitcast.12), channel_id=1, source_target_pairs={{0,1},{1,0},{2,3},{3,2},{4,5},{5,4},{6,7},{7,6},{8,9},{9,8},{10,11... | collective-permute-start | bytes 3145736 | tf_op jit(solution)/shard_map/ppermute | solution.py:401
  2.6 15.1 %all-to-all-start = ((f32[32,8,128]{2,1,0:T(8,128)}), f32[32,8,128]{2,1,0:T(8,128)S(1)}, u32[]{:S(2)}, u32[]{:S(2)}) async-start(f32[32,8,128]{2,1,0:T(8,128)} %get-tuple-element.26), calls=%async_computation | async-start | bytes 262144 | tf_op jit(solution)/shard_map/all_to_all | solution.py:418
  9.6 1.2 %collective-permute-start.1 = (s32[2,1,32]{2,1,0:T(1,128)S(1)}, s32[2,1,32]{2,1,0:T(1,128)S(1)}, u32[]{:S(2)}, u32[]{:S(2)}) collective-permute-start(s32[2,1,32]{2,1,0:T(1,128)S(1)} %get-tuple-element.28.own_places), channel_id=1, source_target_pairs={{0,1},{1,0},{2,3},{3,2},{4,5},{5,4},{6,7},{7,6},{8,9},{9,8},{10,11... | collective-permute-start | bytes 776 | tf_op jit(solution)/shard_map/ppermute | solution.py:401
  40.4 7.4 %collective-permute-start.2 = (f32[8,8,128]{2,1,0:T(8,128)S(1)}, f32[8,8,128]{2,1,0:T(8,128)S(1)}, u32[]{:S(2)}, u32[]{:S(2)}) collective-permute-start(f32[8,8,128]{2,1,0:T(8,128)S(1)} %pack.1), channel_id=1, source_target_pairs={{0,1},{1,0},{2,3},{3,2},{4,5},{5,4},{6,7},{7,6},{8,9},{9,8},{10,11... | collective-permute-start | bytes 98312 | tf_op jit(solution)/shard_map/ppermute | solution.py:401
  40.4 9.6 %all-to-all-start.3 = ((f32[32,1,128]{2,1,0:T(1,128)}), f32[32,1,128]{2,1,0:T(1,128)S(1)}, u32[]{:S(2)}, u32[]{:S(2)}) async-start(f32[32,1,128]{2,1,0:T(1,128)} %bitcast.4), calls=%async_computation.3 | async-start | bytes 32768 | tf_op jit(solution)/shard_map/all_to_all | solution.py:445
  43.0 3.7 %collective-permute-start.3 = (f32[8,128]{1,0:T(8,128)S(1)}, f32[8,128]{1,0:T(8,128)S(1)}, u32[]{:S(2)}, u32[]{:S(2)}) collective-permute-start(f32[8,128]{1,0:T(8,128)S(1)} %get-tuple-element.40.same_ref), channel_id=1, source_target_pairs={{0,16},{1,17},{2,18},{3,19},{4,20},{5,21},{6,22},{7,23},{8,24},{9,... | collective-permute-start | bytes 12296 | tf_op jit(solution)/shard_map/ppermute | solution.py:401
  44.8 3.0 %collective-permute-start.4 = (f32[8,128]{1,0:T(8,128)S(1)}, f32[8,128]{1,0:T(8,128)S(1)}, u32[]{:S(2)}, u32[]{:S(2)}) collective-permute-start(f32[8,128]{1,0:T(8,128)S(1)} %get-tuple-element.41.flip_ref), channel_id=1, source_target_pairs={{0,17},{1,16},{2,19},{3,18},{4,21},{5,20},{6,23},{7,22},{8,25},{9,... | collective-permute-start | bytes 12296 | tf_op jit(solution)/shard_map/ppermute | solution.py:401

commit v8 on v7

--- a/solution.py
+++ b/solution.py
@@ -16,6 +16,7 @@
 AXES = ("side", "grp", "dev")
 VMEM_LIMIT = 48 * 2**20
 LENGTH_LANE = ITERS * (ITERS + 1)
+CROSSED = [(0, 1), (0, 2), (1, 2)]
 
 
 def position():
@@ -160,9 +161,8 @@
 
 
 def first_kernel(total, got_ref, pick_ref, weights_ref, chunk_ref, basis_ref, coeff_ref):
-    side, owner, core = position()
+    side, _, _ = position()
     owners = got_ref.shape[0] // 2
-    base = owner - core
     port = got_ref[:owners]
     star = got_ref[owners:]
     sym = port + star
@@ -173,11 +173,7 @@
     coeff_ref[...] = columns({LENGTH_LANE: jnp.sqrt(squares)})
     basis_ref[:owners] = sym * scale
     basis_ref[owners:] = anti * scale
-    images = []
-    for place, tile in enumerate(tiles):
-        here, there = got_ref[base + place], got_ref[owners + base + place]
-        images.append((tile + 0.5 * jnp.where(side == 0, here + there, here - there)) * scale)
-    spread(chunk_ref, *images)
+    spread(chunk_ref, *[tile * scale for tile in tiles])
 
 
 def in_order(got_ref, shift):
@@ -192,36 +188,40 @@
     return got_ref[chip, 0], got_ref[chip, 1]
 
 
-def advanced(total, shift, got_refs, basis_refs, pick_ref, weights_ref):
+def advanced(total, shift, got_refs, basis_refs, overlaps, pick_ref, weights_ref):
     side, _, _ = position()
     got = in_order(got_refs[-1], shift)
     half = got.shape[0] // 2
     tiles = near(jnp.where(side == 0, got[:half], got[half:]), pick_ref, weights_ref)
     got = got.reshape(basis_refs[0].shape)
     inner = 0.5 / total
-    coeffs = [dot(got, ref[...]) * inner for ref in basis_refs]
+    multiples = [
+        dot(got, ref[...]) * inner + 0.5 * overlap for ref, overlap in zip(basis_refs, overlaps)
+    ]
     rest = got
-    for coeff, ref in zip(coeffs, basis_refs):
-        rest = rest - coeff * ref[...]
+    for multiple, ref in zip(multiples, basis_refs):
+        rest = rest - multiple * ref[...]
     squares = dot(rest, rest) * inner + EPSILON
     scale = lax.rsqrt(squares)
     owned = [own_tiles(ref, shift) for ref in got_refs]
-    images = []
-    for place, tile in enumerate(tiles):
-        value = tile + 0.5 * owned[-1][place]
-        for coeff, earlier in zip(coeffs, owned):
-            value = value - coeff * earlier[place]
-        images.append(value * scale)
-    return coeffs + [jnp.sqrt(squares)], rest * scale, images
+    parts = []
+    for place, value in enumerate(tiles):
+        for multiple, earlier in zip(multiples, owned):
+            value = value - multiple * earlier[place]
+        parts.append(value * scale)
+    coeffs = multiples[:-1] + [multiples[-1] + 0.5, jnp.sqrt(squares)]
+    return coeffs, rest * scale, parts
 
 
 def middle_kernel(total, shift, got_ref, basis_ref, known_ref, pick_ref, weights_ref,
                   chunk_ref, next_ref, coeff_ref):
-    coeffs, next_ref[...], images = advanced(
-        total, shift, [got_ref], [basis_ref], pick_ref, weights_ref
-    )
-    coeff_ref[...] = columns(dict(enumerate(coeffs))) + known_ref[...]
-    spread(chunk_ref, *images)
+    known = known_ref[...]
+    length = known[:, LENGTH_LANE : LENGTH_LANE + 1]
+    coeffs, next_ref[...], parts = advanced(
+        total, shift, [got_ref], [basis_ref], [-EPSILON / (length * length)], pick_ref, weights_ref
+    )
+    coeff_ref[...] = columns(dict(enumerate(coeffs))) + known
+    spread(chunk_ref, *parts)
 
 
 def last_kernel(total, shift, first_got_ref, got_ref, zero_ref, one_ref, known_ref, pick_ref,
@@ -229,8 +229,12 @@
     side, owner, core = position()
     owners = two_ref.shape[0] // 2
     refs = [zero_ref, one_ref, two_ref]
+    known = known_ref[...]
+    length = known[:, LENGTH_LANE : LENGTH_LANE + 1]
+    coeff, norm = known[:, 0:1], known[:, 1:2]
+    overlaps = [coeff * EPSILON / (length * length * norm), -EPSILON / (norm * norm)]
     coeffs, two_ref[...], tiles = advanced(
-        total, shift, [first_got_ref, got_ref], refs[:2], pick_ref, weights_ref
+        total, shift, [first_got_ref, got_ref], refs[:2], overlaps, pick_ref, weights_ref
     )
     base = side * owners + owner - core
     rhs = iota((ROWS, BLOCK), 0)
@@ -246,22 +250,29 @@
     row = jnp.sum(spots, axis=0, keepdims=True)
     chunk_ref[...] = jnp.broadcast_to(row, chunk_ref.shape)
     coeffs = columns({place + ITERS + 1: value for place, value in enumerate(coeffs)})
-    coeff_ref[...] = coeffs + known_ref[...]
+    coeff_ref[...] = coeffs + known
     same_ref[...] = jnp.where(core == 0, tiles[0], tiles[1])
     flip_ref[...] = jnp.where(core == 0, tiles[1], tiles[0])
 
 
-def pack_kernel(zero_ref, one_ref, two_ref, coeff_ref, flip_ref, theirs_ref):
+def early_kernel(zero_ref, one_ref, theirs_ref):
     _, owner, core = position()
     owners = zero_ref.shape[0] // 2
-    for index, ref in enumerate((zero_ref, one_ref, two_ref)):
+    for index, ref in enumerate((zero_ref, one_ref)):
         for half in range(2):
             theirs_ref[2 * index + half] = ref[half * owners + owner + 1 - 2 * core]
-    theirs_ref[2 * ITERS] = flip_ref[...]
-    theirs_ref[2 * ITERS + 1] = coeff_ref[...]
-
-
-def keep_kernel(zero_ref, one_ref, two_ref, coeff_ref, same_ref, theirs_ref, across_ref,
+
+
+def pack_kernel(two_ref, coeff_ref, flip_ref, theirs_ref):
+    _, owner, core = position()
+    owners = two_ref.shape[0] // 2
+    for half in range(2):
+        theirs_ref[half] = two_ref[half * owners + owner + 1 - 2 * core]
+    theirs_ref[2] = flip_ref[...]
+    theirs_ref[3] = coeff_ref[...]
+
+
+def keep_kernel(zero_ref, one_ref, two_ref, coeff_ref, same_ref, early_ref, theirs_ref, across_ref,
                 flipped_ref, mirror_ref, kept_ref, known_ref, gram_ref):
     side, owner, core = position()
     owners = zero_ref.shape[0] // 2
@@ -273,11 +284,14 @@
     for index, ref in enumerate((zero_ref, one_ref, two_ref)):
         pairs.append(
             [
-                by_core(ref[half * owners + owner], theirs_ref[2 * index + half])
+                by_core(
+                    ref[half * owners + owner],
+                    early_ref[2 * index + half] if index < 2 else theirs_ref[half],
+                )
                 for half in range(2)
             ]
         )
-    here = by_core(same_ref[...], theirs_ref[2 * ITERS])
+    here = by_core(same_ref[...], theirs_ref[2])
     there = by_core(across_ref[...], flipped_ref[...])
     pairs.append(
         [
@@ -285,7 +299,7 @@
             [jnp.where(side == 0, t, h) for h, t in zip(here, there)],
         ]
     )
-    known = by_core(coeff_ref[...], theirs_ref[2 * ITERS + 1])
+    known = by_core(coeff_ref[...], theirs_ref[3])
     known = jnp.concatenate([tile[:HALF_RHS] for tile in known], axis=0)
     known_ref[...] = jnp.where(iota((ROWS, BLOCK), 1) < LENGTH_LANE, known, 0.0)
 
@@ -333,20 +347,27 @@
         )
         for index in range(ITERS + 1)
     ]
-    coeffs = values[:ITERS]
-    gram = gram_ref[...]
+    dots = values[:ITERS]
+    short = [gram_ref[:, j : j + 1] for j in range(ITERS)]
+    crossed = dict(
+        zip(CROSSED, [gram_ref[:, ITERS + j : ITERS + j + 1] for j in range(len(CROSSED))])
+    )
+    multiples = [
+        dots[0] + 0.5 * crossed[0, 2], dots[1] + 0.5 * crossed[1, 2], dots[2] - 0.5 * short[2]
+    ]
     squares = values[ITERS]
     for j in range(ITERS):
-        squares = squares - coeffs[j] * coeffs[j] * (1.0 + gram[:, j : j + 1])
-    for place, (i, j) in enumerate(((0, 1), (0, 2), (1, 2))):
-        squares = squares + 2.0 * coeffs[i] * coeffs[j] * gram[:, ITERS + place : ITERS + place + 1]
+        squares = squares - multiples[j] * (2.0 * dots[j] - multiples[j] * (1.0 - short[j]))
+    for (i, j), value in crossed.items():
+        squares = squares + 2.0 * multiples[i] * multiples[j] * value
     squares = jnp.maximum(squares, 0.0) + EPSILON
     norm = jnp.sqrt(squares)
     rest = kept_ref[ITERS]
     for j in range(ITERS):
-        rest = rest - coeffs[j] * kept_ref[j]
+        rest = rest - multiples[j] * kept_ref[j]
     basis_ref[:ITERS] = kept_ref[:ITERS]
     basis_ref[ITERS] = rest * lax.rsqrt(squares)
+    coeffs = multiples[:-1] + [multiples[-1] + 0.5]
     place = 2 * (ITERS + 1)
     whole = known_ref[...] + columns(
         {place + index: value for index, value in enumerate(coeffs + [norm])}
@@ -436,6 +457,8 @@
         functools.partial(middle_kernel, total, shift), [chunk, vector, tile], [VMEM] * 5,
         name="middle",
     )(got, zero, coeff, *near_args)
+    [early] = call(early_kernel, [shaped(4, ROWS, BLOCK)], [VMEM] * 2, name="early")(zero, one)
+    early = swapped(early, 1)
     first_got, got = got, exchanged(chunks)
     chunks, two, coeff, same, flip = call(
         functools.partial(last_kernel, total, shift),
@@ -443,13 +466,13 @@
         name="last",
     )(first_got, got, zero, one, coeff, *near_args)
     got = lax.all_to_all(chunks.reshape(devices, 1, BLOCK), AXES, 0, 0)
-    [theirs] = call(
-        pack_kernel, [shaped(2 * ITERS + 2, ROWS, BLOCK)], [VMEM] * 5, name="pack"
-    )(zero, one, two, coeff, flip)
+    [theirs] = call(pack_kernel, [shaped(4, ROWS, BLOCK)], [VMEM] * 3, name="pack")(
+        two, coeff, flip
+    )
     kept, known, gram = call(
-        keep_kernel, [shaped(ITERS + 1, ROWS, panels), tile, tile], [VMEM] * 9, name="keep"
+        keep_kernel, [shaped(ITERS + 1, ROWS, panels), tile, tile], [VMEM] * 10, name="keep"
     )(
-        zero, one, two, coeff, same, swapped(theirs, 1), swapped(same, devices // 2),
+        zero, one, two, coeff, same, early, swapped(theirs, 1), swapped(same, devices // 2),
         swapped(flip, devices // 2 ^ 1), mirror_rows,
     )
     basis, hessenberg = call(

time: 51.3 us -> 51.3 us (level)
    ppermute x5 -> x6, starting transfers between devices: 2.66 us -> 3.08 us  [swapped(): return lax.ppermute(value, AXES, [(i, i ^ bits) for i in range(devices)])]
    ppermute x5 -> x6, waiting for transfers between devices: 3.92 us -> 3.92 us  [swapped(): return lax.ppermute(value, AXES, [(i, i ^ bits) for i in range(devices)])]
  transfers between devices with their start and end apart: 7 -> 8, of which waited for: 5 -> 5; matrix products, arithmetic and copies ran while one was open for 0% -> 0% of each run, Pallas kernels for 5% -> 5%
where the time goes in v8:
time: 51.3 us; the launch traced here: 51 us
  blocking collectives  19.8 us (39%)
  starting transfers between devices  12.6 us (25%)
  waiting for transfers between devices  10.2 us (20%)
  Pallas kernels  7.7 us (15%)
  between operations  0.7 us (1%)
    all_to_all x2, blocking collectives, exchanged(): return lax.all_to_all(chunks, AXES, 0, 0, axis_index_groups=same_core)  19.8 us
    all_to_all x1, starting transfers between devices, on_device(): got = lax.all_to_all(chunks, AXES, 0, 0)  6.96 us
    all_to_all x1, waiting for transfers between devices, on_device(): got = lax.all_to_all(chunks, AXES, 0, 0)  4.84 us
    ppermute x6, waiting for transfers between devices, swapped(): return lax.ppermute(value, AXES, [(i, i ^ bits) for i in range(devices)])  3.92 us
    ppermute x6, starting transfers between devices, swapped(): return lax.ppermute(value, AXES, [(i, i ^ bits) for i in range(devices)])  3.08 us
    all_to_all x1, starting transfers between devices, on_device(): got = lax.all_to_all(chunks.reshape(devices, 1, BLOCK), AXES, 0, 0)  2.54 us
    pallas_call x1, Pallas kernels, on_device(): call(prepare_kernel, [shaped(blocks.shape[0] // 2, 2 * BLOCK, 2 * BLOCK,...  2.12 us
    pallas_call x1, Pallas kernels, on_device(): call(start_kernel, [vector, shaped(*mirror_rows.shape, dtype=jnp.int32),...  1.48 us
  transfers between devices with their start and end apart: 8, of which 5 were waited for; matrix products, arithmetic and copies ran while one was open for 0% of the time, Pallas kernels for 5%

profile of v8, /device:TPU:0, one launch (start us, length us, event | category | flops | bytes accessed | tf_op | source)
XLA Modules:
  0.0 51.0 jit_solution(17159870061891442980)
XLA Ops:
  0.6 1.5 %start.1 = (f32[32,8,128]{2,1,0:T(8,128)}, s32[2,128]{1,0:T(2,128)S(1)}, s32[2,1,32]{2,1,0:T(1,128)S(1)}) custom-call(f32[8,256]{1,0:T(8,128)} %bitcast.14, s32[2,128]{1,0:T(2,128)} %bitcast.15, s32[1,32]{1,0:T(1,128)} %rows_hbm.1, s32[1,32]{1,0:T(1,128)} %cols_hbm.1), custom_call_target="tpu_custom_call" | custom-call | tf_op jit(solution)/shard_map/start/pallas_call | solution.py:427
  2.1 0.5 %collective-permute-start = (bf16[32,128,128]{2,1,0:T(8,128)(2,1)}, bf16[32,128,128]{2,1,0:T(8,128)(2,1)S(1)}, u32[]{:S(2)}, u32[]{:S(2)}) collective-permute-start(bf16[32,128,128]{2,1,0:T(8,128)(2,1)} %bitcast.12), channel_id=1, source_target_pairs={{0,1},{1,0},{2,3},{3,2},{4,5},{5,4},{6,7},{7,6},{8,9},{9,8},{10,11... | collective-permute-start | bytes 3145736 | tf_op jit(solution)/shard_map/ppermute | solution.py:422
  2.6 7.0 %all-to-all-start = ((f32[32,8,128]{2,1,0:T(8,128)}), f32[32,8,128]{2,1,0:T(8,128)S(1)}, u32[]{:S(2)}, u32[]{:S(2)}) async-start(f32[32,8,128]{2,1,0:T(8,128)} %get-tuple-element.26), calls=%async_computation | async-start | bytes 262144 | tf_op jit(solution)/shard_map/all_to_all | solution.py:439
  9.6 0.3 collective-permute-start.1
  9.9 0.9 %collective-permute-done.1.other_places = s32[2,1,32]{2,1,0:T(1,128)S(1)} collective-permute-done((s32[2,1,32]{2,1,0:T(1,128)S(1)}, s32[2,1,32]{2,1,0:T(1,128)S(1)}, u32[]{:S(2)}, u32[]{:S(2)}) %collective-permute-start.1) | collective-permute-done | bytes 288 | tf_op jit(solution)/shard_map/ppermute | solution.py:422
  10.8 0.0 collective-permute-done.other_ref
  10.8 2.1 %prepare.1 = (bf16[16,256,256]{2,1,0:T(8,128)(2,1)S(1)}, bf16[512,128]{1,0:T(8,128)(2,1)S(1)}) custom-call(bf16[32,128,128]{2,1,0:T(8,128)(2,1)} %bitcast.13, bf16[32,128,128]{2,1,0:T(8,128)(2,1)S(1)} %collective-permute-done.other_ref, s32[2,1,32]{2,1,0:T(1,128)S(1)} %get-tuple-element.28.own_places, s32[2,1,32]{2,1,0:T(1,128)S(1)} %collective-permute-done.1.other_places), custom_call_target="tpu_custom_call" | custom-call | tf_op jit(solution)/shard_map/prepare/pallas_call | solution.py:441
  12.9 4.8 %all-to-all-done.got_ref = f32[32,8,128]{2,1,0:T(8,128)S(1)} async-done(((f32[32,8,128]{2,1,0:T(8,128)}), f32[32,8,128]{2,1,0:T(8,128)S(1)}, u32[]{:S(2)}, u32[]{:S(2)}) %all-to-all-start) | async-done | bytes 131104 | tf_op jit(solution)/shard_map/all_to_all | solution.py:439
  17.8 0.7 %first.1 = (f32[16,2,8,128]{3,2,1,0:T(8,128)S(1)}, f32[32,8,128]{2,1,0:T(8,128)S(1)}, f32[8,128]{1,0:T(8,128)S(1)}) custom-call(f32[32,8,128]{2,1,0:T(8,128)S(1)} %all-to-all-done.got_ref, bf16[512,128]{1,0:T(8,128)(2,1)S(1)} %get-tuple-element.29.pick_ref, bf16[16,256,256]{2,1,0:T(8,128)(2,1)S(1)} %get-tuple-element.30.weights_ref), custom_call_target="tpu_custom_call" | custom-call | tf_op jit(solution)/shard_map/first/pallas_call | solution.py:452
  18.5 10.0 %all_to_all.20.got_ref.first_got_ref = f32[16,2,8,128]{3,2,1,0:T(8,128)S(1)} all-to-all(f32[16,2,8,128]{3,2,1,0:T(8,128)S(1)} %get-tuple-element.31), channel_id=1, replica_groups={{2,4,6,8,10,12,14,16,18,20,22,24,26,28,30,0},{3,5,7,9,11,13,15,17,19,21..., dimensions={0} | all-to-all | bytes 262144 | tf_op jit(solution)/shard_map/all_to_all | solution.py:425
  28.5 0.7 %middle.1 = (f32[16,2,8,128]{3,2,1,0:T(8,128)S(1)}, f32[32,8,128]{2,1,0:T(8,128)S(1)}, f32[8,128]{1,0:T(8,128)S(1)}) custom-call(f32[16,2,8,128]{3,2,1,0:T(8,128)S(1)} %all_to_all.20.got_ref.first_got_ref, f32[32,8,128]{2,1,0:T(8,128)S(1)} %get-tuple-element.32.basis_ref.zero_ref, f32[8,128]{1,0:T(8,128)S(1)} %get-tuple-element.33.known_ref, ...), custom_call_target="tpu_custom_call" | custom-call | tf_op jit(solution)/shard_map/middle/pallas_call | solution.py:456
  29.2 9.8 %all_to_all.21.got_ref = f32[16,2,8,128]{3,2,1,0:T(8,128)S(1)} all-to-all(f32[16,2,8,128]{3,2,1,0:T(8,128)S(1)} %get-tuple-element.34), channel_id=1, replica_groups={{2,4,6,8,10,12,14,16,18,20,22,24,26,28,30,0},{3,5,7,9,11,13,15,17,19,21..., dimensions={0} | all-to-all | bytes 262144 | tf_op jit(solution)/shard_map/all_to_all | solution.py:425
  39.0 1.4 %last.1 = (f32[32,128]{1,0:T(8,128)}, f32[32,8,128]{2,1,0:T(8,128)S(1)}, f32[8,128]{1,0:T(8,128)S(1)}, f32[8,128]{1,0:T(8,128)S(1)}, f32[8,128]{1,0:T(8,128)S(1)}) custom-call(f32[16,2,8,128]{3,2,1,0:T(8,128)S(1)} %all_to_all.20.got_ref.first_got_ref, f32[16,2,8,128]{3,2,1,0:T(8,128)S(1)} %all_to_all.21.got_ref, ...), custom_call_target="tpu_custom_call" | custom-call | tf_op jit(solution)/shard_map/last/pallas_call | solution.py:463
  40.4 2.5 %all-to-all-start.3 = ((f32[32,1,128]{2,1,0:T(1,128)}), f32[32,1,128]{2,1,0:T(1,128)S(1)}, u32[]{:S(2)}, u32[]{:S(2)}) async-start(f32[32,1,128]{2,1,0:T(1,128)} %bitcast.4), calls=%async_computation.3 | async-start | bytes 32768 | tf_op jit(solution)/shard_map/all_to_all | solution.py:468
  42.9 0.2 collective-permute-start.2
  43.2 0.4 collective-permute-start.3
  43.5 1.7 %collective-permute-start.4 = (f32[8,128]{1,0:T(8,128)S(1)}, f32[8,128]{1,0:T(8,128)S(1)}, u32[]{:S(2)}, u32[]{:S(2)}) collective-permute-start(f32[8,128]{1,0:T(8,128)S(1)} %get-tuple-element.40.same_ref), channel_id=1, source_target_pairs={{0,16},{1,17},{2,18},{3,19},{4,20},{5,21},{6,22},{7,23},{8,24},{9,... | collective-permute-start | bytes 12296 | tf_op jit(solution)/shard_map/ppermute | solution.py:422
  45.2 0.0 collective-permute-start.5
  45.2 0.0 collective-permute-done.2.early_ref
  45.2 1.9 %collective-permute-done.4.across_ref = f32[8,128]{1,0:T(8,128)S(1)} collective-permute-done((f32[8,128]{1,0:T(8,128)S(1)}, f32[8,128]{1,0:T(8,128)S(1)}, u32[]{:S(2)}, u32[]{:S(2)}) %collective-permute-start.4) | collective-permute-done | bytes 4128 | tf_op jit(solution)/shard_map/ppermute | solution.py:422
  47.1 1.1 %collective-permute-done.5.flipped_ref = f32[8,128]{1,0:T(8,128)S(1)} collective-permute-done((f32[8,128]{1,0:T(8,128)S(1)}, f32[8,128]{1,0:T(8,128)S(1)}, u32[]{:S(2)}, u32[]{:S(2)}) %collective-permute-start.5) | collective-permute-done | bytes 4128 | tf_op jit(solution)/shard_map/ppermute | solution.py:422
  48.2 0.0 collective-permute-done.3.theirs_ref
  48.2 0.3 keep.1
  48.5 1.4 %all-to-all-done.3 = f32[32,1,128]{2,1,0:T(1,128)S(1)} async-done(((f32[32,1,128]{2,1,0:T(1,128)}), f32[32,1,128]{2,1,0:T(1,128)S(1)}, u32[]{:S(2)}, u32[]{:S(2)}) %all-to-all-start.3) | async-done | bytes 16416 | tf_op jit(solution)/shard_map/all_to_all | solution.py:468
  50.0 1.0 %final.1 = (f32[4,8,256]{2,1,0:T(8,128)}, f32[3,4,8]{2,1,0:T(4,128)}) custom-call(f32[32,128]{1,0:T(8,128)S(1)} %bitcast.11, f32[4,8,256]{2,1,0:T(8,128)S(1)} %get-tuple-element.43.kept_ref, f32[8,128]{1,0:T(8,128)S(1)} %get-tuple-element.44.known_ref, f32[8,128]{1,0:T(8,128)S(1)} %get-tuple-element.45.gram_ref), custom_call_target="tpu_custom_call" | custom-call | tf_op jit(solution)/shard_map/final/pallas_call | solution.py:478
  (2 shorter events, 0.0 us)
Async XLA Ops:
  2.1 8.7 %collective-permute-start = (bf16[32,128,128]{2,1,0:T(8,128)(2,1)}, bf16[32,128,128]{2,1,0:T(8,128)(2,1)S(1)}, u32[]{:S(2)}, u32[]{:S(2)}) collective-permute-start(bf16[32,128,128]{2,1,0:T(8,128)(2,1)} %bitcast.12), channel_id=1, source_target_pairs={{0,1},{1,0},{2,3},{3,2},{4,5},{5,4},{6,7},{7,6},{8,9},{9,8},{10,11... | collective-permute-start | bytes 3145736 | tf_op jit(solution)/shard_map/ppermute | solution.py:422
  2.6 15.1 %all-to-all-start = ((f32[32,8,128]{2,1,0:T(8,128)}), f32[32,8,128]{2,1,0:T(8,128)S(1)}, u32[]{:S(2)}, u32[]{:S(2)}) async-start(f32[32,8,128]{2,1,0:T(8,128)} %get-tuple-element.26), calls=%async_computation | async-start | bytes 262144 | tf_op jit(solution)/shard_map/all_to_all | solution.py:439
  9.6 1.2 %collective-permute-start.1 = (s32[2,1,32]{2,1,0:T(1,128)S(1)}, s32[2,1,32]{2,1,0:T(1,128)S(1)}, u32[]{:S(2)}, u32[]{:S(2)}) collective-permute-start(s32[2,1,32]{2,1,0:T(1,128)S(1)} %get-tuple-element.28.own_places), channel_id=1, source_target_pairs={{0,1},{1,0},{2,3},{3,2},{4,5},{5,4},{6,7},{7,6},{8,9},{9,8},{10,11... | collective-permute-start | bytes 776 | tf_op jit(solution)/shard_map/ppermute | solution.py:422
  40.4 9.6 %all-to-all-start.3 = ((f32[32,1,128]{2,1,0:T(1,128)}), f32[32,1,128]{2,1,0:T(1,128)S(1)}, u32[]{:S(2)}, u32[]{:S(2)}) async-start(f32[32,1,128]{2,1,0:T(1,128)} %bitcast.4), calls=%async_computation.3 | async-start | bytes 32768 | tf_op jit(solution)/shard_map/all_to_all | solution.py:468
  42.9 2.3 %collective-permute-start.2 = (f32[4,8,128]{2,1,0:T(8,128)S(1)}, f32[4,8,128]{2,1,0:T(8,128)S(1)}, u32[]{:S(2)}, u32[]{:S(2)}) collective-permute-start(f32[4,8,128]{2,1,0:T(8,128)S(1)} %early.1), channel_id=1, source_target_pairs={{0,1},{1,0},{2,3},{3,2},{4,5},{5,4},{6,7},{7,6},{8,9},{9,8},{10,11... | collective-permute-start | bytes 49160 | tf_op jit(solution)/shard_map/ppermute | solution.py:422
  43.2 5.1 %collective-permute-start.3 = (f32[4,8,128]{2,1,0:T(8,128)S(1)}, f32[4,8,128]{2,1,0:T(8,128)S(1)}, u32[]{:S(2)}, u32[]{:S(2)}) collective-permute-start(f32[4,8,128]{2,1,0:T(8,128)S(1)} %pack.1), channel_id=1, source_target_pairs={{0,1},{1,0},{2,3},{3,2},{4,5},{5,4},{6,7},{7,6},{8,9},{9,8},{10,11... | collective-permute-start | bytes 49160 | tf_op jit(solution)/shard_map/ppermute | solution.py:422
  43.5 3.6 %collective-permute-start.4 = (f32[8,128]{1,0:T(8,128)S(1)}, f32[8,128]{1,0:T(8,128)S(1)}, u32[]{:S(2)}, u32[]{:S(2)}) collective-permute-start(f32[8,128]{1,0:T(8,128)S(1)} %get-tuple-element.40.same_ref), channel_id=1, source_target_pairs={{0,16},{1,17},{2,18},{3,19},{4,20},{5,21},{6,22},{7,23},{8,24},{9,... | collective-permute-start | bytes 12296 | tf_op jit(solution)/shard_map/ppermute | solution.py:422
  45.2 3.0 %collective-permute-start.5 = (f32[8,128]{1,0:T(8,128)S(1)}, f32[8,128]{1,0:T(8,128)S(1)}, u32[]{:S(2)}, u32[]{:S(2)}) collective-permute-start(f32[8,128]{1,0:T(8,128)S(1)} %get-tuple-element.41.flip_ref), channel_id=1, source_target_pairs={{0,17},{1,16},{2,19},{3,18},{4,21},{5,20},{6,23},{7,22},{8,25},{9,... | collective-permute-start | bytes 12296 | tf_op jit(solution)/shard_map/ppermute | solution.py:422

commit v9 on v7

--- a/solution.py
+++ b/solution.py
@@ -16,6 +16,9 @@
 AXES = ("side", "grp", "dev")
 VMEM_LIMIT = 48 * 2**20
 LENGTH_LANE = ITERS * (ITERS + 1)
+START_LANE = LENGTH_LANE + 1
+PACKED = ITERS + 2
+TINY = 1e-30
 
 
 def position():
@@ -160,24 +163,20 @@
 
 
 def first_kernel(total, got_ref, pick_ref, weights_ref, chunk_ref, basis_ref, coeff_ref):
-    side, owner, core = position()
+    side, _, _ = position()
     owners = got_ref.shape[0] // 2
-    base = owner - core
     port = got_ref[:owners]
     star = got_ref[owners:]
-    sym = port + star
-    anti = port - star
-    tiles = near(jnp.where(side == 0, sym, anti), pick_ref, weights_ref)
+    half = jnp.where(side == 0, port + star, port - star)
+    tiles = near(half, pick_ref, weights_ref)
     squares = per_rhs(jnp.sum(port * port + star * star, axis=0)) * (1.0 / total) + EPSILON
-    scale = lax.rsqrt(squares)
-    coeff_ref[...] = columns({LENGTH_LANE: jnp.sqrt(squares)})
-    basis_ref[:owners] = sym * scale
-    basis_ref[owners:] = anti * scale
-    images = []
-    for place, tile in enumerate(tiles):
-        here, there = got_ref[base + place], got_ref[owners + base + place]
-        images.append((tile + 0.5 * jnp.where(side == 0, here + there, here - there)) * scale)
-    spread(chunk_ref, *images)
+    own = dot(half, half) * (0.5 / total)
+    scale = lax.rsqrt(jnp.maximum(own, TINY))
+    coeff_ref[...] = columns(
+        {LENGTH_LANE: jnp.sqrt(squares), START_LANE: jnp.sqrt(own) * lax.rsqrt(squares)}
+    )
+    basis_ref[...] = half * scale
+    spread(chunk_ref, *[tile * scale for tile in tiles])
 
 
 def in_order(got_ref, shift):
@@ -186,53 +185,48 @@
 
 
 def own_tiles(got_ref, shift):
-    side, owner, _ = position()
+    _, owner, _ = position()
     chips = got_ref.shape[0]
-    chip = lax.rem(side * (chips // 2) + owner // 2 + chips - shift, chips)
+    chip = lax.rem(owner // 2 + chips - shift, chips)
     return got_ref[chip, 0], got_ref[chip, 1]
 
 
 def advanced(total, shift, got_refs, basis_refs, pick_ref, weights_ref):
-    side, _, _ = position()
-    got = in_order(got_refs[-1], shift)
-    half = got.shape[0] // 2
-    tiles = near(jnp.where(side == 0, got[:half], got[half:]), pick_ref, weights_ref)
-    got = got.reshape(basis_refs[0].shape)
+    got = in_order(got_refs[-1], shift).reshape(basis_refs[0].shape)
+    tiles = near(got, pick_ref, weights_ref)
     inner = 0.5 / total
     coeffs = [dot(got, ref[...]) * inner for ref in basis_refs]
     rest = got
     for coeff, ref in zip(coeffs, basis_refs):
         rest = rest - coeff * ref[...]
-    squares = dot(rest, rest) * inner + EPSILON
-    scale = lax.rsqrt(squares)
+    squares = dot(rest, rest) * inner
+    scale = lax.rsqrt(jnp.maximum(squares, TINY))
     owned = [own_tiles(ref, shift) for ref in got_refs]
-    images = []
-    for place, tile in enumerate(tiles):
-        value = tile + 0.5 * owned[-1][place]
+    parts = []
+    for place, value in enumerate(tiles):
         for coeff, earlier in zip(coeffs, owned):
             value = value - coeff * earlier[place]
-        images.append(value * scale)
-    return coeffs + [jnp.sqrt(squares)], rest * scale, images
+        parts.append(value * scale)
+    return coeffs + [jnp.sqrt(squares)], rest * scale, parts
 
 
 def middle_kernel(total, shift, got_ref, basis_ref, known_ref, pick_ref, weights_ref,
                   chunk_ref, next_ref, coeff_ref):
-    coeffs, next_ref[...], images = advanced(
+    coeffs, next_ref[...], parts = advanced(
         total, shift, [got_ref], [basis_ref], pick_ref, weights_ref
     )
     coeff_ref[...] = columns(dict(enumerate(coeffs))) + known_ref[...]
-    spread(chunk_ref, *images)
+    spread(chunk_ref, *parts)
 
 
 def last_kernel(total, shift, first_got_ref, got_ref, zero_ref, one_ref, known_ref, pick_ref,
-                weights_ref, chunk_ref, two_ref, coeff_ref, same_ref, flip_ref):
-    side, owner, core = position()
-    owners = two_ref.shape[0] // 2
+                weights_ref, chunk_ref, two_ref, coeff_ref, low_ref, high_ref):
+    _, owner, core = position()
     refs = [zero_ref, one_ref, two_ref]
     coeffs, two_ref[...], tiles = advanced(
         total, shift, [first_got_ref, got_ref], refs[:2], pick_ref, weights_ref
     )
-    base = side * owners + owner - core
+    base = owner - core
     rhs = iota((ROWS, BLOCK), 0)
     lane = iota((ROWS, BLOCK), 1)
     spots = jnp.zeros((ROWS, BLOCK), jnp.float32)
@@ -247,66 +241,123 @@
     chunk_ref[...] = jnp.broadcast_to(row, chunk_ref.shape)
     coeffs = columns({place + ITERS + 1: value for place, value in enumerate(coeffs)})
     coeff_ref[...] = coeffs + known_ref[...]
-    same_ref[...] = jnp.where(core == 0, tiles[0], tiles[1])
-    flip_ref[...] = jnp.where(core == 0, tiles[1], tiles[0])
-
-
-def pack_kernel(zero_ref, one_ref, two_ref, coeff_ref, flip_ref, theirs_ref):
+    low_ref[...] = tiles[0]
+    high_ref[...] = tiles[1]
+
+
+def pack_kernel(zero_ref, one_ref, two_ref, coeff_ref, low_ref, high_ref, mine_ref, theirs_ref):
     _, owner, core = position()
-    owners = zero_ref.shape[0] // 2
-    for index, ref in enumerate((zero_ref, one_ref, two_ref)):
-        for half in range(2):
-            theirs_ref[2 * index + half] = ref[half * owners + owner + 1 - 2 * core]
-    theirs_ref[2 * ITERS] = flip_ref[...]
-    theirs_ref[2 * ITERS + 1] = coeff_ref[...]
-
-
-def keep_kernel(zero_ref, one_ref, two_ref, coeff_ref, same_ref, theirs_ref, across_ref,
-                flipped_ref, mirror_ref, kept_ref, known_ref, gram_ref):
-    side, owner, core = position()
-    owners = zero_ref.shape[0] // 2
-
-    def by_core(mine, theirs):
-        return [jnp.where(core == 0, mine, theirs), jnp.where(core == 0, theirs, mine)]
-
-    pairs = []
-    for index, ref in enumerate((zero_ref, one_ref, two_ref)):
-        pairs.append(
+    for out_ref, which in ((mine_ref, core), (theirs_ref, 1 - core)):
+        for index, ref in enumerate((zero_ref, one_ref, two_ref)):
+            out_ref[index] = ref[owner - core + which]
+        out_ref[ITERS] = jnp.where(which == 0, low_ref[...], high_ref[...])
+        out_ref[ITERS + 1] = coeff_ref[...]
+
+
+def over_halves(products):
+    return sum(one * other for one, other in products)
+
+
+def keep_kernel(mine_ref, partner_ref, across_ref, flipped_ref, mirror_ref, kept_ref, known_ref,
+                terms_ref):
+    side, _, core = position()
+    packed = []
+    for index in range(PACKED):
+        mine, partner = mine_ref[index], partner_ref[index]
+        across, flipped = across_ref[index], flipped_ref[index]
+        here = [jnp.where(core == 0, mine, partner), jnp.where(core == 0, partner, mine)]
+        there = [jnp.where(core == 0, across, flipped), jnp.where(core == 0, flipped, across)]
+        packed.append(
             [
-                by_core(ref[half * owners + owner], theirs_ref[2 * index + half])
-                for half in range(2)
+                [jnp.where(side == 0, h, t) for h, t in zip(here, there)],
+                [jnp.where(side == 0, t, h) for h, t in zip(here, there)],
             ]
         )
-    here = by_core(same_ref[...], theirs_ref[2 * ITERS])
-    there = by_core(across_ref[...], flipped_ref[...])
-    pairs.append(
+    known = [
+        jnp.concatenate([tile[:HALF_RHS] for tile in packed[ITERS + 1][half]], axis=0)
+        for half in range(2)
+    ]
+
+    def entry(half, j, k):
+        place = k * (ITERS + 1) + j
+        return known[half][:, place : place + 1]
+
+    halves = range(2)
+    length = known[0][:, LENGTH_LANE : LENGTH_LANE + 1]
+    start = [known[half][:, START_LANE : START_LANE + 1] for half in halves]
+    zero = [[start[half]] for half in halves]
+    ahead = [[entry(half, 0, 0) * zero[half][0], entry(half, 1, 0) * zero[half][0]] for half in halves]
+    short = [EPSILON / (length * length)]
+    multiple = over_halves([(ahead[half][0], zero[half][0]) for half in halves]) - 0.5 * short[0]
+    rest = [[ahead[half][0] - multiple * zero[half][0], ahead[half][1]] for half in halves]
+    squares = over_halves([(value, value) for half in halves for value in rest[half]]) + EPSILON
+    norms = [jnp.sqrt(squares)]
+    one = [[value * lax.rsqrt(squares) for value in rest[half]] for half in halves]
+    heads = {(0, 0): multiple + 0.5, (1, 0): norms[0]}
+    short.append(EPSILON / squares)
+    cross = heads[0, 0] * short[0] / norms[0]
+    ahead = [
         [
-            [jnp.where(side == 0, h, t) for h, t in zip(here, there)],
-            [jnp.where(side == 0, t, h) for h, t in zip(here, there)],
+            entry(half, 0, 0) * one[half][0] + entry(half, 0, 1) * one[half][1],
+            entry(half, 1, 0) * one[half][0] + entry(half, 1, 1) * one[half][1],
+            entry(half, 2, 1) * one[half][1],
         ]
-    )
-    known = by_core(coeff_ref[...], theirs_ref[2 * ITERS + 1])
-    known = jnp.concatenate([tile[:HALF_RHS] for tile in known], axis=0)
-    known_ref[...] = jnp.where(iota((ROWS, BLOCK), 1) < LENGTH_LANE, known, 0.0)
-
-    def entry(j, k):
-        place = k * (ITERS + 1) + j
-        return known[:, place : place + 1]
-
-    norms = [known[:, LENGTH_LANE : LENGTH_LANE + 1], entry(1, 0), entry(2, 1)]
-    short = [EPSILON / (norm * norm) for norm in norms]
-    zero_one = entry(0, 0) * short[0] / norms[1]
-    zero_two = (entry(0, 1) * short[0] - entry(1, 1) * zero_one) / norms[2]
-    one_two = (entry(1, 1) * short[1] - entry(0, 1) * zero_one) / norms[2]
-    gram_ref[...] = columns(dict(enumerate(short + [zero_one, zero_two, one_two])))
+        for half in halves
+    ]
+    multiples = [
+        over_halves([(ahead[half][0], zero[half][0]) for half in halves]) + 0.5 * cross,
+        over_halves([pair for half in halves for pair in zip(ahead[half], one[half])])
+        - 0.5 * short[1],
+    ]
+    rest = [
+        [
+            ahead[half][0] - multiples[0] * zero[half][0] - multiples[1] * one[half][0],
+            ahead[half][1] - multiples[1] * one[half][1],
+            ahead[half][2],
+        ]
+        for half in halves
+    ]
+    squares = over_halves([(value, value) for half in halves for value in rest[half]]) + EPSILON
+    norms.append(jnp.sqrt(squares))
+    two = [[value * lax.rsqrt(squares) for value in rest[half]] for half in halves]
+    heads.update({(0, 1): multiples[0], (1, 1): multiples[1] + 0.5, (2, 1): norms[1]})
+    short.append(EPSILON / squares)
+    crosses = [
+        (heads[0, 1] * short[0] - heads[1, 1] * cross) / norms[1],
+        (heads[1, 1] * short[1] - heads[0, 1] * cross) / norms[1],
+    ]
+    ahead = [
+        [
+            entry(half, 0, 0) * two[half][0] + entry(half, 0, 1) * two[half][1],
+            entry(half, 1, 0) * two[half][0] + entry(half, 1, 1) * two[half][1],
+            entry(half, 2, 1) * two[half][1],
+        ]
+        for half in halves
+    ]
+    known_ref[...] = columns({k * (ITERS + 1) + j: value for (j, k), value in heads.items()})
+    terms = [0.5 * crosses[0], 0.5 * crosses[1], -0.5 * short[2]]
+    for half in halves:
+        terms += zero[half] + one[half] + two[half] + ahead[half]
+    for index, value in enumerate(terms):
+        terms_ref[index] = jnp.broadcast_to(value, (ROWS, BLOCK))
     for block in range(BLK_DEV):
         rows = slice(block * HALF_RHS, (block + 1) * HALF_RHS)
-        ports, stars = [], []
-        for sym, anti in pairs:
-            sym = jnp.concatenate([tile[rows] for tile in sym], axis=0)
-            anti = jnp.concatenate([tile[rows] for tile in anti], axis=0)
-            ports.append(0.5 * (sym + anti))
-            stars.append(0.5 * (sym - anti))
+        vectors = []
+        for half in halves:
+            parts = [
+                jnp.concatenate([tile[rows] for tile in packed[index][half]], axis=0)
+                for index in range(ITERS + 1)
+            ]
+            vectors.append(
+                [
+                    over_halves(zip(weights, parts))
+                    for weights in (
+                        zero[half], one[half], two[half], ahead[half] + [two[half][2]]
+                    )
+                ]
+            )
+        ports = [0.5 * (sym + anti) for sym, anti in zip(*vectors)]
+        stars = [0.5 * (sym - anti) for sym, anti in zip(*vectors)]
         back = exact_dot(
             jnp.concatenate(stars, axis=0), mirror_onehot(mirror_ref, block), ((1,), (1,))
         )
@@ -316,41 +367,73 @@
             )
 
 
-def final_kernel(total, got_ref, kept_ref, known_ref, gram_ref, basis_ref, hessenberg_ref):
+TERMS = 3 + 2 * 9
+
+
+def final_kernel(total, got_ref, kept_ref, known_ref, terms_ref, basis_ref, hessenberg_ref):
     inner = 0.5 / total
-    sums = jnp.sum(got_ref[...].reshape(-1, ROWS, BLOCK), axis=0)
+    got = got_ref[...]
+    devices = got.shape[0]
     even = iota((ROWS, BLOCK), 0) % 2 == 0
-    lower = jnp.sum(jnp.where(even, sums, 0.0), axis=0, keepdims=True)
-    upper = jnp.sum(jnp.where(even, 0.0, sums), axis=0, keepdims=True)
     rhs = iota((ROWS, BLOCK), 0)
     lane = iota((ROWS, BLOCK), 1)
-    spots = jnp.where(rhs < HALF_RHS, lower, upper) * inner
-    values = [
-        jnp.sum(
-            jnp.where((lane // ROWS == index) & (lane % HALF_RHS == rhs % HALF_RHS), spots, 0.0),
-            axis=1,
-            keepdims=True,
+    halves = range(2)
+    values = []
+    for half in halves:
+        rows = got[half * devices // 2 : (half + 1) * devices // 2]
+        sums = jnp.sum(rows.reshape(-1, ROWS, BLOCK), axis=0)
+        lower = jnp.sum(jnp.where(even, sums, 0.0), axis=0, keepdims=True)
+        upper = jnp.sum(jnp.where(even, 0.0, sums), axis=0, keepdims=True)
+        spots = jnp.where(rhs < HALF_RHS, lower, upper) * inner
+        values.append(
+            [
+                jnp.sum(
+                    jnp.where(
+                        (lane // ROWS == index) & (lane % HALF_RHS == rhs % HALF_RHS), spots, 0.0
+                    ),
+                    axis=1,
+                    keepdims=True,
+                )
+                for index in range(ITERS + 1)
+            ]
         )
-        for index in range(ITERS + 1)
-    ]
-    coeffs = values[:ITERS]
-    gram = gram_ref[...]
-    squares = values[ITERS]
-    for j in range(ITERS):
-        squares = squares - coeffs[j] * coeffs[j] * (1.0 + gram[:, j : j + 1])
-    for place, (i, j) in enumerate(((0, 1), (0, 2), (1, 2))):
-        squares = squares + 2.0 * coeffs[i] * coeffs[j] * gram[:, ITERS + place : ITERS + place + 1]
-    squares = jnp.maximum(squares, 0.0) + EPSILON
-    norm = jnp.sqrt(squares)
-    rest = kept_ref[ITERS]
-    for j in range(ITERS):
-        rest = rest - coeffs[j] * kept_ref[j]
+    terms = [terms_ref[index] for index in range(TERMS)]
+    zero, one, two, ahead = [], [], [], []
+    for half in halves:
+        own = terms[3 + 9 * half : 12 + 9 * half]
+        zero.append(own[0:1])
+        one.append(own[1:3])
+        two.append(own[3:6])
+        ahead.append(
+            [known + own[5] * value for known, value in zip(own[6:9], values[half][:ITERS])]
+        )
+    multiples = [
+        over_halves([pair for half in halves for pair in zip(ahead[half], vector[half])]) + term
+        for vector, term in zip((zero, one, two), terms[:3])
+    ]
+    squares = jnp.full((ROWS, BLOCK), EPSILON, jnp.float32)
+    for half in halves:
+        beyond = values[half][ITERS]
+        for value in values[half][:ITERS]:
+            beyond = beyond - value * value
+        squares = squares + jnp.maximum(beyond, 0.0) * two[half][2] * two[half][2]
+        for index in range(ITERS):
+            value = ahead[half][index]
+            for multiple, vector in zip(multiples, (zero, one, two)):
+                if index < len(vector[half]):
+                    value = value - multiple * vector[half][index]
+            squares = squares + value * value
+    scale = lax.rsqrt(squares)
     basis_ref[:ITERS] = kept_ref[:ITERS]
-    basis_ref[ITERS] = rest * lax.rsqrt(squares)
+    for block in range(BLK_DEV):
+        span = slice(block * BLOCK, (block + 1) * BLOCK)
+        rest = kept_ref[ITERS, :, span]
+        for j in range(ITERS):
+            rest = rest - multiples[j] * kept_ref[j, :, span]
+        basis_ref[ITERS, :, span] = rest * scale
     place = 2 * (ITERS + 1)
-    whole = known_ref[...] + columns(
-        {place + index: value for index, value in enumerate(coeffs + [norm])}
-    )
+    coeffs = multiples[:-1] + [multiples[-1] + 0.5, jnp.sqrt(squares)]
+    whole = known_ref[...] + columns({place + index: value for index, value in enumerate(coeffs)})
     turned = whole.T
     for k in range(ITERS):
         hessenberg_ref[k] = turned[k * (ITERS + 1) : (k + 1) * (ITERS + 1), :]
@@ -387,26 +470,32 @@
     chips = devices // 2
     panels = sources.shape[2]
     total = 1.0 * panels * devices
-    shift = 1
-    same_core = [
-        [(2 * (chip + shift) + core) % devices for chip in range(chips)] for core in range(2)
+    shift = 5 % (chips // 2)
+    groups = [
+        [
+            2 * (side * (chips // 2) + (chip + shift) % (chips // 2)) + core
+            for chip in range(chips // 2)
+        ]
+        for side in range(2)
+        for core in range(2)
     ]
     mirror_rows = mirror.reshape(BLK_DEV, BLOCK)
     blocks = near_blocks[0]
-    vector = shaped(devices, ROWS, BLOCK)
-    chunk = shaped(chips, 2, ROWS, BLOCK)
+    everything = shaped(devices, ROWS, BLOCK)
+    vector = shaped(owners, ROWS, BLOCK)
+    chunk = shaped(chips // 2, 2, ROWS, BLOCK)
     tile = shaped(ROWS, BLOCK)
 
     def swapped(value, bits):
         return lax.ppermute(value, AXES, [(i, i ^ bits) for i in range(devices)])
 
     def exchanged(chunks):
-        return lax.all_to_all(chunks, AXES, 0, 0, axis_index_groups=same_core)
+        return lax.all_to_all(chunks, AXES, 0, 0, axis_index_groups=groups)
 
     chunks, mirror_rows, places = call(
         start_kernel,
         [
-            vector,
+            everything,
             shaped(*mirror_rows.shape, dtype=jnp.int32),
             shaped(2, *block_rows.shape, dtype=jnp.int32),
         ],
@@ -437,26 +526,28 @@
         name="middle",
     )(got, zero, coeff, *near_args)
     first_got, got = got, exchanged(chunks)
-    chunks, two, coeff, same, flip = call(
+    chunks, two, coeff, low, high = call(
         functools.partial(last_kernel, total, shift),
-        [shaped(devices, BLOCK), vector, tile, tile, tile], [VMEM] * 7,
-        name="last",
+        [shaped(devices, BLOCK), vector, tile, tile, tile], [VMEM] * 7, name="last",
     )(first_got, got, zero, one, coeff, *near_args)
     got = lax.all_to_all(chunks.reshape(devices, 1, BLOCK), AXES, 0, 0)
-    [theirs] = call(
-        pack_kernel, [shaped(2 * ITERS + 2, ROWS, BLOCK)], [VMEM] * 5, name="pack"
-    )(zero, one, two, coeff, flip)
-    kept, known, gram = call(
-        keep_kernel, [shaped(ITERS + 1, ROWS, panels), tile, tile], [VMEM] * 9, name="keep"
+    packed = shaped(PACKED, ROWS, BLOCK)
+    mine, theirs = call(pack_kernel, [packed, packed], [VMEM] * 6, name="pack")(
+        zero, one, two, coeff, low, high
+    )
+    kept, known, terms = call(
+        keep_kernel,
+        [shaped(ITERS + 1, ROWS, panels), tile, shaped(TERMS, ROWS, BLOCK)], [VMEM] * 5,
+        name="keep",
     )(
-        zero, one, two, coeff, same, swapped(theirs, 1), swapped(same, devices // 2),
-        swapped(flip, devices // 2 ^ 1), mirror_rows,
+        mine, swapped(theirs, 1), swapped(mine, devices // 2), swapped(theirs, devices // 2 ^ 1),
+        mirror_rows,
     )
     basis, hessenberg = call(
         functools.partial(final_kernel, total),
         [shaped(ITERS + 1, ROWS, panels), shaped(ITERS, ITERS + 1, ROWS)], [VMEM] * 4,
         name="final",
-    )(got.reshape(devices, BLOCK), kept, known, gram)
+    )(got.reshape(devices, BLOCK), kept, known, terms)
     return basis[:, None], hessenberg.transpose(2, 1, 0)
 
 

time: 51.3 us -> 48.5 us (0.945)
  blocking collectives: 19.8 us -> 17.3 us
  waiting for transfers between devices: 10.7 us -> 9.44 us
  Pallas kernels: 7.64 us -> 8.24 us
    all_to_all x2, blocking collectives: 19.8 us -> 17.3 us  [exchanged(): return lax.all_to_all(chunks, AXES, 0, 0, axis_index_groups=groups)]
    all_to_all x1, waiting for transfers between devices: 1.9 us -> 0.69 us  [on_device(): got = lax.all_to_all(chunks.reshape(devices, 1, BLOCK), AXES, 0, 0)]
    pallas_call x3, Pallas kernels: 1.79 us -> 2.61 us  [the longest x1 1.48 us: on_device(): call(start_kernel, [everything, shaped(*mirror_rows.shape, dtype=jnp.int3...]
  transfers between devices with their start and end apart: 7 -> 7, of which waited for: 5 -> 5; matrix products, arithmetic and copies ran while one was open for 0% -> 0% of each run, Pallas kernels for 5% -> 7%
where the time goes in v9:
time: 48.5 us; the launch traced here: 48.2 us
  blocking collectives  17.3 us (36%)
  starting transfers between devices  12.6 us (26%)
  waiting for transfers between devices  9.44 us (19%)
  Pallas kernels  8.24 us (17%)
  between operations  0.68 us (1%)
    all_to_all x2, blocking collectives, exchanged(): return lax.all_to_all(chunks, AXES, 0, 0, axis_index_groups=groups)  17.3 us
    all_to_all x1, starting transfers between devices, on_device(): got = lax.all_to_all(chunks, AXES, 0, 0)  6.96 us
    all_to_all x1, waiting for transfers between devices, on_device(): got = lax.all_to_all(chunks, AXES, 0, 0)  4.84 us
    ppermute x5, waiting for transfers between devices, swapped(): return lax.ppermute(value, AXES, [(i, i ^ bits) for i in range(devices)])  3.91 us
    ppermute x5, starting transfers between devices, swapped(): return lax.ppermute(value, AXES, [(i, i ^ bits) for i in range(devices)])  3.04 us
    all_to_all x1, starting transfers between devices, on_device(): got = lax.all_to_all(chunks.reshape(devices, 1, BLOCK), AXES, 0, 0)  2.56 us
    pallas_call x1, Pallas kernels, on_device(): call(prepare_kernel, [shaped(blocks.shape[0] // 2, 2 * BLOCK, 2 * BLOCK,...  2.12 us
    pallas_call x1, Pallas kernels, on_device(): call(start_kernel, [everything, shaped(*mirror_rows.shape, dtype=jnp.int3...  1.48 us
  transfers between devices with their start and end apart: 7, of which 5 were waited for; matrix products, arithmetic and copies ran while one was open for 0% of the time, Pallas kernels for 7%

profile of v9, /device:TPU:0, one launch (start us, length us, event | category | flops | bytes accessed | tf_op | source)
XLA Modules:
  0.0 48.2 jit_solution(15412474975530731879)
XLA Ops:
  0.6 1.5 %start.1 = (f32[32,8,128]{2,1,0:T(8,128)}, s32[2,128]{1,0:T(2,128)S(1)}, s32[2,1,32]{2,1,0:T(1,128)S(1)}) custom-call(f32[8,256]{1,0:T(8,128)} %bitcast.14, s32[2,128]{1,0:T(2,128)} %bitcast.15, s32[1,32]{1,0:T(1,128)} %rows_hbm.1, s32[1,32]{1,0:T(1,128)} %cols_hbm.1), custom_call_target="tpu_custom_call" | custom-call | tf_op jit(solution)/shard_map/start/pallas_call | solution.py:495
  2.1 0.5 %collective-permute-start = (bf16[32,128,128]{2,1,0:T(8,128)(2,1)}, bf16[32,128,128]{2,1,0:T(8,128)(2,1)S(1)}, u32[]{:S(2)}, u32[]{:S(2)}) collective-permute-start(bf16[32,128,128]{2,1,0:T(8,128)(2,1)} %bitcast.12), channel_id=1, source_target_pairs={{0,1},{1,0},{2,3},{3,2},{4,5},{5,4},{6,7},{7,6},{8,9},{9,8},{10,11... | collective-permute-start | bytes 3145736 | tf_op jit(solution)/shard_map/ppermute | solution.py:490
  2.6 7.0 %all-to-all-start = ((f32[32,8,128]{2,1,0:T(8,128)}), f32[32,8,128]{2,1,0:T(8,128)S(1)}, u32[]{:S(2)}, u32[]{:S(2)}) async-start(f32[32,8,128]{2,1,0:T(8,128)} %get-tuple-element.28), calls=%async_computation | async-start | bytes 262144 | tf_op jit(solution)/shard_map/all_to_all | solution.py:507
  9.6 0.3 collective-permute-start.1
  9.9 0.9 %collective-permute-done.1.other_places = s32[2,1,32]{2,1,0:T(1,128)S(1)} collective-permute-done((s32[2,1,32]{2,1,0:T(1,128)S(1)}, s32[2,1,32]{2,1,0:T(1,128)S(1)}, u32[]{:S(2)}, u32[]{:S(2)}) %collective-permute-start.1) | collective-permute-done | bytes 288 | tf_op jit(solution)/shard_map/ppermute | solution.py:490
  10.8 0.0 collective-permute-done.other_ref
  10.8 2.1 %prepare.1 = (bf16[16,256,256]{2,1,0:T(8,128)(2,1)S(1)}, bf16[512,128]{1,0:T(8,128)(2,1)S(1)}) custom-call(bf16[32,128,128]{2,1,0:T(8,128)(2,1)} %bitcast.13, bf16[32,128,128]{2,1,0:T(8,128)(2,1)S(1)} %collective-permute-done.other_ref, s32[2,1,32]{2,1,0:T(1,128)S(1)} %get-tuple-element.30.own_places, s32[2,1,32]{2,1,0:T(1,128)S(1)} %collective-permute-done.1.other_places), custom_call_target="tpu_custom_call" | custom-call | tf_op jit(solution)/shard_map/prepare/pallas_call | solution.py:509
  12.9 4.8 %all-to-all-done.got_ref = f32[32,8,128]{2,1,0:T(8,128)S(1)} async-done(((f32[32,8,128]{2,1,0:T(8,128)}), f32[32,8,128]{2,1,0:T(8,128)S(1)}, u32[]{:S(2)}, u32[]{:S(2)}) %all-to-all-start) | async-done | bytes 131104 | tf_op jit(solution)/shard_map/all_to_all | solution.py:507
  17.8 0.7 %first.1 = (f32[8,2,8,128]{3,2,1,0:T(8,128)S(1)}, f32[16,8,128]{2,1,0:T(8,128)S(1)}, f32[8,128]{1,0:T(8,128)S(1)}) custom-call(f32[32,8,128]{2,1,0:T(8,128)S(1)} %all-to-all-done.got_ref, bf16[512,128]{1,0:T(8,128)(2,1)S(1)} %get-tuple-element.31.pick_ref, bf16[16,256,256]{2,1,0:T(8,128)(2,1)S(1)} %get-tuple-element.32.weights_ref), custom_call_target="tpu_custom_call" | custom-call | tf_op jit(solution)/shard_map/first/pallas_call | solution.py:520
  18.5 8.6 %all_to_all.20.got_ref.first_got_ref = f32[8,2,8,128]{3,2,1,0:T(8,128)S(1)} all-to-all(f32[8,2,8,128]{3,2,1,0:T(8,128)S(1)} %get-tuple-element.33), channel_id=1, replica_groups={{10,12,14,0,2,4,6,8},{11,13,15,1,3,5,7,9},{26,28,30,16,18,20,22,24},{27..., dimensions={0} | all-to-all | bytes 131072 | tf_op jit(solution)/shard_map/all_to_all | solution.py:493
  27.1 0.7 %middle.1 = (f32[8,2,8,128]{3,2,1,0:T(8,128)S(1)}, f32[16,8,128]{2,1,0:T(8,128)S(1)}, f32[8,128]{1,0:T(8,128)S(1)}) custom-call(f32[8,2,8,128]{3,2,1,0:T(8,128)S(1)} %all_to_all.20.got_ref.first_got_ref, f32[16,8,128]{2,1,0:T(8,128)S(1)} %get-tuple-element.34.basis_ref.zero_ref, f32[8,128]{1,0:T(8,128)S(1)} %get-tuple-element.35.known_ref, ...), custom_call_target="tpu_custom_call" | custom-call | tf_op jit(solution)/shard_map/middle/pallas_call | solution.py:524
  27.8 8.6 %all_to_all.21.got_ref = f32[8,2,8,128]{3,2,1,0:T(8,128)S(1)} all-to-all(f32[8,2,8,128]{3,2,1,0:T(8,128)S(1)} %get-tuple-element.36), channel_id=1, replica_groups={{10,12,14,0,2,4,6,8},{11,13,15,1,3,5,7,9},{26,28,30,16,18,20,22,24},{27..., dimensions={0} | all-to-all | bytes 131072 | tf_op jit(solution)/shard_map/all_to_all | solution.py:493
  36.4 1.4 %last.1 = (f32[32,128]{1,0:T(8,128)}, f32[16,8,128]{2,1,0:T(8,128)S(1)}, f32[8,128]{1,0:T(8,128)S(1)}, f32[8,128]{1,0:T(8,128)S(1)}, f32[8,128]{1,0:T(8,128)S(1)}) custom-call(f32[8,2,8,128]{3,2,1,0:T(8,128)S(1)} %all_to_all.20.got_ref.first_got_ref, f32[8,2,8,128]{3,2,1,0:T(8,128)S(1)} %all_to_all.21.got_ref, ...), custom_call_target="tpu_custom_call" | custom-call | tf_op jit(solution)/shard_map/last/pallas_call | solution.py:529
  37.8 2.6 %all-to-all-start.3 = ((f32[32,1,128]{2,1,0:T(1,128)}), f32[32,1,128]{2,1,0:T(1,128)S(1)}, u32[]{:S(2)}, u32[]{:S(2)}) async-start(f32[32,1,128]{2,1,0:T(1,128)} %bitcast.4), calls=%async_computation.3 | async-start | bytes 32768 | tf_op jit(solution)/shard_map/all_to_all | solution.py:533
  40.4 1.8 %collective-permute-start.3 = (f32[5,8,128]{2,1,0:T(8,128)S(1)}, f32[5,8,128]{2,1,0:T(8,128)S(1)}, u32[]{:S(2)}, u32[]{:S(2)}) collective-permute-start(f32[5,8,128]{2,1,0:T(8,128)S(1)} %get-tuple-element.44.mine_ref), channel_id=1, source_target_pairs={{0,16},{1,17},{2,18},{3,19},{4,20},{5,21},{6,22},{7,23},{8,24},{9,... | collective-permute-start | bytes 61448 | tf_op jit(solution)/shard_map/ppermute | solution.py:490
  42.2 0.0 collective-permute-start.4
  42.2 0.4 collective-permute-start.2
  42.6 1.7 %collective-permute-done.3.across_ref = f32[5,8,128]{2,1,0:T(8,128)S(1)} collective-permute-done((f32[5,8,128]{2,1,0:T(8,128)S(1)}, f32[5,8,128]{2,1,0:T(8,128)S(1)}, u32[]{:S(2)}, u32[]{:S(2)}) %collective-permute-start.3) | collective-permute-done | bytes 20512 | tf_op jit(solution)/shard_map/ppermute | solution.py:490
  44.2 1.4 %collective-permute-done.4.flipped_ref = f32[5,8,128]{2,1,0:T(8,128)S(1)} collective-permute-done((f32[5,8,128]{2,1,0:T(8,128)S(1)}, f32[5,8,128]{2,1,0:T(8,128)S(1)}, u32[]{:S(2)}, u32[]{:S(2)}) %collective-permute-start.4) | collective-permute-done | bytes 20512 | tf_op jit(solution)/shard_map/ppermute | solution.py:490
  45.6 0.0 collective-permute-done.2.partner_ref
  45.6 1.1 %keep.1 = (f32[4,8,256]{2,1,0:T(8,128)S(1)}, f32[8,128]{1,0:T(8,128)S(1)}, f32[21,8,128]{2,1,0:T(8,128)S(1)}) custom-call(f32[5,8,128]{2,1,0:T(8,128)S(1)} %get-tuple-element.44.mine_ref, f32[5,8,128]{2,1,0:T(8,128)S(1)} %collective-permute-done.2.partner_ref, f32[5,8,128]{2,1,0:T(8,128)S(1)} %collective-permute-done.3.across_ref, ...), custom_call_target="tpu_custom_call" | custom-call | tf_op jit(solution)/shard_map/keep/pallas_call | solution.py:538
  46.7 0.7 %all-to-all-done.3 = f32[32,1,128]{2,1,0:T(1,128)S(1)} async-done(((f32[32,1,128]{2,1,0:T(1,128)}), f32[32,1,128]{2,1,0:T(1,128)S(1)}, u32[]{:S(2)}, u32[]{:S(2)}) %all-to-all-start.3) | async-done | bytes 16416 | tf_op jit(solution)/shard_map/all_to_all | solution.py:533
  47.4 0.8 %final.1 = (f32[4,8,256]{2,1,0:T(8,128)}, f32[3,4,8]{2,1,0:T(4,128)}) custom-call(f32[32,128]{1,0:T(8,128)S(1)} %bitcast.11, f32[4,8,256]{2,1,0:T(8,128)S(1)} %get-tuple-element.47.kept_ref, f32[8,128]{1,0:T(8,128)S(1)} %get-tuple-element.48.known_ref, f32[21,8,128]{2,1,0:T(8,128)S(1)} %get-tuple-element.49.terms_ref), custom_call_target="tpu_custom_call" | custom-call | tf_op jit(solution)/shard_map/final/pallas_call | solution.py:546
  (1 shorter events, 0.0 us)
Async XLA Ops:
  2.1 8.7 %collective-permute-start = (bf16[32,128,128]{2,1,0:T(8,128)(2,1)}, bf16[32,128,128]{2,1,0:T(8,128)(2,1)S(1)}, u32[]{:S(2)}, u32[]{:S(2)}) collective-permute-start(bf16[32,128,128]{2,1,0:T(8,128)(2,1)} %bitcast.12), channel_id=1, source_target_pairs={{0,1},{1,0},{2,3},{3,2},{4,5},{5,4},{6,7},{7,6},{8,9},{9,8},{10,11... | collective-permute-start | bytes 3145736 | tf_op jit(solution)/shard_map/ppermute | solution.py:490
  2.6 15.1 %all-to-all-start = ((f32[32,8,128]{2,1,0:T(8,128)}), f32[32,8,128]{2,1,0:T(8,128)S(1)}, u32[]{:S(2)}, u32[]{:S(2)}) async-start(f32[32,8,128]{2,1,0:T(8,128)} %get-tuple-element.28), calls=%async_computation | async-start | bytes 262144 | tf_op jit(solution)/shard_map/all_to_all | solution.py:507
  9.6 1.2 %collective-permute-start.1 = (s32[2,1,32]{2,1,0:T(1,128)S(1)}, s32[2,1,32]{2,1,0:T(1,128)S(1)}, u32[]{:S(2)}, u32[]{:S(2)}) collective-permute-start(s32[2,1,32]{2,1,0:T(1,128)S(1)} %get-tuple-element.30.own_places), channel_id=1, source_target_pairs={{0,1},{1,0},{2,3},{3,2},{4,5},{5,4},{6,7},{7,6},{8,9},{9,8},{10,11... | collective-permute-start | bytes 776 | tf_op jit(solution)/shard_map/ppermute | solution.py:490
  37.8 9.6 %all-to-all-start.3 = ((f32[32,1,128]{2,1,0:T(1,128)}), f32[32,1,128]{2,1,0:T(1,128)S(1)}, u32[]{:S(2)}, u32[]{:S(2)}) async-start(f32[32,1,128]{2,1,0:T(1,128)} %bitcast.4), calls=%async_computation.3 | async-start | bytes 32768 | tf_op jit(solution)/shard_map/all_to_all | solution.py:533
  40.4 3.9 %collective-permute-start.3 = (f32[5,8,128]{2,1,0:T(8,128)S(1)}, f32[5,8,128]{2,1,0:T(8,128)S(1)}, u32[]{:S(2)}, u32[]{:S(2)}) collective-permute-start(f32[5,8,128]{2,1,0:T(8,128)S(1)} %get-tuple-element.44.mine_ref), channel_id=1, source_target_pairs={{0,16},{1,17},{2,18},{3,19},{4,20},{5,21},{6,22},{7,23},{8,24},{9,... | collective-permute-start | bytes 61448 | tf_op jit(solution)/shard_map/ppermute | solution.py:490
  42.2 3.4 %collective-permute-start.4 = (f32[5,8,128]{2,1,0:T(8,128)S(1)}, f32[5,8,128]{2,1,0:T(8,128)S(1)}, u32[]{:S(2)}, u32[]{:S(2)}) collective-permute-start(f32[5,8,128]{2,1,0:T(8,128)S(1)} %get-tuple-element.45), channel_id=1, source_target_pairs={{0,17},{1,16},{2,19},{3,18},{4,21},{5,20},{6,23},{7,22},{8,25},{9,... | collective-permute-start | bytes 61448 | tf_op jit(solution)/shard_map/ppermute | solution.py:490
  42.2 3.4 %collective-permute-start.2 = (f32[5,8,128]{2,1,0:T(8,128)S(1)}, f32[5,8,128]{2,1,0:T(8,128)S(1)}, u32[]{:S(2)}, u32[]{:S(2)}) collective-permute-start(f32[5,8,128]{2,1,0:T(8,128)S(1)} %get-tuple-element.45), channel_id=1, source_target_pairs={{0,1},{1,0},{2,3},{3,2},{4,5},{5,4},{6,7},{7,6},{8,9},{9,8},{10,11... | collective-permute-start | bytes 61448 | tf_op jit(solution)/shard_map/ppermute | solution.py:490

commit v10 on v9

--- a/solution.py
+++ b/solution.py
@@ -258,6 +258,10 @@
     return sum(one * other for one, other in products)
 
 
+def squared(vector):
+    return over_halves([(value, value) for half in vector for value in half])
+
+
 def keep_kernel(mine_ref, partner_ref, across_ref, flipped_ref, mirror_ref, kept_ref, known_ref,
                 terms_ref):
     side, _, core = position()
@@ -288,12 +292,13 @@
     zero = [[start[half]] for half in halves]
     ahead = [[entry(half, 0, 0) * zero[half][0], entry(half, 1, 0) * zero[half][0]] for half in halves]
     short = [EPSILON / (length * length)]
-    multiple = over_halves([(ahead[half][0], zero[half][0]) for half in halves]) - 0.5 * short[0]
+    product = over_halves([(ahead[half][0], zero[half][0]) for half in halves])
+    multiple = product - 0.5 * short[0]
     rest = [[ahead[half][0] - multiple * zero[half][0], ahead[half][1]] for half in halves]
-    squares = over_halves([(value, value) for half in halves for value in rest[half]]) + EPSILON
+    squares = squared(rest) + EPSILON
     norms = [jnp.sqrt(squares)]
     one = [[value * lax.rsqrt(squares) for value in rest[half]] for half in halves]
-    heads = {(0, 0): multiple + 0.5, (1, 0): norms[0]}
+    heads = {(0, 0): product + 0.5 * squared(zero), (1, 0): norms[0]}
     short.append(EPSILON / squares)
     cross = heads[0, 0] * short[0] / norms[0]
     ahead = [
@@ -304,10 +309,10 @@
         ]
         for half in halves
     ]
+    product = over_halves([pair for half in halves for pair in zip(ahead[half], one[half])])
     multiples = [
         over_halves([(ahead[half][0], zero[half][0]) for half in halves]) + 0.5 * cross,
-        over_halves([pair for half in halves for pair in zip(ahead[half], one[half])])
-        - 0.5 * short[1],
+        product - 0.5 * short[1],
     ]
     rest = [
         [
@@ -317,10 +322,10 @@
         ]
         for half in halves
     ]
-    squares = over_halves([(value, value) for half in halves for value in rest[half]]) + EPSILON
+    squares = squared(rest) + EPSILON
     norms.append(jnp.sqrt(squares))
     two = [[value * lax.rsqrt(squares) for value in rest[half]] for half in halves]
-    heads.update({(0, 1): multiples[0], (1, 1): multiples[1] + 0.5, (2, 1): norms[1]})
+    heads.update({(0, 1): multiples[0], (1, 1): product + 0.5 * squared(one), (2, 1): norms[1]})
     short.append(EPSILON / squares)
     crosses = [
         (heads[0, 1] * short[0] - heads[1, 1] * cross) / norms[1],
@@ -407,10 +412,11 @@
         ahead.append(
             [known + own[5] * value for known, value in zip(own[6:9], values[half][:ITERS])]
         )
-    multiples = [
-        over_halves([pair for half in halves for pair in zip(ahead[half], vector[half])]) + term
-        for vector, term in zip((zero, one, two), terms[:3])
-    ]
+    products = [
+        over_halves([pair for half in halves for pair in zip(ahead[half], vector[half])])
+        for vector in (zero, one, two)
+    ]
+    multiples = [product + term for product, term in zip(products, terms[:3])]
     squares = jnp.full((ROWS, BLOCK), EPSILON, jnp.float32)
     for half in halves:
         beyond = values[half][ITERS]
@@ -432,7 +438,7 @@
             rest = rest - multiples[j] * kept_ref[j, :, span]
         basis_ref[ITERS, :, span] = rest * scale
     place = 2 * (ITERS + 1)
-    coeffs = multiples[:-1] + [multiples[-1] + 0.5, jnp.sqrt(squares)]
+    coeffs = multiples[:-1] + [products[-1] + 0.5 * squared(two), jnp.sqrt(squares)]
     whole = known_ref[...] + columns({place + index: value for index, value in enumerate(coeffs)})
     turned = whole.T
     for k in range(ITERS):

time: 48.5 us -> 48.5 us (level)
  no operation moved by 1% of the time
where the time goes in v10:
time: 48.5 us; the launch traced here: 48.2 us
  blocking collectives  17.3 us (36%)
  starting transfers between devices  12.6 us (26%)
  waiting for transfers between devices  9.44 us (19%)
  Pallas kernels  8.24 us (17%)
  between operations  0.68 us (1%)
    all_to_all x2, blocking collectives, exchanged(): return lax.all_to_all(chunks, AXES, 0, 0, axis_index_groups=groups)  17.3 us
    all_to_all x1, starting transfers between devices, on_device(): got = lax.all_to_all(chunks, AXES, 0, 0)  6.96 us
    all_to_all x1, waiting for transfers between devices, on_device(): got = lax.all_to_all(chunks, AXES, 0, 0)  4.84 us
    ppermute x5, waiting for transfers between devices, swapped(): return lax.ppermute(value, AXES, [(i, i ^ bits) for i in range(devices)])  3.91 us
    ppermute x5, starting transfers between devices, swapped(): return lax.ppermute(value, AXES, [(i, i ^ bits) for i in range(devices)])  3.04 us
    all_to_all x1, starting transfers between devices, on_device(): got = lax.all_to_all(chunks.reshape(devices, 1, BLOCK), AXES, 0, 0)  2.56 us
    pallas_call x1, Pallas kernels, on_device(): call(prepare_kernel, [shaped(blocks.shape[0] // 2, 2 * BLOCK, 2 * BLOCK,...  2.12 us
    pallas_call x1, Pallas kernels, on_device(): call(start_kernel, [everything, shaped(*mirror_rows.shape, dtype=jnp.int3...  1.48 us
  transfers between devices with their start and end apart: 7, of which 5 were waited for; matrix products, arithmetic and copies ran while one was open for 0% of the time, Pallas kernels for 7%

profile of v10, /device:TPU:0, one launch (start us, length us, event | category | flops | bytes accessed | tf_op | source)
XLA Modules:
  0.0 48.2 jit_solution(17036742338004617838)
XLA Ops:
  0.6 1.5 %start.1 = (f32[32,8,128]{2,1,0:T(8,128)}, s32[2,128]{1,0:T(2,128)S(1)}, s32[2,1,32]{2,1,0:T(1,128)S(1)}) custom-call(f32[8,256]{1,0:T(8,128)} %bitcast.14, s32[2,128]{1,0:T(2,128)} %bitcast.15, s32[1,32]{1,0:T(1,128)} %rows_hbm.1, s32[1,32]{1,0:T(1,128)} %cols_hbm.1), custom_call_target="tpu_custom_call" | custom-call | tf_op jit(solution)/shard_map/start/pallas_call | solution.py:501
  2.1 0.5 %collective-permute-start = (bf16[32,128,128]{2,1,0:T(8,128)(2,1)}, bf16[32,128,128]{2,1,0:T(8,128)(2,1)S(1)}, u32[]{:S(2)}, u32[]{:S(2)}) collective-permute-start(bf16[32,128,128]{2,1,0:T(8,128)(2,1)} %bitcast.12), channel_id=1, source_target_pairs={{0,1},{1,0},{2,3},{3,2},{4,5},{5,4},{6,7},{7,6},{8,9},{9,8},{10,11... | collective-permute-start | bytes 3145736 | tf_op jit(solution)/shard_map/ppermute | solution.py:496
  2.6 7.0 %all-to-all-start = ((f32[32,8,128]{2,1,0:T(8,128)}), f32[32,8,128]{2,1,0:T(8,128)S(1)}, u32[]{:S(2)}, u32[]{:S(2)}) async-start(f32[32,8,128]{2,1,0:T(8,128)} %get-tuple-element.28), calls=%async_computation | async-start | bytes 262144 | tf_op jit(solution)/shard_map/all_to_all | solution.py:513
  9.6 0.3 collective-permute-start.1
  9.9 0.9 %collective-permute-done.1.other_places = s32[2,1,32]{2,1,0:T(1,128)S(1)} collective-permute-done((s32[2,1,32]{2,1,0:T(1,128)S(1)}, s32[2,1,32]{2,1,0:T(1,128)S(1)}, u32[]{:S(2)}, u32[]{:S(2)}) %collective-permute-start.1) | collective-permute-done | bytes 288 | tf_op jit(solution)/shard_map/ppermute | solution.py:496
  10.8 0.0 collective-permute-done.other_ref
  10.8 2.1 %prepare.1 = (bf16[16,256,256]{2,1,0:T(8,128)(2,1)S(1)}, bf16[512,128]{1,0:T(8,128)(2,1)S(1)}) custom-call(bf16[32,128,128]{2,1,0:T(8,128)(2,1)} %bitcast.13, bf16[32,128,128]{2,1,0:T(8,128)(2,1)S(1)} %collective-permute-done.other_ref, s32[2,1,32]{2,1,0:T(1,128)S(1)} %get-tuple-element.30.own_places, s32[2,1,32]{2,1,0:T(1,128)S(1)} %collective-permute-done.1.other_places), custom_call_target="tpu_custom_call" | custom-call | tf_op jit(solution)/shard_map/prepare/pallas_call | solution.py:515
  12.9 4.8 %all-to-all-done.got_ref = f32[32,8,128]{2,1,0:T(8,128)S(1)} async-done(((f32[32,8,128]{2,1,0:T(8,128)}), f32[32,8,128]{2,1,0:T(8,128)S(1)}, u32[]{:S(2)}, u32[]{:S(2)}) %all-to-all-start) | async-done | bytes 131104 | tf_op jit(solution)/shard_map/all_to_all | solution.py:513
  17.8 0.7 %first.1 = (f32[8,2,8,128]{3,2,1,0:T(8,128)S(1)}, f32[16,8,128]{2,1,0:T(8,128)S(1)}, f32[8,128]{1,0:T(8,128)S(1)}) custom-call(f32[32,8,128]{2,1,0:T(8,128)S(1)} %all-to-all-done.got_ref, bf16[512,128]{1,0:T(8,128)(2,1)S(1)} %get-tuple-element.31.pick_ref, bf16[16,256,256]{2,1,0:T(8,128)(2,1)S(1)} %get-tuple-element.32.weights_ref), custom_call_target="tpu_custom_call" | custom-call | tf_op jit(solution)/shard_map/first/pallas_call | solution.py:526
  18.5 8.6 %all_to_all.20.got_ref.first_got_ref = f32[8,2,8,128]{3,2,1,0:T(8,128)S(1)} all-to-all(f32[8,2,8,128]{3,2,1,0:T(8,128)S(1)} %get-tuple-element.33), channel_id=1, replica_groups={{10,12,14,0,2,4,6,8},{11,13,15,1,3,5,7,9},{26,28,30,16,18,20,22,24},{27..., dimensions={0} | all-to-all | bytes 131072 | tf_op jit(solution)/shard_map/all_to_all | solution.py:499
  27.1 0.7 %middle.1 = (f32[8,2,8,128]{3,2,1,0:T(8,128)S(1)}, f32[16,8,128]{2,1,0:T(8,128)S(1)}, f32[8,128]{1,0:T(8,128)S(1)}) custom-call(f32[8,2,8,128]{3,2,1,0:T(8,128)S(1)} %all_to_all.20.got_ref.first_got_ref, f32[16,8,128]{2,1,0:T(8,128)S(1)} %get-tuple-element.34.basis_ref.zero_ref, f32[8,128]{1,0:T(8,128)S(1)} %get-tuple-element.35.known_ref, ...), custom_call_target="tpu_custom_call" | custom-call | tf_op jit(solution)/shard_map/middle/pallas_call | solution.py:530
  27.8 8.6 %all_to_all.21.got_ref = f32[8,2,8,128]{3,2,1,0:T(8,128)S(1)} all-to-all(f32[8,2,8,128]{3,2,1,0:T(8,128)S(1)} %get-tuple-element.36), channel_id=1, replica_groups={{10,12,14,0,2,4,6,8},{11,13,15,1,3,5,7,9},{26,28,30,16,18,20,22,24},{27..., dimensions={0} | all-to-all | bytes 131072 | tf_op jit(solution)/shard_map/all_to_all | solution.py:499
  36.4 1.4 %last.1 = (f32[32,128]{1,0:T(8,128)}, f32[16,8,128]{2,1,0:T(8,128)S(1)}, f32[8,128]{1,0:T(8,128)S(1)}, f32[8,128]{1,0:T(8,128)S(1)}, f32[8,128]{1,0:T(8,128)S(1)}) custom-call(f32[8,2,8,128]{3,2,1,0:T(8,128)S(1)} %all_to_all.20.got_ref.first_got_ref, f32[8,2,8,128]{3,2,1,0:T(8,128)S(1)} %all_to_all.21.got_ref, ...), custom_call_target="tpu_custom_call" | custom-call | tf_op jit(solution)/shard_map/last/pallas_call | solution.py:535
  37.8 2.6 %all-to-all-start.3 = ((f32[32,1,128]{2,1,0:T(1,128)}), f32[32,1,128]{2,1,0:T(1,128)S(1)}, u32[]{:S(2)}, u32[]{:S(2)}) async-start(f32[32,1,128]{2,1,0:T(1,128)} %bitcast.4), calls=%async_computation.3 | async-start | bytes 32768 | tf_op jit(solution)/shard_map/all_to_all | solution.py:539
  40.4 1.8 %collective-permute-start.3 = (f32[5,8,128]{2,1,0:T(8,128)S(1)}, f32[5,8,128]{2,1,0:T(8,128)S(1)}, u32[]{:S(2)}, u32[]{:S(2)}) collective-permute-start(f32[5,8,128]{2,1,0:T(8,128)S(1)} %get-tuple-element.44.mine_ref), channel_id=1, source_target_pairs={{0,16},{1,17},{2,18},{3,19},{4,20},{5,21},{6,22},{7,23},{8,24},{9,... | collective-permute-start | bytes 61448 | tf_op jit(solution)/shard_map/ppermute | solution.py:496
  42.2 0.0 collective-permute-start.4
  42.2 0.4 collective-permute-start.2
  42.6 1.7 %collective-permute-done.3.across_ref = f32[5,8,128]{2,1,0:T(8,128)S(1)} collective-permute-done((f32[5,8,128]{2,1,0:T(8,128)S(1)}, f32[5,8,128]{2,1,0:T(8,128)S(1)}, u32[]{:S(2)}, u32[]{:S(2)}) %collective-permute-start.3) | collective-permute-done | bytes 20512 | tf_op jit(solution)/shard_map/ppermute | solution.py:496
  44.2 1.4 %collective-permute-done.4.flipped_ref = f32[5,8,128]{2,1,0:T(8,128)S(1)} collective-permute-done((f32[5,8,128]{2,1,0:T(8,128)S(1)}, f32[5,8,128]{2,1,0:T(8,128)S(1)}, u32[]{:S(2)}, u32[]{:S(2)}) %collective-permute-start.4) | collective-permute-done | bytes 20512 | tf_op jit(solution)/shard_map/ppermute | solution.py:496
  45.6 0.0 collective-permute-done.2.partner_ref
  45.6 1.1 %keep.1 = (f32[4,8,256]{2,1,0:T(8,128)S(1)}, f32[8,128]{1,0:T(8,128)S(1)}, f32[21,8,128]{2,1,0:T(8,128)S(1)}) custom-call(f32[5,8,128]{2,1,0:T(8,128)S(1)} %get-tuple-element.44.mine_ref, f32[5,8,128]{2,1,0:T(8,128)S(1)} %collective-permute-done.2.partner_ref, f32[5,8,128]{2,1,0:T(8,128)S(1)} %collective-permute-done.3.across_ref, ...), custom_call_target="tpu_custom_call" | custom-call | tf_op jit(solution)/shard_map/keep/pallas_call | solution.py:544
  46.7 0.7 %all-to-all-done.3 = f32[32,1,128]{2,1,0:T(1,128)S(1)} async-done(((f32[32,1,128]{2,1,0:T(1,128)}), f32[32,1,128]{2,1,0:T(1,128)S(1)}, u32[]{:S(2)}, u32[]{:S(2)}) %all-to-all-start.3) | async-done | bytes 16416 | tf_op jit(solution)/shard_map/all_to_all | solution.py:539
  47.4 0.8 %final.1 = (f32[4,8,256]{2,1,0:T(8,128)}, f32[3,4,8]{2,1,0:T(4,128)}) custom-call(f32[32,128]{1,0:T(8,128)S(1)} %bitcast.11, f32[4,8,256]{2,1,0:T(8,128)S(1)} %get-tuple-element.47.kept_ref, f32[8,128]{1,0:T(8,128)S(1)} %get-tuple-element.48.known_ref, f32[21,8,128]{2,1,0:T(8,128)S(1)} %get-tuple-element.49.terms_ref), custom_call_target="tpu_custom_call" | custom-call | tf_op jit(solution)/shard_map/final/pallas_call | solution.py:552
  (1 shorter events, 0.0 us)
Async XLA Ops:
  2.1 8.7 %collective-permute-start = (bf16[32,128,128]{2,1,0:T(8,128)(2,1)}, bf16[32,128,128]{2,1,0:T(8,128)(2,1)S(1)}, u32[]{:S(2)}, u32[]{:S(2)}) collective-permute-start(bf16[32,128,128]{2,1,0:T(8,128)(2,1)} %bitcast.12), channel_id=1, source_target_pairs={{0,1},{1,0},{2,3},{3,2},{4,5},{5,4},{6,7},{7,6},{8,9},{9,8},{10,11... | collective-permute-start | bytes 3145736 | tf_op jit(solution)/shard_map/ppermute | solution.py:496
  2.6 15.1 %all-to-all-start = ((f32[32,8,128]{2,1,0:T(8,128)}), f32[32,8,128]{2,1,0:T(8,128)S(1)}, u32[]{:S(2)}, u32[]{:S(2)}) async-start(f32[32,8,128]{2,1,0:T(8,128)} %get-tuple-element.28), calls=%async_computation | async-start | bytes 262144 | tf_op jit(solution)/shard_map/all_to_all | solution.py:513
  9.6 1.2 %collective-permute-start.1 = (s32[2,1,32]{2,1,0:T(1,128)S(1)}, s32[2,1,32]{2,1,0:T(1,128)S(1)}, u32[]{:S(2)}, u32[]{:S(2)}) collective-permute-start(s32[2,1,32]{2,1,0:T(1,128)S(1)} %get-tuple-element.30.own_places), channel_id=1, source_target_pairs={{0,1},{1,0},{2,3},{3,2},{4,5},{5,4},{6,7},{7,6},{8,9},{9,8},{10,11... | collective-permute-start | bytes 776 | tf_op jit(solution)/shard_map/ppermute | solution.py:496
  37.8 9.6 %all-to-all-start.3 = ((f32[32,1,128]{2,1,0:T(1,128)}), f32[32,1,128]{2,1,0:T(1,128)S(1)}, u32[]{:S(2)}, u32[]{:S(2)}) async-start(f32[32,1,128]{2,1,0:T(1,128)} %bitcast.4), calls=%async_computation.3 | async-start | bytes 32768 | tf_op jit(solution)/shard_map/all_to_all | solution.py:539
  40.4 3.9 %collective-permute-start.3 = (f32[5,8,128]{2,1,0:T(8,128)S(1)}, f32[5,8,128]{2,1,0:T(8,128)S(1)}, u32[]{:S(2)}, u32[]{:S(2)}) collective-permute-start(f32[5,8,128]{2,1,0:T(8,128)S(1)} %get-tuple-element.44.mine_ref), channel_id=1, source_target_pairs={{0,16},{1,17},{2,18},{3,19},{4,20},{5,21},{6,22},{7,23},{8,24},{9,... | collective-permute-start | bytes 61448 | tf_op jit(solution)/shard_map/ppermute | solution.py:496
  42.2 3.4 %collective-permute-start.4 = (f32[5,8,128]{2,1,0:T(8,128)S(1)}, f32[5,8,128]{2,1,0:T(8,128)S(1)}, u32[]{:S(2)}, u32[]{:S(2)}) collective-permute-start(f32[5,8,128]{2,1,0:T(8,128)S(1)} %get-tuple-element.45), channel_id=1, source_target_pairs={{0,17},{1,16},{2,19},{3,18},{4,21},{5,20},{6,23},{7,22},{8,25},{9,... | collective-permute-start | bytes 61448 | tf_op jit(solution)/shard_map/ppermute | solution.py:496
  42.2 3.4 %collective-permute-start.2 = (f32[5,8,128]{2,1,0:T(8,128)S(1)}, f32[5,8,128]{2,1,0:T(8,128)S(1)}, u32[]{:S(2)}, u32[]{:S(2)}) collective-permute-start(f32[5,8,128]{2,1,0:T(8,128)S(1)} %get-tuple-element.45), channel_id=1, source_target_pairs={{0,1},{1,0},{2,3},{3,2},{4,5},{5,4},{6,7},{7,6},{8,9},{9,8},{10,11... | collective-permute-start | bytes 61448 | tf_op jit(solution)/shard_map/ppermute | solution.py:496

commit v11 on v10

--- a/solution.py
+++ b/solution.py
@@ -86,11 +86,13 @@
     chips = chunk_ref.shape[0] // 2
 
     def store(chip, carry):
-        chunk_ref[2 * chip] = tiles[0]
-        chunk_ref[2 * chip + 1] = tiles[1]
+        chunk_ref[2 * chip + 1] = tiles[0]
+        chunk_ref[2 * chip + 2] = tiles[1]
         return carry
 
-    lax.fori_loop(0, chips, store, 0, unroll=chips <= 32)
+    chunk_ref[0] = tiles[0]
+    lax.fori_loop(0, chips - 1, store, 0, unroll=chips <= 32)
+    chunk_ref[2 * chips - 1] = tiles[1]
 
 
 def prepare_kernel(own_hbm, other_ref, own_places, other_places, weights_ref, pick_ref, own_ref,
@@ -165,8 +167,9 @@
 def first_kernel(total, got_ref, pick_ref, weights_ref, chunk_ref, basis_ref, coeff_ref):
     side, _, _ = position()
     owners = got_ref.shape[0] // 2
-    port = got_ref[:owners]
-    star = got_ref[owners:]
+    last = 2 * owners - 1
+    port = got_ref[1 : owners + 1]
+    star = jnp.concatenate([got_ref[owners + 1 : last], got_ref[:1], got_ref[last:]], axis=0)
     half = jnp.where(side == 0, port + star, port - star)
     tiles = near(half, pick_ref, weights_ref)
     squares = per_rhs(jnp.sum(port * port + star * star, axis=0)) * (1.0 / total) + EPSILON
@@ -379,16 +382,19 @@
     inner = 0.5 / total
     got = got_ref[...]
     devices = got.shape[0]
-    even = iota((ROWS, BLOCK), 0) % 2 == 0
+    place = iota(got.shape, 0)
+    device = jnp.where(
+        place == 0, devices - 2, jnp.where(place == devices - 1, devices - 1, place - 1)
+    )
     rhs = iota((ROWS, BLOCK), 0)
     lane = iota((ROWS, BLOCK), 1)
     halves = range(2)
     values = []
     for half in halves:
-        rows = got[half * devices // 2 : (half + 1) * devices // 2]
-        sums = jnp.sum(rows.reshape(-1, ROWS, BLOCK), axis=0)
-        lower = jnp.sum(jnp.where(even, sums, 0.0), axis=0, keepdims=True)
-        upper = jnp.sum(jnp.where(even, 0.0, sums), axis=0, keepdims=True)
+        here = (device >= devices // 2) if half == 1 else (device < devices // 2)
+        even = device % 2 == 0
+        lower = jnp.sum(jnp.where(here & even, got, 0.0), axis=0, keepdims=True)
+        upper = jnp.sum(jnp.where(here & ~even, got, 0.0), axis=0, keepdims=True)
         spots = jnp.where(rhs < HALF_RHS, lower, upper) * inner
         values.append(
             [
@@ -485,6 +491,7 @@
         for side in range(2)
         for core in range(2)
     ]
+    listed = [[devices - 2, *range(devices - 2), devices - 1]]
     mirror_rows = mirror.reshape(BLK_DEV, BLOCK)
     blocks = near_blocks[0]
     everything = shaped(devices, ROWS, BLOCK)
@@ -510,7 +517,7 @@
         name="start",
     )(in_hbm(sources[0]), in_hbm(mirror_rows), in_hbm(block_rows), in_hbm(block_cols))
     chunks, blocks = lax.optimization_barrier((chunks, blocks))
-    got = lax.all_to_all(chunks, AXES, 0, 0)
+    got = lax.all_to_all(chunks, AXES, 0, 0, axis_index_groups=listed)
     other_blocks = swapped(blocks, 1)
     weights, pick = call(
         prepare_kernel,
@@ -536,7 +543,9 @@
         functools.partial(last_kernel, total, shift),
         [shaped(devices, BLOCK), vector, tile, tile, tile], [VMEM] * 7, name="last",
     )(first_got, got, zero, one, coeff, *near_args)
-    got = lax.all_to_all(chunks.reshape(devices, 1, BLOCK), AXES, 0, 0)
+    got = lax.all_to_all(
+        chunks.reshape(devices, 1, BLOCK), AXES, 0, 0, axis_index_groups=listed
+    )
     packed = shaped(PACKED, ROWS, BLOCK)
     mine, theirs = call(pack_kernel, [packed, packed], [VMEM] * 6, name="pack")(
         zero, one, two, coeff, low, high

time: 48.5 us -> 48.2 us (level)
  waiting for transfers between devices: 9.44 us -> 8.74 us
    all_to_all x2, waiting for transfers between devices: 5.52 us -> 4.82 us  [the longest x1 4.18 us: on_device(): got = lax.all_to_all(chunks, AXES, 0, 0, axis_index_groups=listed)]
where the time goes in v11:
time: 48.2 us; the launch traced here: 47.8 us
  blocking collectives  17.5 us (36%)
  starting transfers between devices  12.7 us (26%)
  waiting for transfers between devices  8.74 us (18%)
  Pallas kernels  8.25 us (17%)
  between operations  0.68 us (1%)
    all_to_all x2, blocking collectives, exchanged(): return lax.all_to_all(chunks, AXES, 0, 0, axis_index_groups=groups)  17.5 us
    all_to_all x1, starting transfers between devices, on_device(): got = lax.all_to_all(chunks, AXES, 0, 0, axis_index_groups=listed)  6.96 us
    all_to_all x1, waiting for transfers between devices, on_device(): got = lax.all_to_all(chunks, AXES, 0, 0, axis_index_groups=listed)  4.18 us
    ppermute x5, waiting for transfers between devices, swapped(): return lax.ppermute(value, AXES, [(i, i ^ bits) for i in range(devices)])  3.92 us
    ppermute x5, starting transfers between devices, swapped(): return lax.ppermute(value, AXES, [(i, i ^ bits) for i in range(devices)])  3.04 us
    all_to_all x1, starting transfers between devices, on_device(): lax.all_to_all(chunks.reshape(devices, 1, BLOCK), AXES, 0, 0, axis_index_...  2.66 us
    pallas_call x1, Pallas kernels, on_device(): call(prepare_kernel, [shaped(blocks.shape[0] // 2, 2 * BLOCK, 2 * BLOCK,...  2.12 us
    pallas_call x1, Pallas kernels, on_device(): call(start_kernel, [everything, shaped(*mirror_rows.shape, dtype=jnp.int3...  1.48 us
  transfers between devices with their start and end apart: 7, of which 5 were waited for; matrix products, arithmetic and copies ran while one was open for 0% of the time, Pallas kernels for 7%

profile of v11, /device:TPU:0, one launch (start us, length us, event | category | flops | bytes accessed | tf_op | source)
XLA Modules:
  0.0 47.8 jit_solution(18052300729699212950)
XLA Ops:
  0.6 1.5 %start.1 = (f32[32,8,128]{2,1,0:T(8,128)}, s32[2,128]{1,0:T(2,128)S(1)}, s32[2,1,32]{2,1,0:T(1,128)S(1)}) custom-call(f32[8,256]{1,0:T(8,128)} %bitcast.14, s32[2,128]{1,0:T(2,128)} %bitcast.15, s32[1,32]{1,0:T(1,128)} %rows_hbm.1, s32[1,32]{1,0:T(1,128)} %cols_hbm.1), custom_call_target="tpu_custom_call" | custom-call | tf_op jit(solution)/shard_map/start/pallas_call | solution.py:508
  2.1 0.5 %collective-permute-start = (bf16[32,128,128]{2,1,0:T(8,128)(2,1)}, bf16[32,128,128]{2,1,0:T(8,128)(2,1)S(1)}, u32[]{:S(2)}, u32[]{:S(2)}) collective-permute-start(bf16[32,128,128]{2,1,0:T(8,128)(2,1)} %bitcast.12), channel_id=1, source_target_pairs={{0,1},{1,0},{2,3},{3,2},{4,5},{5,4},{6,7},{7,6},{8,9},{9,8},{10,11... | collective-permute-start | bytes 3145736 | tf_op jit(solution)/shard_map/ppermute | solution.py:503
  2.6 7.0 %all-to-all-start = ((f32[32,8,128]{2,1,0:T(8,128)}), f32[32,8,128]{2,1,0:T(8,128)S(1)}, u32[]{:S(2)}, u32[]{:S(2)}) async-start(f32[32,8,128]{2,1,0:T(8,128)} %get-tuple-element.28), calls=%async_computation | async-start | bytes 262144 | tf_op jit(solution)/shard_map/all_to_all | solution.py:520
  9.6 0.3 collective-permute-start.1
  9.9 0.9 %collective-permute-done.1.other_places = s32[2,1,32]{2,1,0:T(1,128)S(1)} collective-permute-done((s32[2,1,32]{2,1,0:T(1,128)S(1)}, s32[2,1,32]{2,1,0:T(1,128)S(1)}, u32[]{:S(2)}, u32[]{:S(2)}) %collective-permute-start.1) | collective-permute-done | bytes 288 | tf_op jit(solution)/shard_map/ppermute | solution.py:503
  10.8 0.0 collective-permute-done.other_ref
  10.8 2.1 %prepare.1 = (bf16[16,256,256]{2,1,0:T(8,128)(2,1)S(1)}, bf16[512,128]{1,0:T(8,128)(2,1)S(1)}) custom-call(bf16[32,128,128]{2,1,0:T(8,128)(2,1)} %bitcast.13, bf16[32,128,128]{2,1,0:T(8,128)(2,1)S(1)} %collective-permute-done.other_ref, s32[2,1,32]{2,1,0:T(1,128)S(1)} %get-tuple-element.30.own_places, s32[2,1,32]{2,1,0:T(1,128)S(1)} %collective-permute-done.1.other_places), custom_call_target="tpu_custom_call" | custom-call | tf_op jit(solution)/shard_map/prepare/pallas_call | solution.py:522
  12.9 4.2 %all-to-all-done.got_ref = f32[32,8,128]{2,1,0:T(8,128)S(1)} async-done(((f32[32,8,128]{2,1,0:T(8,128)}), f32[32,8,128]{2,1,0:T(8,128)S(1)}, u32[]{:S(2)}, u32[]{:S(2)}) %all-to-all-start) | async-done | bytes 131104 | tf_op jit(solution)/shard_map/all_to_all | solution.py:520
  17.1 0.7 %first.1 = (f32[8,2,8,128]{3,2,1,0:T(8,128)S(1)}, f32[16,8,128]{2,1,0:T(8,128)S(1)}, f32[8,128]{1,0:T(8,128)S(1)}) custom-call(f32[32,8,128]{2,1,0:T(8,128)S(1)} %all-to-all-done.got_ref, bf16[512,128]{1,0:T(8,128)(2,1)S(1)} %get-tuple-element.31.pick_ref, bf16[16,256,256]{2,1,0:T(8,128)(2,1)S(1)} %get-tuple-element.32.weights_ref), custom_call_target="tpu_custom_call" | custom-call | tf_op jit(solution)/shard_map/first/pallas_call | solution.py:533
  17.8 8.9 %all_to_all.20.got_ref.first_got_ref = f32[8,2,8,128]{3,2,1,0:T(8,128)S(1)} all-to-all(f32[8,2,8,128]{3,2,1,0:T(8,128)S(1)} %get-tuple-element.33), channel_id=1, replica_groups={{10,12,14,0,2,4,6,8},{11,13,15,1,3,5,7,9},{26,28,30,16,18,20,22,24},{27..., dimensions={0} | all-to-all | bytes 131072 | tf_op jit(solution)/shard_map/all_to_all | solution.py:506
  26.7 0.7 %middle.1 = (f32[8,2,8,128]{3,2,1,0:T(8,128)S(1)}, f32[16,8,128]{2,1,0:T(8,128)S(1)}, f32[8,128]{1,0:T(8,128)S(1)}) custom-call(f32[8,2,8,128]{3,2,1,0:T(8,128)S(1)} %all_to_all.20.got_ref.first_got_ref, f32[16,8,128]{2,1,0:T(8,128)S(1)} %get-tuple-element.34.basis_ref.zero_ref, f32[8,128]{1,0:T(8,128)S(1)} %get-tuple-element.35.known_ref, ...), custom_call_target="tpu_custom_call" | custom-call | tf_op jit(solution)/shard_map/middle/pallas_call | solution.py:537
  27.4 8.6 %all_to_all.21.got_ref = f32[8,2,8,128]{3,2,1,0:T(8,128)S(1)} all-to-all(f32[8,2,8,128]{3,2,1,0:T(8,128)S(1)} %get-tuple-element.36), channel_id=1, replica_groups={{10,12,14,0,2,4,6,8},{11,13,15,1,3,5,7,9},{26,28,30,16,18,20,22,24},{27..., dimensions={0} | all-to-all | bytes 131072 | tf_op jit(solution)/shard_map/all_to_all | solution.py:506
  36.0 1.4 %last.1 = (f32[32,128]{1,0:T(8,128)}, f32[16,8,128]{2,1,0:T(8,128)S(1)}, f32[8,128]{1,0:T(8,128)S(1)}, f32[8,128]{1,0:T(8,128)S(1)}, f32[8,128]{1,0:T(8,128)S(1)}) custom-call(f32[8,2,8,128]{3,2,1,0:T(8,128)S(1)} %all_to_all.20.got_ref.first_got_ref, f32[8,2,8,128]{3,2,1,0:T(8,128)S(1)} %all_to_all.21.got_ref, ...), custom_call_target="tpu_custom_call" | custom-call | tf_op jit(solution)/shard_map/last/pallas_call | solution.py:542
  37.4 2.7 %all-to-all-start.3 = ((f32[32,1,128]{2,1,0:T(1,128)}), f32[32,1,128]{2,1,0:T(1,128)S(1)}, u32[]{:S(2)}, u32[]{:S(2)}) async-start(f32[32,1,128]{2,1,0:T(1,128)} %bitcast.4), calls=%async_computation.3 | async-start | bytes 32768 | tf_op jit(solution)/shard_map/all_to_all | solution.py:546
  40.1 1.8 %collective-permute-start.3 = (f32[5,8,128]{2,1,0:T(8,128)S(1)}, f32[5,8,128]{2,1,0:T(8,128)S(1)}, u32[]{:S(2)}, u32[]{:S(2)}) collective-permute-start(f32[5,8,128]{2,1,0:T(8,128)S(1)} %get-tuple-element.44.mine_ref), channel_id=1, source_target_pairs={{0,16},{1,17},{2,18},{3,19},{4,20},{5,21},{6,22},{7,23},{8,24},{9,... | collective-permute-start | bytes 61448 | tf_op jit(solution)/shard_map/ppermute | solution.py:503
  41.9 0.0 collective-permute-start.4
  41.9 0.4 collective-permute-start.2
  42.3 1.7 %collective-permute-done.3.across_ref = f32[5,8,128]{2,1,0:T(8,128)S(1)} collective-permute-done((f32[5,8,128]{2,1,0:T(8,128)S(1)}, f32[5,8,128]{2,1,0:T(8,128)S(1)}, u32[]{:S(2)}, u32[]{:S(2)}) %collective-permute-start.3) | collective-permute-done | bytes 20512 | tf_op jit(solution)/shard_map/ppermute | solution.py:503
  43.9 1.4 %collective-permute-done.4.flipped_ref = f32[5,8,128]{2,1,0:T(8,128)S(1)} collective-permute-done((f32[5,8,128]{2,1,0:T(8,128)S(1)}, f32[5,8,128]{2,1,0:T(8,128)S(1)}, u32[]{:S(2)}, u32[]{:S(2)}) %collective-permute-start.4) | collective-permute-done | bytes 20512 | tf_op jit(solution)/shard_map/ppermute | solution.py:503
  45.3 0.0 collective-permute-done.2.partner_ref
  45.3 1.1 %keep.1 = (f32[4,8,256]{2,1,0:T(8,128)S(1)}, f32[8,128]{1,0:T(8,128)S(1)}, f32[21,8,128]{2,1,0:T(8,128)S(1)}) custom-call(f32[5,8,128]{2,1,0:T(8,128)S(1)} %get-tuple-element.44.mine_ref, f32[5,8,128]{2,1,0:T(8,128)S(1)} %collective-permute-done.2.partner_ref, f32[5,8,128]{2,1,0:T(8,128)S(1)} %collective-permute-done.3.across_ref, ...), custom_call_target="tpu_custom_call" | custom-call | tf_op jit(solution)/shard_map/keep/pallas_call | solution.py:553
  46.4 0.6 %all-to-all-done.3 = f32[32,1,128]{2,1,0:T(1,128)S(1)} async-done(((f32[32,1,128]{2,1,0:T(1,128)}), f32[32,1,128]{2,1,0:T(1,128)S(1)}, u32[]{:S(2)}, u32[]{:S(2)}) %all-to-all-start.3) | async-done | bytes 16416 | tf_op jit(solution)/shard_map/all_to_all | solution.py:546
  47.1 0.8 %final.1 = (f32[4,8,256]{2,1,0:T(8,128)}, f32[3,4,8]{2,1,0:T(4,128)}) custom-call(f32[32,128]{1,0:T(8,128)S(1)} %bitcast.11, f32[4,8,256]{2,1,0:T(8,128)S(1)} %get-tuple-element.47.kept_ref, f32[8,128]{1,0:T(8,128)S(1)} %get-tuple-element.48.known_ref, f32[21,8,128]{2,1,0:T(8,128)S(1)} %get-tuple-element.49.terms_ref), custom_call_target="tpu_custom_call" | custom-call | tf_op jit(solution)/shard_map/final/pallas_call | solution.py:561
  (1 shorter events, 0.0 us)
Async XLA Ops:
  2.1 8.7 %collective-permute-start = (bf16[32,128,128]{2,1,0:T(8,128)(2,1)}, bf16[32,128,128]{2,1,0:T(8,128)(2,1)S(1)}, u32[]{:S(2)}, u32[]{:S(2)}) collective-permute-start(bf16[32,128,128]{2,1,0:T(8,128)(2,1)} %bitcast.12), channel_id=1, source_target_pairs={{0,1},{1,0},{2,3},{3,2},{4,5},{5,4},{6,7},{7,6},{8,9},{9,8},{10,11... | collective-permute-start | bytes 3145736 | tf_op jit(solution)/shard_map/ppermute | solution.py:503
  2.6 14.5 %all-to-all-start = ((f32[32,8,128]{2,1,0:T(8,128)}), f32[32,8,128]{2,1,0:T(8,128)S(1)}, u32[]{:S(2)}, u32[]{:S(2)}) async-start(f32[32,8,128]{2,1,0:T(8,128)} %get-tuple-element.28), calls=%async_computation | async-start | bytes 262144 | tf_op jit(solution)/shard_map/all_to_all | solution.py:520
  9.6 1.2 %collective-permute-start.1 = (s32[2,1,32]{2,1,0:T(1,128)S(1)}, s32[2,1,32]{2,1,0:T(1,128)S(1)}, u32[]{:S(2)}, u32[]{:S(2)}) collective-permute-start(s32[2,1,32]{2,1,0:T(1,128)S(1)} %get-tuple-element.30.own_places), channel_id=1, source_target_pairs={{0,1},{1,0},{2,3},{3,2},{4,5},{5,4},{6,7},{7,6},{8,9},{9,8},{10,11... | collective-permute-start | bytes 776 | tf_op jit(solution)/shard_map/ppermute | solution.py:503
  37.4 9.7 %all-to-all-start.3 = ((f32[32,1,128]{2,1,0:T(1,128)}), f32[32,1,128]{2,1,0:T(1,128)S(1)}, u32[]{:S(2)}, u32[]{:S(2)}) async-start(f32[32,1,128]{2,1,0:T(1,128)} %bitcast.4), calls=%async_computation.3 | async-start | bytes 32768 | tf_op jit(solution)/shard_map/all_to_all | solution.py:546
  40.1 3.9 %collective-permute-start.3 = (f32[5,8,128]{2,1,0:T(8,128)S(1)}, f32[5,8,128]{2,1,0:T(8,128)S(1)}, u32[]{:S(2)}, u32[]{:S(2)}) collective-permute-start(f32[5,8,128]{2,1,0:T(8,128)S(1)} %get-tuple-element.44.mine_ref), channel_id=1, source_target_pairs={{0,16},{1,17},{2,18},{3,19},{4,20},{5,21},{6,22},{7,23},{8,24},{9,... | collective-permute-start | bytes 61448 | tf_op jit(solution)/shard_map/ppermute | solution.py:503
  41.9 3.4 %collective-permute-start.4 = (f32[5,8,128]{2,1,0:T(8,128)S(1)}, f32[5,8,128]{2,1,0:T(8,128)S(1)}, u32[]{:S(2)}, u32[]{:S(2)}) collective-permute-start(f32[5,8,128]{2,1,0:T(8,128)S(1)} %get-tuple-element.45), channel_id=1, source_target_pairs={{0,17},{1,16},{2,19},{3,18},{4,21},{5,20},{6,23},{7,22},{8,25},{9,... | collective-permute-start | bytes 61448 | tf_op jit(solution)/shard_map/ppermute | solution.py:503
  41.9 3.4 %collective-permute-start.2 = (f32[5,8,128]{2,1,0:T(8,128)S(1)}, f32[5,8,128]{2,1,0:T(8,128)S(1)}, u32[]{:S(2)}, u32[]{:S(2)}) collective-permute-start(f32[5,8,128]{2,1,0:T(8,128)S(1)} %get-tuple-element.45), channel_id=1, source_target_pairs={{0,1},{1,0},{2,3},{3,2},{4,5},{5,4},{6,7},{7,6},{8,9},{9,8},{10,11... | collective-permute-start | bytes 61448 | tf_op jit(solution)/shard_map/ppermute | solution.py:503

commit v12 on v11

--- a/solution.py
+++ b/solution.py
@@ -130,7 +130,7 @@
         pick_ref[...], jnp.concatenate([coarse, fine], axis=1), (((1,), (0,)), ((), ())),
         preferred_element_type=jnp.float32,
     ).astype(jnp.bfloat16)
-    sums = [jnp.zeros((4 * ROWS, 2 * BLOCK), jnp.float32) for _ in range(2)]
+    sums = [jnp.zeros((4 * ROWS, 2 * BLOCK), jnp.float32) for _ in range(4)]
     for group in range(weights_ref.shape[0]):
         rows = [
             slice(2 * ROWS * place, 2 * ROWS * (place + 1)) for place in (2 * group, 2 * group + 1)
@@ -142,10 +142,10 @@
             ],
             axis=0,
         )
-        sums[group % 2] += lax.dot_general(
+        sums[group % 4] += lax.dot_general(
             left, weights_ref[group], (((1,), (0,)), ((), ())), preferred_element_type=jnp.float32
         )
-    total = sums[0] + sums[1]
+    total = (sums[0] + sums[1]) + (sums[2] + sums[3])
     total = total[: 2 * ROWS] + total[2 * ROWS :]
     _, _, core = position()
     own = total[:ROWS, :BLOCK]

time: 48.2 us -> 48.1 us (level)
  no operation moved by 1% of the time
where the time goes in v12:
time: 48.1 us; the launch traced here: 47.8 us
  blocking collectives  17.5 us (36%)
  starting transfers between devices  12.7 us (26%)
  waiting for transfers between devices  8.74 us (18%)
  Pallas kernels  8.16 us (17%)
  between operations  0.68 us (1%)
    all_to_all x2, blocking collectives, exchanged(): return lax.all_to_all(chunks, AXES, 0, 0, axis_index_groups=groups)  17.5 us
    all_to_all x1, starting transfers between devices, on_device(): got = lax.all_to_all(chunks, AXES, 0, 0, axis_index_groups=listed)  6.96 us
    all_to_all x1, waiting for transfers between devices, on_device(): got = lax.all_to_all(chunks, AXES, 0, 0, axis_index_groups=listed)  4.18 us
    ppermute x5, waiting for transfers between devices, swapped(): return lax.ppermute(value, AXES, [(i, i ^ bits) for i in range(devices)])  3.92 us
    ppermute x5, starting transfers between devices, swapped(): return lax.ppermute(value, AXES, [(i, i ^ bits) for i in range(devices)])  3.04 us
    all_to_all x1, starting transfers between devices, on_device(): lax.all_to_all(chunks.reshape(devices, 1, BLOCK), AXES, 0, 0, axis_index_...  2.66 us
    pallas_call x1, Pallas kernels, on_device(): call(prepare_kernel, [shaped(blocks.shape[0] // 2, 2 * BLOCK, 2 * BLOCK,...  2.12 us
    pallas_call x1, Pallas kernels, on_device(): call(start_kernel, [everything, shaped(*mirror_rows.shape, dtype=jnp.int3...  1.48 us
  transfers between devices with their start and end apart: 7, of which 5 were waited for; matrix products, arithmetic and copies ran while one was open for 0% of the time, Pallas kernels for 7%

profile of v12, /device:TPU:0, one launch (start us, length us, event | category | flops | bytes accessed | tf_op | source)
XLA Modules:
  0.0 47.8 jit_solution(9340905615254207162)
XLA Ops:
  0.6 1.5 %start.1 = (f32[32,8,128]{2,1,0:T(8,128)}, s32[2,128]{1,0:T(2,128)S(1)}, s32[2,1,32]{2,1,0:T(1,128)S(1)}) custom-call(f32[8,256]{1,0:T(8,128)} %bitcast.14, s32[2,128]{1,0:T(2,128)} %bitcast.15, s32[1,32]{1,0:T(1,128)} %rows_hbm.1, s32[1,32]{1,0:T(1,128)} %cols_hbm.1), custom_call_target="tpu_custom_call" | custom-call | tf_op jit(solution)/shard_map/start/pallas_call | solution.py:508
  2.1 0.5 %collective-permute-start = (bf16[32,128,128]{2,1,0:T(8,128)(2,1)}, bf16[32,128,128]{2,1,0:T(8,128)(2,1)S(1)}, u32[]{:S(2)}, u32[]{:S(2)}) collective-permute-start(bf16[32,128,128]{2,1,0:T(8,128)(2,1)} %bitcast.12), channel_id=1, source_target_pairs={{0,1},{1,0},{2,3},{3,2},{4,5},{5,4},{6,7},{7,6},{8,9},{9,8},{10,11... | collective-permute-start | bytes 3145736 | tf_op jit(solution)/shard_map/ppermute | solution.py:503
  2.6 7.0 %all-to-all-start = ((f32[32,8,128]{2,1,0:T(8,128)}), f32[32,8,128]{2,1,0:T(8,128)S(1)}, u32[]{:S(2)}, u32[]{:S(2)}) async-start(f32[32,8,128]{2,1,0:T(8,128)} %get-tuple-element.28), calls=%async_computation | async-start | bytes 262144 | tf_op jit(solution)/shard_map/all_to_all | solution.py:520
  9.6 0.3 collective-permute-start.1
  9.9 0.9 %collective-permute-done.1.other_places = s32[2,1,32]{2,1,0:T(1,128)S(1)} collective-permute-done((s32[2,1,32]{2,1,0:T(1,128)S(1)}, s32[2,1,32]{2,1,0:T(1,128)S(1)}, u32[]{:S(2)}, u32[]{:S(2)}) %collective-permute-start.1) | collective-permute-done | bytes 288 | tf_op jit(solution)/shard_map/ppermute | solution.py:503
  10.8 0.0 collective-permute-done.other_ref
  10.8 2.1 %prepare.1 = (bf16[16,256,256]{2,1,0:T(8,128)(2,1)S(1)}, bf16[512,128]{1,0:T(8,128)(2,1)S(1)}) custom-call(bf16[32,128,128]{2,1,0:T(8,128)(2,1)} %bitcast.13, bf16[32,128,128]{2,1,0:T(8,128)(2,1)S(1)} %collective-permute-done.other_ref, s32[2,1,32]{2,1,0:T(1,128)S(1)} %get-tuple-element.30.own_places, s32[2,1,32]{2,1,0:T(1,128)S(1)} %collective-permute-done.1.other_places), custom_call_target="tpu_custom_call" | custom-call | tf_op jit(solution)/shard_map/prepare/pallas_call | solution.py:522
  12.9 4.2 %all-to-all-done.got_ref = f32[32,8,128]{2,1,0:T(8,128)S(1)} async-done(((f32[32,8,128]{2,1,0:T(8,128)}), f32[32,8,128]{2,1,0:T(8,128)S(1)}, u32[]{:S(2)}, u32[]{:S(2)}) %all-to-all-start) | async-done | bytes 131104 | tf_op jit(solution)/shard_map/all_to_all | solution.py:520
  17.1 0.6 %first.1 = (f32[8,2,8,128]{3,2,1,0:T(8,128)S(1)}, f32[16,8,128]{2,1,0:T(8,128)S(1)}, f32[8,128]{1,0:T(8,128)S(1)}) custom-call(f32[32,8,128]{2,1,0:T(8,128)S(1)} %all-to-all-done.got_ref, bf16[512,128]{1,0:T(8,128)(2,1)S(1)} %get-tuple-element.31.pick_ref, bf16[16,256,256]{2,1,0:T(8,128)(2,1)S(1)} %get-tuple-element.32.weights_ref), custom_call_target="tpu_custom_call" | custom-call | tf_op jit(solution)/shard_map/first/pallas_call | solution.py:533
  17.8 8.9 %all_to_all.20.got_ref.first_got_ref = f32[8,2,8,128]{3,2,1,0:T(8,128)S(1)} all-to-all(f32[8,2,8,128]{3,2,1,0:T(8,128)S(1)} %get-tuple-element.33), channel_id=1, replica_groups={{10,12,14,0,2,4,6,8},{11,13,15,1,3,5,7,9},{26,28,30,16,18,20,22,24},{27..., dimensions={0} | all-to-all | bytes 131072 | tf_op jit(solution)/shard_map/all_to_all | solution.py:506
  26.7 0.6 %middle.1 = (f32[8,2,8,128]{3,2,1,0:T(8,128)S(1)}, f32[16,8,128]{2,1,0:T(8,128)S(1)}, f32[8,128]{1,0:T(8,128)S(1)}) custom-call(f32[8,2,8,128]{3,2,1,0:T(8,128)S(1)} %all_to_all.20.got_ref.first_got_ref, f32[16,8,128]{2,1,0:T(8,128)S(1)} %get-tuple-element.34.basis_ref.zero_ref, f32[8,128]{1,0:T(8,128)S(1)} %get-tuple-element.35.known_ref, ...), custom_call_target="tpu_custom_call" | custom-call | tf_op jit(solution)/shard_map/middle/pallas_call | solution.py:537
  27.3 8.6 %all_to_all.21.got_ref = f32[8,2,8,128]{3,2,1,0:T(8,128)S(1)} all-to-all(f32[8,2,8,128]{3,2,1,0:T(8,128)S(1)} %get-tuple-element.36), channel_id=1, replica_groups={{10,12,14,0,2,4,6,8},{11,13,15,1,3,5,7,9},{26,28,30,16,18,20,22,24},{27..., dimensions={0} | all-to-all | bytes 131072 | tf_op jit(solution)/shard_map/all_to_all | solution.py:506
  35.9 1.3 %last.1 = (f32[32,128]{1,0:T(8,128)}, f32[16,8,128]{2,1,0:T(8,128)S(1)}, f32[8,128]{1,0:T(8,128)S(1)}, f32[8,128]{1,0:T(8,128)S(1)}, f32[8,128]{1,0:T(8,128)S(1)}) custom-call(f32[8,2,8,128]{3,2,1,0:T(8,128)S(1)} %all_to_all.20.got_ref.first_got_ref, f32[8,2,8,128]{3,2,1,0:T(8,128)S(1)} %all_to_all.21.got_ref, ...), custom_call_target="tpu_custom_call" | custom-call | tf_op jit(solution)/shard_map/last/pallas_call | solution.py:542
  37.3 2.7 %all-to-all-start.3 = ((f32[32,1,128]{2,1,0:T(1,128)}), f32[32,1,128]{2,1,0:T(1,128)S(1)}, u32[]{:S(2)}, u32[]{:S(2)}) async-start(f32[32,1,128]{2,1,0:T(1,128)} %bitcast.4), calls=%async_computation.3 | async-start | bytes 32768 | tf_op jit(solution)/shard_map/all_to_all | solution.py:546
  40.0 1.8 %collective-permute-start.3 = (f32[5,8,128]{2,1,0:T(8,128)S(1)}, f32[5,8,128]{2,1,0:T(8,128)S(1)}, u32[]{:S(2)}, u32[]{:S(2)}) collective-permute-start(f32[5,8,128]{2,1,0:T(8,128)S(1)} %get-tuple-element.44.mine_ref), channel_id=1, source_target_pairs={{0,16},{1,17},{2,18},{3,19},{4,20},{5,21},{6,22},{7,23},{8,24},{9,... | collective-permute-start | bytes 61448 | tf_op jit(solution)/shard_map/ppermute | solution.py:503
  41.8 0.0 collective-permute-start.4
  41.8 0.4 collective-permute-start.2
  42.2 1.7 %collective-permute-done.3.across_ref = f32[5,8,128]{2,1,0:T(8,128)S(1)} collective-permute-done((f32[5,8,128]{2,1,0:T(8,128)S(1)}, f32[5,8,128]{2,1,0:T(8,128)S(1)}, u32[]{:S(2)}, u32[]{:S(2)}) %collective-permute-start.3) | collective-permute-done | bytes 20512 | tf_op jit(solution)/shard_map/ppermute | solution.py:503
  43.8 1.4 %collective-permute-done.4.flipped_ref = f32[5,8,128]{2,1,0:T(8,128)S(1)} collective-permute-done((f32[5,8,128]{2,1,0:T(8,128)S(1)}, f32[5,8,128]{2,1,0:T(8,128)S(1)}, u32[]{:S(2)}, u32[]{:S(2)}) %collective-permute-start.4) | collective-permute-done | bytes 20512 | tf_op jit(solution)/shard_map/ppermute | solution.py:503
  45.2 0.0 collective-permute-done.2.partner_ref
  45.2 1.1 %keep.1 = (f32[4,8,256]{2,1,0:T(8,128)S(1)}, f32[8,128]{1,0:T(8,128)S(1)}, f32[21,8,128]{2,1,0:T(8,128)S(1)}) custom-call(f32[5,8,128]{2,1,0:T(8,128)S(1)} %get-tuple-element.44.mine_ref, f32[5,8,128]{2,1,0:T(8,128)S(1)} %collective-permute-done.2.partner_ref, f32[5,8,128]{2,1,0:T(8,128)S(1)} %collective-permute-done.3.across_ref, ...), custom_call_target="tpu_custom_call" | custom-call | tf_op jit(solution)/shard_map/keep/pallas_call | solution.py:553
  46.3 0.6 %all-to-all-done.3 = f32[32,1,128]{2,1,0:T(1,128)S(1)} async-done(((f32[32,1,128]{2,1,0:T(1,128)}), f32[32,1,128]{2,1,0:T(1,128)S(1)}, u32[]{:S(2)}, u32[]{:S(2)}) %all-to-all-start.3) | async-done | bytes 16416 | tf_op jit(solution)/shard_map/all_to_all | solution.py:546
  47.0 0.8 %final.1 = (f32[4,8,256]{2,1,0:T(8,128)}, f32[3,4,8]{2,1,0:T(4,128)}) custom-call(f32[32,128]{1,0:T(8,128)S(1)} %bitcast.11, f32[4,8,256]{2,1,0:T(8,128)S(1)} %get-tuple-element.47.kept_ref, f32[8,128]{1,0:T(8,128)S(1)} %get-tuple-element.48.known_ref, f32[21,8,128]{2,1,0:T(8,128)S(1)} %get-tuple-element.49.terms_ref), custom_call_target="tpu_custom_call" | custom-call | tf_op jit(solution)/shard_map/final/pallas_call | solution.py:561
  (1 shorter events, 0.0 us)
Async XLA Ops:
  2.1 8.7 %collective-permute-start = (bf16[32,128,128]{2,1,0:T(8,128)(2,1)}, bf16[32,128,128]{2,1,0:T(8,128)(2,1)S(1)}, u32[]{:S(2)}, u32[]{:S(2)}) collective-permute-start(bf16[32,128,128]{2,1,0:T(8,128)(2,1)} %bitcast.12), channel_id=1, source_target_pairs={{0,1},{1,0},{2,3},{3,2},{4,5},{5,4},{6,7},{7,6},{8,9},{9,8},{10,11... | collective-permute-start | bytes 3145736 | tf_op jit(solution)/shard_map/ppermute | solution.py:503
  2.6 14.5 %all-to-all-start = ((f32[32,8,128]{2,1,0:T(8,128)}), f32[32,8,128]{2,1,0:T(8,128)S(1)}, u32[]{:S(2)}, u32[]{:S(2)}) async-start(f32[32,8,128]{2,1,0:T(8,128)} %get-tuple-element.28), calls=%async_computation | async-start | bytes 262144 | tf_op jit(solution)/shard_map/all_to_all | solution.py:520
  9.6 1.2 %collective-permute-start.1 = (s32[2,1,32]{2,1,0:T(1,128)S(1)}, s32[2,1,32]{2,1,0:T(1,128)S(1)}, u32[]{:S(2)}, u32[]{:S(2)}) collective-permute-start(s32[2,1,32]{2,1,0:T(1,128)S(1)} %get-tuple-element.30.own_places), channel_id=1, source_target_pairs={{0,1},{1,0},{2,3},{3,2},{4,5},{5,4},{6,7},{7,6},{8,9},{9,8},{10,11... | collective-permute-start | bytes 776 | tf_op jit(solution)/shard_map/ppermute | solution.py:503
  37.3 9.7 %all-to-all-start.3 = ((f32[32,1,128]{2,1,0:T(1,128)}), f32[32,1,128]{2,1,0:T(1,128)S(1)}, u32[]{:S(2)}, u32[]{:S(2)}) async-start(f32[32,1,128]{2,1,0:T(1,128)} %bitcast.4), calls=%async_computation.3 | async-start | bytes 32768 | tf_op jit(solution)/shard_map/all_to_all | solution.py:546
  40.0 3.9 %collective-permute-start.3 = (f32[5,8,128]{2,1,0:T(8,128)S(1)}, f32[5,8,128]{2,1,0:T(8,128)S(1)}, u32[]{:S(2)}, u32[]{:S(2)}) collective-permute-start(f32[5,8,128]{2,1,0:T(8,128)S(1)} %get-tuple-element.44.mine_ref), channel_id=1, source_target_pairs={{0,16},{1,17},{2,18},{3,19},{4,20},{5,21},{6,22},{7,23},{8,24},{9,... | collective-permute-start | bytes 61448 | tf_op jit(solution)/shard_map/ppermute | solution.py:503
  41.8 3.4 %collective-permute-start.4 = (f32[5,8,128]{2,1,0:T(8,128)S(1)}, f32[5,8,128]{2,1,0:T(8,128)S(1)}, u32[]{:S(2)}, u32[]{:S(2)}) collective-permute-start(f32[5,8,128]{2,1,0:T(8,128)S(1)} %get-tuple-element.45), channel_id=1, source_target_pairs={{0,17},{1,16},{2,19},{3,18},{4,21},{5,20},{6,23},{7,22},{8,25},{9,... | collective-permute-start | bytes 61448 | tf_op jit(solution)/shard_map/ppermute | solution.py:503
  41.8 3.4 %collective-permute-start.2 = (f32[5,8,128]{2,1,0:T(8,128)S(1)}, f32[5,8,128]{2,1,0:T(8,128)S(1)}, u32[]{:S(2)}, u32[]{:S(2)}) collective-permute-start(f32[5,8,128]{2,1,0:T(8,128)S(1)} %get-tuple-element.45), channel_id=1, source_target_pairs={{0,1},{1,0},{2,3},{3,2},{4,5},{5,4},{6,7},{7,6},{8,9},{9,8},{10,11... | collective-permute-start | bytes 61448 | tf_op jit(solution)/shard_map/ppermute | solution.py:503
